TPU v7x, 512 devices: a whole 4x8x8 slice. The times are simulated.
512 devices in a mesh: shard: 64 (over y, x, core), rep: 8 (over z).
Axes of the slice: x: 4, y: 8, z: 8, core: 2. Of those that a mesh axis runs over, the one named last changes fastest.
Arguments:
- pooled_grad: bfloat16 [65536, 64, 128], P(('shard', 'rep')), may hold values from -6 to 6
- cold_ids: int32 [65536, 64, 8], P(('shard', 'rep')), may hold values from 0 to 1023
- lengths: int32 [65536, 64], P(('shard', 'rep')), may hold values from 1 to 8
- hot_ids: int32 [65536, 64, 2], P(('shard', 'rep')), may hold values from 0 to 1023
- table: float32 [65536, 128], P('shard'), may hold values from -1.5 to 1.5
- accum: float32 [65536], P('shard'), may hold values from 100 to 1000
- hot_table: float32 [1024, 128], replicated, may hold values from -1.5 to 1.5
- hot_accum: float32 [1024], replicated, may hold values from 5000 to 50000
Outputs:
- new_table: float32 [65536, 128], P('shard')
- new_accum: float32 [65536], P('shard')
- new_hot_table: float32 [1024, 128], replicated
- new_hot_accum: float32 [1024], replicated
All inputs are finite; a program needn't handle non-finite values.
Results may differ from a plain program's by a relative error of at most 0.0003.
Values may be sent and summed in bfloat16 or wider, within the bound.
No kernel may reach another device: no remote copies, remote signals or barrier semaphores. Data moves between devices by JAX's collectives and lax.ppermute only.
A program may use at most 64 MiB of HBM per device.

v0:
```python
import jax
import jax.numpy as jnp
from jax import lax
from jax.sharding import PartitionSpec as P

V = 1024


learning_rate = 0.5
epsilon = 1e-06


def adagrad(weights, accumulator, grad):
    fresh = accumulator + jnp.mean(grad * grad, axis=1)
    return (weights - learning_rate * grad / (jnp.sqrt(fresh)[:, None] + epsilon), fresh)


def bag_sum(ids, values, limit):
    samples = ids.shape[0]
    block = min(512, samples)
    steps = samples // block
    table_rows = lax.broadcasted_iota(jnp.int32, (limit, 1, 1), 0)

    def accumulate(index, total):
        start = index * block
        id_block = lax.dynamic_slice_in_dim(ids, start, block, 0)
        value_block = lax.dynamic_slice_in_dim(values, start, block, 0)
        counts = jnp.sum((table_rows == id_block[None, :, :]).astype(jnp.bfloat16), axis=2)
        return total + jnp.dot(counts, value_block, preferred_element_type=jnp.float32)

    start_total = jnp.zeros((limit, values.shape[1]), jnp.float32)
    return lax.fori_loop(0, steps, accumulate, start_total)


def per_device(pooled_grad, cold_ids, lengths, hot_ids, table, accum, hot_table, hot_accum):
    width = pooled_grad.shape[2]
    position = lax.broadcasted_iota(jnp.int32, cold_ids.shape, 2)
    masked = jnp.where(position < lengths[:, :, None], cold_ids, V)
    moved_grad = lax.all_to_all(pooled_grad, "shard", split_axis=1, concat_axis=0, tiled=True)
    moved_ids = lax.all_to_all(masked, "shard", split_axis=1, concat_axis=0, tiled=True)
    pieces = bag_sum(moved_ids[:, 0, :], moved_grad[:, 0, :], V)
    hot_flat = hot_ids.reshape(-1, hot_ids.shape[2])
    hot_grad = bag_sum(hot_flat, pooled_grad.reshape(-1, width), hot_table.shape[0])
    total = lax.psum(pieces, "rep")
    new_table, new_accum = adagrad(table, accum, total)
    hot_total = lax.psum(hot_grad, ("shard", "rep"))
    new_hot_table, new_hot_accum = adagrad(hot_table, hot_accum, hot_total)
    return (new_table, new_accum, new_hot_table, new_hot_accum)


def solution(mesh):
    in_specs = (
        P(("shard", "rep"), None, None),
        P(("shard", "rep"), None, None),
        P(("shard", "rep"), None),
        P(("shard", "rep"), None, None),
        P("shard", None),
        P("shard"),
        P(),
        P(),
    )
    out_specs = (P("shard", None), P("shard"), P(), P())
    return jax.shard_map(
        per_device, mesh=mesh, in_specs=in_specs, out_specs=out_specs, check_vma=False
    )
```

profile of v0, /device:TPU:6, one launch (start us, length us, event | category | flops | bytes accessed | tf_op | source)
XLA Modules:
  0.0 441.1 jit_solution(2694310400624907374)
XLA Ops:
  7.2 1.7 fusion.12
  8.9 10.6 %all-to-all-start = ((s32[128,64,8]{0,2,1:T(8,128)}), s32[128,64,8]{0,2,1:T(8,128)S(1)}, u32[]{:S(2)}, u32[]{:S(2)}) async-start(s32[128,64,8]{0,2,1:T(8,128)} %fusion.12), calls=%async_computation | async-start | bytes 524288 | tf_op jit(solution)/shard_map/all_to_all | solution.py:40
  19.5 4.3 copy.24
  24.0 7.4 %all-to-all-done = s32[128,64,8]{0,2,1:T(8,128)S(1)} async-done(((s32[128,64,8]{0,2,1:T(8,128)}), s32[128,64,8]{0,2,1:T(8,128)S(1)}, u32[]{:S(2)}, u32[]{:S(2)}) %all-to-all-start) | async-done | bytes 262176 | tf_op jit(solution)/shard_map/all_to_all | solution.py:40
  31.4 6.4 %all-to-all-start.1 = ((bf16[128,64,128]{2,0,1:T(8,128)(2,1)}), bf16[128,64,128]{2,0,1:T(8,128)(2,1)}, u32[]{:S(2)}, u32[]{:S(2)}) async-start(bf16[128,64,128]{2,0,1:T(8,128)(2,1)} %copy.24), calls=%async_computation.1 | async-start | bytes 4194304 | tf_op jit(solution)/shard_map/all_to_all | solution.py:39
  37.9 38.6 %while.33 = (s32[]{:T(128)}, f32[1024,128]{1,0:T(8,128)S(1)}, s32[8192,2]{0,1:T(2,128)S(1)}, bf16[8192,128]{1,0:T(8,128)(2,1)}, s32[]{:T(128)}, /*index=5*/s32[]{:T(128)}, s32[]{:T(128)}, s32[]{:T(128)}) while((s32[]{:T(128)}, f32[1024,128]{1,0:T(8,128)S(1)}, s32[8192,2]{0,1:T(2,128)S(1)}, bf16[8192,128]{1,0:T(8,128)(2,1)}, ...), condition=%wide.region_7.8_spmd.clone, body=%wide.region_5.0_spmd.clone.sunk | while | flops 137101312 | bytes 3289237 | solution.py:32
  55.8 1.4 convolution_add_fusion.5
  70.2 1.4 convolution_add_fusion.5
  77.5 11.6 %all-to-all-done.1 = bf16[128,64,128]{2,0,1:T(8,128)(2,1)} async-done(((bf16[128,64,128]{2,0,1:T(8,128)(2,1)}), bf16[128,64,128]{2,0,1:T(8,128)(2,1)}, u32[]{:S(2)}, u32[]{:S(2)}) %all-to-all-start.1) | async-done | bytes 2097184 | tf_op jit(solution)/shard_map/all_to_all | solution.py:39
  89.1 153.2 %while.32 = (s32[]{:T(128)}, f32[1024,128]{1,0:T(8,128)S(1)}, s32[8192,8]{0,1:T(8,128)S(1)}, bf16[8192,128]{1,0:T(8,128)(2,1)}, s32[]{:T(128)}, /*index=5*/s32[]{:T(128)}, s32[]{:T(128)}, s32[]{:T(128)}) while((s32[]{:T(128)}, f32[1024,128]{1,0:T(8,128)S(1)}, s32[8192,8]{0,1:T(8,128)S(1)}, bf16[8192,128]{1,0:T(8,128)(2,1)}, ...), condition=%wide.region_2.3_spmd.clone, body=%wide.region_0.2_spmd.clone.sunk | while | flops 146538496 | bytes 3326101 | solution.py:32
  89.1 8.1 %fusion.23 = bf16[1024,512]{1,0:T(8,128)(2,1)S(1)} fusion(s32[512,8]{0,1:T(8,128)S(1)} %constant_dynamic-slice_fusion.4), kind=kLoop, calls=%fused_computation.4.clone.1 | loop fusion | flops 12058624 | bytes 1064960 | tf_op jit(solution)/shard_map/while/body/eval_jaxpr/reduce_sum | solution.py:28
  97.3 1.4 convolution_add_fusion.4
  98.7 8.1 %fusion.23 = bf16[1024,512]{1,0:T(8,128)(2,1)S(1)} fusion(s32[512,8]{0,1:T(8,128)S(1)} %constant_dynamic-slice_fusion.4), kind=kLoop, calls=%fused_computation.4.clone.1 | loop fusion | flops 12058624 | bytes 1064960 | tf_op jit(solution)/shard_map/while/body/eval_jaxpr/reduce_sum | solution.py:28
  108.3 8.1 %fusion.23 = bf16[1024,512]{1,0:T(8,128)(2,1)S(1)} fusion(s32[512,8]{0,1:T(8,128)S(1)} %constant_dynamic-slice_fusion.4), kind=kLoop, calls=%fused_computation.4.clone.1 | loop fusion | flops 12058624 | bytes 1064960 | tf_op jit(solution)/shard_map/while/body/eval_jaxpr/reduce_sum | solution.py:28
  117.9 8.1 %fusion.23 = bf16[1024,512]{1,0:T(8,128)(2,1)S(1)} fusion(s32[512,8]{0,1:T(8,128)S(1)} %constant_dynamic-slice_fusion.4), kind=kLoop, calls=%fused_computation.4.clone.1 | loop fusion | flops 12058624 | bytes 1064960 | tf_op jit(solution)/shard_map/while/body/eval_jaxpr/reduce_sum | solution.py:28
  127.4 8.1 %fusion.23 = bf16[1024,512]{1,0:T(8,128)(2,1)S(1)} fusion(s32[512,8]{0,1:T(8,128)S(1)} %constant_dynamic-slice_fusion.4), kind=kLoop, calls=%fused_computation.4.clone.1 | loop fusion | flops 12058624 | bytes 1064960 | tf_op jit(solution)/shard_map/while/body/eval_jaxpr/reduce_sum | solution.py:28
  137.0 8.1 %fusion.23 = bf16[1024,512]{1,0:T(8,128)(2,1)S(1)} fusion(s32[512,8]{0,1:T(8,128)S(1)} %constant_dynamic-slice_fusion.4), kind=kLoop, calls=%fused_computation.4.clone.1 | loop fusion | flops 12058624 | bytes 1064960 | tf_op jit(solution)/shard_map/while/body/eval_jaxpr/reduce_sum | solution.py:28
  146.6 8.1 %fusion.23 = bf16[1024,512]{1,0:T(8,128)(2,1)S(1)} fusion(s32[512,8]{0,1:T(8,128)S(1)} %constant_dynamic-slice_fusion.4), kind=kLoop, calls=%fused_computation.4.clone.1 | loop fusion | flops 12058624 | bytes 1064960 | tf_op jit(solution)/shard_map/while/body/eval_jaxpr/reduce_sum | solution.py:28
  154.7 1.4 convolution_add_fusion.4
  156.2 8.1 %fusion.23 = bf16[1024,512]{1,0:T(8,128)(2,1)S(1)} fusion(s32[512,8]{0,1:T(8,128)S(1)} %constant_dynamic-slice_fusion.4), kind=kLoop, calls=%fused_computation.4.clone.1 | loop fusion | flops 12058624 | bytes 1064960 | tf_op jit(solution)/shard_map/while/body/eval_jaxpr/reduce_sum | solution.py:28
  165.8 8.1 %fusion.23 = bf16[1024,512]{1,0:T(8,128)(2,1)S(1)} fusion(s32[512,8]{0,1:T(8,128)S(1)} %constant_dynamic-slice_fusion.4), kind=kLoop, calls=%fused_computation.4.clone.1 | loop fusion | flops 12058624 | bytes 1064960 | tf_op jit(solution)/shard_map/while/body/eval_jaxpr/reduce_sum | solution.py:28
  175.3 8.1 %fusion.23 = bf16[1024,512]{1,0:T(8,128)(2,1)S(1)} fusion(s32[512,8]{0,1:T(8,128)S(1)} %constant_dynamic-slice_fusion.4), kind=kLoop, calls=%fused_computation.4.clone.1 | loop fusion | flops 12058624 | bytes 1064960 | tf_op jit(solution)/shard_map/while/body/eval_jaxpr/reduce_sum | solution.py:28
  184.9 8.1 %fusion.23 = bf16[1024,512]{1,0:T(8,128)(2,1)S(1)} fusion(s32[512,8]{0,1:T(8,128)S(1)} %constant_dynamic-slice_fusion.4), kind=kLoop, calls=%fused_computation.4.clone.1 | loop fusion | flops 12058624 | bytes 1064960 | tf_op jit(solution)/shard_map/while/body/eval_jaxpr/reduce_sum | solution.py:28
  194.5 8.1 %fusion.23 = bf16[1024,512]{1,0:T(8,128)(2,1)S(1)} fusion(s32[512,8]{0,1:T(8,128)S(1)} %constant_dynamic-slice_fusion.4), kind=kLoop, calls=%fused_computation.4.clone.1 | loop fusion | flops 12058624 | bytes 1064960 | tf_op jit(solution)/shard_map/while/body/eval_jaxpr/reduce_sum | solution.py:28
  204.1 8.1 %fusion.23 = bf16[1024,512]{1,0:T(8,128)(2,1)S(1)} fusion(s32[512,8]{0,1:T(8,128)S(1)} %constant_dynamic-slice_fusion.4), kind=kLoop, calls=%fused_computation.4.clone.1 | loop fusion | flops 12058624 | bytes 1064960 | tf_op jit(solution)/shard_map/while/body/eval_jaxpr/reduce_sum | solution.py:28
  213.6 8.1 %fusion.23 = bf16[1024,512]{1,0:T(8,128)(2,1)S(1)} fusion(s32[512,8]{0,1:T(8,128)S(1)} %constant_dynamic-slice_fusion.4), kind=kLoop, calls=%fused_computation.4.clone.1 | loop fusion | flops 12058624 | bytes 1064960 | tf_op jit(solution)/shard_map/while/body/eval_jaxpr/reduce_sum | solution.py:28
  223.2 8.1 %fusion.23 = bf16[1024,512]{1,0:T(8,128)(2,1)S(1)} fusion(s32[512,8]{0,1:T(8,128)S(1)} %constant_dynamic-slice_fusion.4), kind=kLoop, calls=%fused_computation.4.clone.1 | loop fusion | flops 12058624 | bytes 1064960 | tf_op jit(solution)/shard_map/while/body/eval_jaxpr/reduce_sum | solution.py:28
  232.8 8.1 %fusion.23 = bf16[1024,512]{1,0:T(8,128)(2,1)S(1)} fusion(s32[512,8]{0,1:T(8,128)S(1)} %constant_dynamic-slice_fusion.4), kind=kLoop, calls=%fused_computation.4.clone.1 | loop fusion | flops 12058624 | bytes 1064960 | tf_op jit(solution)/shard_map/while/body/eval_jaxpr/reduce_sum | solution.py:28
  243.2 106.8 %all-reduce.5.cloned.1.call-done = f32[1024,128]{1,0:T(8,128)} async-done(((f32[1024,128]{1,0:T(8,128)}), f32[1024,128]{1,0:T(8,128)}) %all-reduce.5.cloned.1.call-update) | async-done | bytes 524304 | tf_op jit(solution)/shard_map/psum | solution.py:46
  351.8 2.0 divide_subtract_fusion
  353.9 76.5 %all-reduce.3.cloned.1.call-done = f32[1024,128]{1,0:T(8,128)} async-done(((f32[1024,128]{1,0:T(8,128)}), f32[1024,128]{1,0:T(8,128)}) %all-reduce.3.cloned.1.call-update) | async-done | bytes 524304 | tf_op jit(solution)/shard_map/psum | solution.py:44
  432.2 2.0 divide_subtract_fusion.1
  (102 shorter events, 60.5 us)
Async XLA Ops:
  8.9 22.6 %all-to-all-start = ((s32[128,64,8]{0,2,1:T(8,128)}), s32[128,64,8]{0,2,1:T(8,128)S(1)}, u32[]{:S(2)}, u32[]{:S(2)}) async-start(s32[128,64,8]{0,2,1:T(8,128)} %fusion.12), calls=%async_computation | async-start | bytes 524288 | tf_op jit(solution)/shard_map/all_to_all | solution.py:40
  19.5 4.3 copy-start.4
  31.4 57.7 %all-to-all-start.1 = ((bf16[128,64,128]{2,0,1:T(8,128)(2,1)}), bf16[128,64,128]{2,0,1:T(8,128)(2,1)}, u32[]{:S(2)}, u32[]{:S(2)}) async-start(bf16[128,64,128]{2,0,1:T(8,128)(2,1)} %copy.24), calls=%async_computation.1 | async-start | bytes 4194304 | tf_op jit(solution)/shard_map/all_to_all | solution.py:39
  37.8 312.1 %all-reduce.5.cloned.1.call-start = ((), (), s32[]{:S(2)}) async-start(), calls=%async_computation.3 | async-start | bytes 1048576 | tf_op jit(solution)/shard_map/psum | solution.py:46
  76.5 0.8 copy-start
  77.3 353.1 %all-reduce.3.cloned.1.call-start = ((), (), s32[]{:S(2)}) async-start(), calls=%async_computation.2 | async-start | bytes 1048576 | tf_op jit(solution)/shard_map/psum | solution.py:44
  89.1 262.1 %copy-start.5 = (f32[1024]{0:T(1024)S(1)}, f32[1024]{0:T(1024)}, u32[]{:S(2)}) copy-start(f32[1024]{0:T(1024)} %param.19) | copy-start | bytes 12292
  89.1 262.7 %copy-start.2 = (f32[1024,128]{1,0:T(8,128)S(1)}, f32[1024,128]{1,0:T(8,128)}, u32[]{:S(2)}) copy-start(f32[1024,128]{1,0:T(8,128)} %param.18) | copy-start | bytes 1572868
  242.3 0.8 copy-start.1
  242.4 189.3 %copy-start.6 = (f32[1024]{0:T(1024)S(1)}, f32[1024]{0:T(1024)}, u32[]{:S(2)}) copy-start(f32[1024]{0:T(1024)} %param.17) | copy-start | bytes 12292
  242.4 189.8 %copy-start.3 = (f32[1024,128]{1,0:T(8,128)S(1)}, f32[1024,128]{1,0:T(8,128)}, u32[]{:S(2)}) copy-start(f32[1024,128]{1,0:T(8,128)} %param.16) | copy-start | bytes 1572868
Sparse Core Ops, SparseCore 0:
  77.4 272.5 all-reduce.4
  353.0 77.3 all-reduce.2
where the time goes:
time: 442 us; the launch traced here: 441 us
  waiting for transfers between devices  202 us (46%)
  other arithmetic  155 us (35%)
  matrix products  44.6 us (10%)
  starting transfers between devices  17.3 us (4%)
  between operations  14.2 us (3%)
  local copies, waits for them, and re-layouts  6.35 us (1%)
    reduce_sum x32, other arithmetic, accumulate(): jnp.sum((table_rows == id_block[None, :, :]).astype(jnp.bfloat16), axis=2)  145 us
    psum x1, waiting for transfers between devices, per_device(): hot_total = lax.psum(hot_grad, ('shard', 'rep'))  107 us
    psum x1, waiting for transfers between devices, per_device(): total = lax.psum(pieces, 'rep')  76.5 us
    dot_general x32, matrix products, accumulate(): jnp.dot(counts, value_block, preferred_element_type=jnp.float32)  44.6 us
    all_to_all x1, waiting for transfers between devices, per_device(): lax.all_to_all(pooled_grad, 'shard', split_axis=1, concat_axis=0, tiled=T...  11.6 us
    all_to_all x1, starting transfers between devices, per_device(): lax.all_to_all(masked, 'shard', split_axis=1, concat_axis=0, tiled=True)  10.6 us
  transfers between devices with their start and end apart: 4, of which 4 were waited for; matrix products, arithmetic and copies ran while one was open for 45% of the time, Pallas kernels for 0%

commit v1 on v0

v1 whole, which is shorter than its diff:
```python
import functools

import jax
import jax.numpy as jnp
from jax import lax
from jax.experimental import pallas as pl
from jax.experimental.pallas import tpu as pltpu
from jax.sharding import PartitionSpec as P

V = 1024
GROUP = 128
FIELDS = 8
BITS = 4

learning_rate = 0.5
epsilon = 1e-06


def adagrad(weights, accumulator, grad):
    fresh = accumulator + jnp.mean(grad * grad, axis=1)
    return (weights - learning_rate * grad / (jnp.sqrt(fresh)[:, None] + epsilon), fresh)


def encode_ids(cold_ids, lengths):
    ids = jnp.transpose(cold_ids, (1, 2, 0))
    used = jnp.transpose(lengths, (1, 0))[:, None, :]
    position = lax.broadcasted_iota(jnp.int32, ids.shape, 1)
    low, high = ids & (GROUP - 1), ids >> 7
    return jnp.where(position < used, (GROUP + low) << high, 0).astype(jnp.bfloat16)


def decode_ids(code):
    key = jnp.zeros(code.shape, jnp.float32)
    unit = jnp.zeros(code.shape, jnp.int32)
    for field in range(FIELDS):
        reached = code >= float(GROUP * 2**field)
        key = jnp.where(reached, code * 2.0**-field - float(GROUP), key)
        unit = jnp.where(reached, 1 << (BITS * field), unit)
    return key.astype(jnp.int32), unit


def packed_counts(key, unit):
    rows = lax.broadcasted_iota(jnp.int32, (GROUP, key.shape[1]), 0)
    total = jnp.where(rows == key[0:1], unit[0:1], 0)
    for slot in range(1, key.shape[0]):
        total = total + jnp.where(rows == key[slot : slot + 1], unit[slot : slot + 1], 0)
    return total


def unpacked_counts(packed):
    groups = []
    for field in range(FIELDS):
        if field == FIELDS - 1:
            part = lax.shift_right_logical(packed, jnp.int32(BITS * field))
        else:
            part = packed & jnp.int32(((1 << BITS) - 1) << (BITS * field))
        groups.append(part.astype(jnp.float32).astype(jnp.bfloat16))
    return jnp.concatenate(groups, 0)


def block_sum(bags, values, pair):
    total = None
    for first in range(0, len(bags), pair):
        counts = jnp.concatenate([unpacked_counts(packed_counts(*bag)) for bag in bags[first : first + pair]], 1)
        rows = jnp.concatenate(values[first : first + pair], 0)
        product = jnp.dot(counts, rows, preferred_element_type=jnp.float32)
        total = product if total is None else total + product
    return total


def hot_kernel(x_ref, ids_ref, out_ref, *, blocks, pair):
    step = pl.program_id(0)

    @pl.when(step == 0)
    def _():
        out_ref[...] = jnp.zeros_like(out_ref)

    bags, values = [], []
    for block in range(blocks):
        ids = ids_ref[block]
        shift = lax.shift_right_logical(ids, 7) * BITS
        bags.append((ids & (GROUP - 1), lax.shift_left(jnp.ones_like(ids), shift)))
        values.append(x_ref[block, 0:GROUP, :])
    out_ref[...] += block_sum(bags, values, pair)

    @pl.when(step == pl.num_programs(0) - 1)
    def _():
        for field in range(1, FIELDS - 1):
            out_ref[field * GROUP : (field + 1) * GROUP, :] *= 2.0 ** (-BITS * field)


def hot_sum(rows, ids, blocks=16, pair=4):
    count, height, width = rows.shape
    return pl.pallas_call(
        functools.partial(hot_kernel, blocks=blocks, pair=pair),
        grid=(count // blocks,),
        in_specs=[
            pl.BlockSpec((blocks, height, width), lambda i: (i, 0, 0)),
            pl.BlockSpec((blocks, ids.shape[1], GROUP), lambda i: (i, 0, 0)),
        ],
        out_specs=pl.BlockSpec((V, width), lambda i: (0, 0)),
        out_shape=jax.ShapeDtypeStruct((V, width), jnp.float32),
        compiler_params=pltpu.CompilerParams(vmem_limit_bytes=40 << 20),
        cost_estimate=pl.CostEstimate(flops=2 * V * count * GROUP * width, bytes_accessed=3 << 20, transcendentals=0),
        name="hot_sum",
    )(rows, ids)


def cold_kernel(x_ref, hot_ref, out_ref, *, blocks, pair):
    step = pl.program_id(0)

    @pl.when(step == 0)
    def _():
        out_ref[...] = jnp.zeros_like(out_ref)

    bags, values = [], []
    for block in range(blocks):
        code = x_ref[block, GROUP : GROUP + 8, :].astype(jnp.float32)
        bags.append(decode_ids(code))
        values.append(x_ref[block, 0:GROUP, :])
    total = block_sum(bags, values, pair)
    for field in range(FIELDS):
        out_ref[field, 0:GROUP, :] += total[field * GROUP : (field + 1) * GROUP]

    @pl.when(step == pl.num_programs(0) - 1)
    def _():
        for field in range(FIELDS):
            if 0 < field < FIELDS - 1:
                out_ref[field, 0:GROUP, :] *= 2.0 ** (-BITS * field)
            out_ref[field, GROUP:, :] = hot_ref[...]


def cold_sum(rows, hot_rows, blocks=16, pair=4):
    count, height, width = rows.shape
    tall = GROUP + hot_rows.shape[0]
    return pl.pallas_call(
        functools.partial(cold_kernel, blocks=blocks, pair=pair),
        grid=(count // blocks,),
        in_specs=[
            pl.BlockSpec((blocks, height, width), lambda i: (i, 0, 0)),
            pl.BlockSpec(hot_rows.shape, lambda i: (0, 0)),
        ],
        out_specs=pl.BlockSpec((FIELDS, tall, width), lambda i: (0, 0, 0)),
        out_shape=jax.ShapeDtypeStruct((FIELDS, tall, width), jnp.float32),
        compiler_params=pltpu.CompilerParams(vmem_limit_bytes=40 << 20),
        cost_estimate=pl.CostEstimate(flops=2 * V * count * GROUP * width, bytes_accessed=3 << 20, transcendentals=0),
        name="cold_sum",
    )(rows, hot_rows)


def halve(rows, axis, size, bit):
    half = rows.shape[0] // 2
    mine = (lax.axis_index(axis) // bit) % 2
    pairs = [(i, i ^ bit) for i in range(size)]
    got = lax.ppermute(lax.dynamic_slice_in_dim(rows, (1 - mine) * half, half), axis, pairs)
    return lax.dynamic_slice_in_dim(rows, mine * half, half) + got


def double(rows, axis, size, bit):
    mine = (lax.axis_index(axis) // bit) % 2
    got = lax.ppermute(rows, axis, [(i, i ^ bit) for i in range(size)])
    return jnp.where(mine == 0, jnp.concatenate([rows, got], 0), jnp.concatenate([got, rows], 0))


def per_device(pooled_grad, cold_ids, lengths, hot_ids, table, accum, hot_table, hot_accum):
    shards = lax.axis_size("shard")
    bits = [1 << b for b in range(6)]
    rows = jnp.concatenate([jnp.transpose(pooled_grad, (1, 0, 2)), encode_ids(cold_ids, lengths)], 1)
    moved = lax.all_to_all(rows, "shard", split_axis=0, concat_axis=0, tiled=True)
    hot = hot_sum(rows, jnp.transpose(hot_ids, (1, 2, 0)))
    for bit in bits:
        hot = halve(hot, "shard", shards, bit)
    pieces = cold_sum(moved, hot)
    shared = lax.all_to_all(pieces, "rep", split_axis=0, concat_axis=0, tiled=True)
    total = jnp.sum(shared, axis=0)
    cold_total = lax.all_gather(total[:GROUP], "rep", tiled=True)
    hot = total[GROUP:]
    for bit in reversed(bits):
        hot = double(hot, "shard", shards, bit)
    new_table, new_accum = adagrad(table, accum, cold_total)
    new_hot_table, new_hot_accum = adagrad(hot_table, hot_accum, hot)
    return (new_table, new_accum, new_hot_table, new_hot_accum)


def solution(mesh):
    in_specs = (
        P(("shard", "rep"), None, None),
        P(("shard", "rep"), None, None),
        P(("shard", "rep"), None),
        P(("shard", "rep"), None, None),
        P("shard", None),
        P("shard"),
        P(),
        P(),
    )
    out_specs = (P("shard", None), P("shard"), P(), P())
    return jax.shard_map(
        per_device, mesh=mesh, in_specs=in_specs, out_specs=out_specs, check_vma=False
    )
```

time: 442 us -> 184 us (0.42)
  waiting for transfers between devices: 202 us -> 48.5 us
  other arithmetic: 155 us -> 5.41 us
  blocking collectives: 0 us -> 52.1 us
  matrix products: 44.6 us -> 0 us
  starting transfers between devices: 17.3 us -> 56.6 us
  Pallas kernels: 0 us -> 15.8 us
  between operations: 14.2 us -> 1.22 us
    psum x2 -> x0, waiting for transfers between devices: 183 us -> none  [the longest x1 107 us: per_device(): hot_total = lax.psum(hot_grad, ('shard', 'rep'))]
    reduce_sum x32 -> x1, other arithmetic: 145 us -> 0.03 us  [per_device(): total = jnp.sum(shared, axis=0)]
    ppermute x0 -> x12, waiting for transfers between devices: none -> 48.5 us  [the longest x6 35.4 us: halve(): lax.ppermute(lax.dynamic_slice_in_dim(rows, (1 - mine) * half, half), axi...]
    ppermute x0 -> x12, starting transfers between devices: none -> 45.9 us  [the longest x6 23.9 us: halve(): lax.ppermute(lax.dynamic_slice_in_dim(rows, (1 - mine) * half, half), axi...]
    dot_general x32 -> x0, matrix products: 44.6 us -> none  [accumulate(): jnp.dot(counts, value_block, preferred_element_type=jnp.float32)]
    all_to_all x0 -> x1, blocking collectives: none -> 26.6 us  [per_device(): lax.all_to_all(pieces, 'rep', split_axis=0, concat_axis=0, tiled=True)]
    all_gather x0 -> x1, blocking collectives: none -> 25.5 us  [per_device(): cold_total = lax.all_gather(total[:GROUP], 'rep', tiled=True)]
    all_to_all x2 -> x1, waiting for transfers between devices: 19 us -> 0.01 us  [per_device(): lax.all_to_all(rows, 'shard', split_axis=0, concat_axis=0, tiled=True)]
  transfers between devices with their start and end apart: 4 -> 13, of which waited for: 4 -> 11; matrix products, arithmetic and copies ran while one was open for 45% -> 1% of each run, Pallas kernels for 0% -> 4%
where the time goes in v1:
time: 184 us; the launch traced here: 183 us
  starting transfers between devices  56.6 us (31%)
  blocking collectives  52.1 us (28%)
  waiting for transfers between devices  48.5 us (26%)
  Pallas kernels  15.8 us (9%)
  other arithmetic  5.41 us (3%)
  local copies, waits for them, and re-layouts  3.12 us (2%)
    ppermute x6, waiting for transfers between devices, halve(): lax.ppermute(lax.dynamic_slice_in_dim(rows, (1 - mine) * half, half), axi...  35.4 us
    all_to_all x1, blocking collectives, per_device(): lax.all_to_all(pieces, 'rep', split_axis=0, concat_axis=0, tiled=True)  26.6 us
    all_gather x1, blocking collectives, per_device(): cold_total = lax.all_gather(total[:GROUP], 'rep', tiled=True)  25.5 us
    ppermute x6, starting transfers between devices, halve(): lax.ppermute(lax.dynamic_slice_in_dim(rows, (1 - mine) * half, half), axi...  23.9 us
    ppermute x6, starting transfers between devices, double(): got = lax.ppermute(rows, axis, [(i, i ^ bit) for i in range(size)])  22 us
    ppermute x6, waiting for transfers between devices, double(): got = lax.ppermute(rows, axis, [(i, i ^ bit) for i in range(size)])  13.1 us
    all_to_all x1, starting transfers between devices, per_device(): lax.all_to_all(rows, 'shard', split_axis=0, concat_axis=0, tiled=True)  10.7 us
    pallas_call x1, Pallas kernels, cold_sum(): pl.pallas_call(functools.partial(cold_kernel, blocks=blocks, pair=pair),...  9.22 us
  transfers between devices with their start and end apart: 13, of which 11 were waited for; matrix products, arithmetic and copies ran while one was open for 1% of the time, Pallas kernels for 4%

profile of v1, /device:TPU:6, one launch (start us, length us, event | category | flops | bytes accessed | tf_op | source)
XLA Modules:
  0.0 182.8 jit_solution(1194732930806345217)
XLA Ops:
  0.7 3.0 %copy.14 = bf16[128,64,128]{2,0,1:T(8,128)(2,1)S(1)} copy(bf16[128,64,128]{2,1,0:T(8,128)(2,1)} %param.8) | data formatting | bytes 4194304 | tf_op args[0]
  3.7 1.6 pad_maximum_fusion.x_ref
  5.3 10.7 %all-to-all-start = ((bf16[64,136,128]{2,1,0:T(8,128)(2,1)}), bf16[64,136,128]{2,1,0:T(8,128)(2,1)S(1)}, u32[]{:S(2)}, u32[]{:S(2)}) async-start(bf16[64,136,128]{2,1,0:T(8,128)(2,1)} %pad_maximum_fusion.x_ref), calls=%async_computation | async-start | bytes 4456448 | tf_op jit(solution)/shard_map/all_to_all | solution.py:169
  16.1 6.6 %hot_sum.1 = f32[1024,128]{1,0:T(8,128)S(1)} custom-call(bf16[64,136,128]{2,1,0:T(8,128)(2,1)} %pad_maximum_fusion.x_ref, s32[64,2,128]{2,1,0:T(2,128)S(1)} %bitcast.9), custom_call_target="tpu_custom_call" | custom-call | flops 2147483648 | bytes 3145728 | tf_op jit(solution)/shard_map/hot_sum/pallas_call | solution.py:94
  22.7 2.1 %collective-permute-start = (f32[512,128]{1,0:T(8,128)S(1)}, f32[512,128]{1,0:T(8,128)S(1)}, u32[]{:S(2)}, u32[]{:S(2)}) collective-permute-start(f32[512,128]{1,0:T(8,128)S(1)} %constant_dynamic-slice_fusion.5), channel_id=1, source_target_pairs={{0,8},{8,0},{16,24},{24,16},{32,40},{40,32},{48,56},{56,48},{64,72... | collective-permute-start | bytes 786440 | tf_op jit(solution)/shard_map/ppermute | solution.py:155
  24.8 1.3 collective-permute-done
  26.2 2.8 %collective-permute-start.1 = (f32[256,128]{1,0:T(8,128)S(1)}, f32[256,128]{1,0:T(8,128)S(1)}, u32[]{:S(2)}, u32[]{:S(2)}) collective-permute-start(f32[256,128]{1,0:T(8,128)S(1)} %constant_dynamic-slice_fusion.4), channel_id=1, source_target_pairs={{0,16},{8,24},{16,0},{24,8},{32,48},{40,56},{48,32},{56,40},{64,80... | collective-permute-start | bytes 393224 | tf_op jit(solution)/shard_map/ppermute | solution.py:155
  29.0 6.9 %collective-permute-done.1 = f32[256,128]{1,0:T(8,128)S(1)} collective-permute-done((f32[256,128]{1,0:T(8,128)S(1)}, f32[256,128]{1,0:T(8,128)S(1)}, u32[]{:S(2)}, u32[]{:S(2)}) %collective-permute-start.1) | collective-permute-done | bytes 131104 | tf_op jit(solution)/shard_map/ppermute | solution.py:155
  35.9 4.4 %collective-permute-start.2 = (f32[128,128]{1,0:T(8,128)S(1)}, f32[128,128]{1,0:T(8,128)S(1)}, u32[]{:S(2)}, u32[]{:S(2)}) collective-permute-start(f32[128,128]{1,0:T(8,128)S(1)} %constant_dynamic-slice_fusion.3), channel_id=1, source_target_pairs={{0,32},{8,40},{16,48},{24,56},{32,0},{40,8},{48,16},{56,24},{64,96... | collective-permute-start | bytes 196616 | tf_op jit(solution)/shard_map/ppermute | solution.py:155
  40.4 3.8 %collective-permute-done.2 = f32[128,128]{1,0:T(8,128)S(1)} collective-permute-done((f32[128,128]{1,0:T(8,128)S(1)}, f32[128,128]{1,0:T(8,128)S(1)}, u32[]{:S(2)}, u32[]{:S(2)}) %collective-permute-start.2) | collective-permute-done | bytes 65568 | tf_op jit(solution)/shard_map/ppermute | solution.py:155
  44.2 3.9 %collective-permute-start.3 = (f32[64,128]{1,0:T(8,128)S(1)}, f32[64,128]{1,0:T(8,128)S(1)}, u32[]{:S(2)}, u32[]{:S(2)}) collective-permute-start(f32[64,128]{1,0:T(8,128)S(1)} %constant_dynamic-slice_fusion.2), channel_id=1, source_target_pairs={{0,64},{8,72},{16,80},{24,88},{32,96},{40,104},{48,112},{56,120},{... | collective-permute-start | bytes 98312 | tf_op jit(solution)/shard_map/ppermute | solution.py:155
  48.1 18.3 %collective-permute-done.3 = f32[64,128]{1,0:T(8,128)S(1)} collective-permute-done((f32[64,128]{1,0:T(8,128)S(1)}, f32[64,128]{1,0:T(8,128)S(1)}, u32[]{:S(2)}, u32[]{:S(2)}) %collective-permute-start.3) | collective-permute-done | bytes 32800 | tf_op jit(solution)/shard_map/ppermute | solution.py:155
  66.5 3.9 %collective-permute-start.4 = (f32[32,128]{1,0:T(8,128)S(1)}, f32[32,128]{1,0:T(8,128)S(1)}, u32[]{:S(2)}, u32[]{:S(2)}) collective-permute-start(f32[32,128]{1,0:T(8,128)S(1)} %constant_dynamic-slice_fusion.1), channel_id=1, source_target_pairs={{0,128},{8,136},{16,144},{24,152},{32,160},{40,168},{48,176},{56,1... | collective-permute-start | bytes 49160 | tf_op jit(solution)/shard_map/ppermute | solution.py:155
  70.4 2.6 %collective-permute-done.4 = f32[32,128]{1,0:T(8,128)S(1)} collective-permute-done((f32[32,128]{1,0:T(8,128)S(1)}, f32[32,128]{1,0:T(8,128)S(1)}, u32[]{:S(2)}, u32[]{:S(2)}) %collective-permute-start.4) | collective-permute-done | bytes 16416 | tf_op jit(solution)/shard_map/ppermute | solution.py:155
  73.0 6.9 %collective-permute-start.5 = (f32[16,128]{1,0:T(8,128)S(1)}, f32[16,128]{1,0:T(8,128)S(1)}, u32[]{:S(2)}, u32[]{:S(2)}) collective-permute-start(f32[16,128]{1,0:T(8,128)S(1)} %constant_dynamic-slice_fusion), channel_id=1, source_target_pairs={{0,256},{8,264},{16,272},{24,280},{32,288},{40,296},{48,304},{56,3... | collective-permute-start | bytes 24584 | tf_op jit(solution)/shard_map/ppermute | solution.py:155
  79.9 2.5 %collective-permute-done.5 = f32[16,128]{1,0:T(8,128)S(1)} collective-permute-done((f32[16,128]{1,0:T(8,128)S(1)}, f32[16,128]{1,0:T(8,128)S(1)}, u32[]{:S(2)}, u32[]{:S(2)}) %collective-permute-start.5) | collective-permute-done | bytes 8224 | tf_op jit(solution)/shard_map/ppermute | solution.py:155
  82.5 9.2 %cold_sum.1 = f32[8,144,128]{2,1,0:T(8,128)S(1)} custom-call(bf16[64,136,128]{2,1,0:T(8,128)(2,1)S(1)} %all-to-all-done.x_ref, f32[16,128]{1,0:T(8,128)S(1)} %dynamic-slice_add_fusion.5.hot_ref), custom_call_target="tpu_custom_call" | custom-call | flops 2147483648 | bytes 3145728 | tf_op jit(solution)/shard_map/cold_sum/pallas_call | solution.py:136
  91.7 26.6 %all_to_all.10 = f32[8,144,128]{2,1,0:T(8,128)S(1)} all-to-all(f32[8,144,128]{2,1,0:T(8,128)S(1)} %cold_sum.1), channel_id=1, replica_groups=mesh['shard'=64,'rep'=8] {'rep'}, dimensions={0} | all-to-all | bytes 1179648 | tf_op jit(solution)/shard_map/all_to_all | solution.py:174
  118.4 7.3 %collective-permute-start.6 = (f32[16,128]{1,0:T(8,128)S(1)}, f32[16,128]{1,0:T(8,128)S(1)}, u32[]{:S(2)}, u32[]{:S(2)}) collective-permute-start(f32[16,128]{1,0:T(8,128)S(1)} %slice.9), channel_id=1, source_target_pairs={{0,256},{8,264},{16,272},{24,280},{32,288},{40,296},{48,304},{56,3... | collective-permute-start | bytes 24584 | tf_op jit(solution)/shard_map/ppermute | solution.py:161
  125.7 2.3 %collective-permute-done.6 = f32[16,128]{1,0:T(8,128)S(1)} collective-permute-done((f32[16,128]{1,0:T(8,128)S(1)}, f32[16,128]{1,0:T(8,128)S(1)}, u32[]{:S(2)}, u32[]{:S(2)}) %collective-permute-start.6) | collective-permute-done | bytes 8224 | tf_op jit(solution)/shard_map/ppermute | solution.py:161
  128.0 3.8 %collective-permute-start.7 = (f32[32,128]{1,0:T(8,128)S(1)}, f32[32,128]{1,0:T(8,128)S(1)}, u32[]{:S(2)}, u32[]{:S(2)}) collective-permute-start(f32[32,128]{1,0:T(8,128)S(1)} %maximum_select_fusion.5), channel_id=1, source_target_pairs={{0,128},{8,136},{16,144},{24,152},{32,160},{40,168},{48,176},{56,1... | collective-permute-start | bytes 49160 | tf_op jit(solution)/shard_map/ppermute | solution.py:161
  131.8 2.7 %collective-permute-done.7 = f32[32,128]{1,0:T(8,128)S(1)} collective-permute-done((f32[32,128]{1,0:T(8,128)S(1)}, f32[32,128]{1,0:T(8,128)S(1)}, u32[]{:S(2)}, u32[]{:S(2)}) %collective-permute-start.7) | collective-permute-done | bytes 16416 | tf_op jit(solution)/shard_map/ppermute | solution.py:161
  134.5 2.9 %collective-permute-start.8 = (f32[64,128]{1,0:T(8,128)S(1)}, f32[64,128]{1,0:T(8,128)S(1)}, u32[]{:S(2)}, u32[]{:S(2)}) collective-permute-start(f32[64,128]{1,0:T(8,128)S(1)} %maximum_select_fusion.4), channel_id=1, source_target_pairs={{0,64},{8,72},{16,80},{24,88},{32,96},{40,104},{48,112},{56,120},{... | collective-permute-start | bytes 98312 | tf_op jit(solution)/shard_map/ppermute | solution.py:161
  137.4 25.5 %all_gather.3 = f32[1024,128]{1,0:T(8,128)S(1)} all-gather(f32[128,128]{1,0:T(8,128)S(1)} %slice.8), channel_id=1, replica_groups=mesh['shard'=64,'rep'=8] {'rep'}, dimensions={0}, use_global_device_ids=true | all-gather | bytes 589824 | tf_op jit(solution)/shard_map/all_gather | solution.py:176
  162.9 3.3 %collective-permute-start.9 = (f32[128,128]{1,0:T(8,128)S(1)}, f32[128,128]{1,0:T(8,128)S(1)}, u32[]{:S(2)}, u32[]{:S(2)}) collective-permute-start(f32[128,128]{1,0:T(8,128)S(1)} %maximum_select_fusion.3), channel_id=1, source_target_pairs={{0,32},{8,40},{16,48},{24,56},{32,0},{40,8},{48,16},{56,24},{64,96... | collective-permute-start | bytes 196616 | tf_op jit(solution)/shard_map/ppermute | solution.py:161
  166.5 4.1 %collective-permute-done.9 = f32[128,128]{1,0:T(8,128)S(1)} collective-permute-done((f32[128,128]{1,0:T(8,128)S(1)}, f32[128,128]{1,0:T(8,128)S(1)}, u32[]{:S(2)}, u32[]{:S(2)}) %collective-permute-start.9) | collective-permute-done | bytes 65568 | tf_op jit(solution)/shard_map/ppermute | solution.py:161
  170.6 2.8 %collective-permute-start.10 = (f32[256,128]{1,0:T(8,128)S(1)}, f32[256,128]{1,0:T(8,128)S(1)}, u32[]{:S(2)}, u32[]{:S(2)}) collective-permute-start(f32[256,128]{1,0:T(8,128)S(1)} %maximum_select_fusion.2), channel_id=1, source_target_pairs={{0,16},{8,24},{16,0},{24,8},{32,48},{40,56},{48,32},{56,40},{64,80... | collective-permute-start | bytes 393224 | tf_op jit(solution)/shard_map/ppermute | solution.py:161
  173.4 0.6 sqrt_add_fusion.1
  174.0 3.4 %collective-permute-done.10 = f32[256,128]{1,0:T(8,128)S(1)} collective-permute-done((f32[256,128]{1,0:T(8,128)S(1)}, f32[256,128]{1,0:T(8,128)S(1)}, u32[]{:S(2)}, u32[]{:S(2)}) %collective-permute-start.10) | collective-permute-done | bytes 131104 | tf_op jit(solution)/shard_map/ppermute | solution.py:161
  177.5 1.9 %collective-permute-start.11 = (f32[512,128]{1,0:T(8,128)S(1)}, f32[512,128]{1,0:T(8,128)S(1)}, u32[]{:S(2)}, u32[]{:S(2)}) collective-permute-start(f32[512,128]{1,0:T(8,128)S(1)} %maximum_select_fusion.1), channel_id=1, source_target_pairs={{0,8},{8,0},{16,24},{24,16},{32,40},{40,32},{48,56},{56,48},{64,72... | collective-permute-start | bytes 786440 | tf_op jit(solution)/shard_map/ppermute | solution.py:161
  179.4 1.0 divide_subtract_fusion.1
  181.8 1.0 divide_subtract_fusion
  (41 shorter events, 1.9 us)
Async XLA Ops:
  0.6 3.0 %copy-start.4 = (s32[128,64]{0,1:T(8,128)S(1)}, s32[128,64]{0,1:T(8,128)}, u32[]{:S(2)}) copy-start(s32[128,64]{0,1:T(8,128)} %param.10) | copy-start | bytes 98308
  0.6 3.0 %copy-start.3 = (s32[128,64,8]{0,2,1:T(8,128)S(1)}, s32[128,64,8]{0,2,1:T(8,128)}, u32[]{:S(2)}) copy-start(s32[128,64,8]{0,2,1:T(8,128)} %param.9) | copy-start | bytes 786436
  5.3 10.8 %copy-start = (s32[128,64,2]{0,2,1:T(2,128)S(1)}, s32[128,64,2]{0,2,1:T(2,128)}, u32[]{:S(2)}) copy-start(s32[128,64,2]{0,2,1:T(2,128)} %param.11) | copy-start | bytes 196612
  5.3 77.2 %all-to-all-start = ((bf16[64,136,128]{2,1,0:T(8,128)(2,1)}), bf16[64,136,128]{2,1,0:T(8,128)(2,1)S(1)}, u32[]{:S(2)}, u32[]{:S(2)}) async-start(bf16[64,136,128]{2,1,0:T(8,128)(2,1)} %pad_maximum_fusion.x_ref), calls=%async_computation | async-start | bytes 4456448 | tf_op jit(solution)/shard_map/all_to_all | solution.py:169
  22.7 3.4 %collective-permute-start = (f32[512,128]{1,0:T(8,128)S(1)}, f32[512,128]{1,0:T(8,128)S(1)}, u32[]{:S(2)}, u32[]{:S(2)}) collective-permute-start(f32[512,128]{1,0:T(8,128)S(1)} %constant_dynamic-slice_fusion.5), channel_id=1, source_target_pairs={{0,8},{8,0},{16,24},{24,16},{32,40},{40,32},{48,56},{56,48},{64,72... | collective-permute-start | bytes 786440 | tf_op jit(solution)/shard_map/ppermute | solution.py:155
  26.2 9.7 %collective-permute-start.1 = (f32[256,128]{1,0:T(8,128)S(1)}, f32[256,128]{1,0:T(8,128)S(1)}, u32[]{:S(2)}, u32[]{:S(2)}) collective-permute-start(f32[256,128]{1,0:T(8,128)S(1)} %constant_dynamic-slice_fusion.4), channel_id=1, source_target_pairs={{0,16},{8,24},{16,0},{24,8},{32,48},{40,56},{48,32},{56,40},{64,80... | collective-permute-start | bytes 393224 | tf_op jit(solution)/shard_map/ppermute | solution.py:155
  35.9 8.2 %collective-permute-start.2 = (f32[128,128]{1,0:T(8,128)S(1)}, f32[128,128]{1,0:T(8,128)S(1)}, u32[]{:S(2)}, u32[]{:S(2)}) collective-permute-start(f32[128,128]{1,0:T(8,128)S(1)} %constant_dynamic-slice_fusion.3), channel_id=1, source_target_pairs={{0,32},{8,40},{16,48},{24,56},{32,0},{40,8},{48,16},{56,24},{64,96... | collective-permute-start | bytes 196616 | tf_op jit(solution)/shard_map/ppermute | solution.py:155
  44.2 22.3 %collective-permute-start.3 = (f32[64,128]{1,0:T(8,128)S(1)}, f32[64,128]{1,0:T(8,128)S(1)}, u32[]{:S(2)}, u32[]{:S(2)}) collective-permute-start(f32[64,128]{1,0:T(8,128)S(1)} %constant_dynamic-slice_fusion.2), channel_id=1, source_target_pairs={{0,64},{8,72},{16,80},{24,88},{32,96},{40,104},{48,112},{56,120},{... | collective-permute-start | bytes 98312 | tf_op jit(solution)/shard_map/ppermute | solution.py:155
  66.5 6.5 %collective-permute-start.4 = (f32[32,128]{1,0:T(8,128)S(1)}, f32[32,128]{1,0:T(8,128)S(1)}, u32[]{:S(2)}, u32[]{:S(2)}) collective-permute-start(f32[32,128]{1,0:T(8,128)S(1)} %constant_dynamic-slice_fusion.1), channel_id=1, source_target_pairs={{0,128},{8,136},{16,144},{24,152},{32,160},{40,168},{48,176},{56,1... | collective-permute-start | bytes 49160 | tf_op jit(solution)/shard_map/ppermute | solution.py:155
  73.0 9.4 %collective-permute-start.5 = (f32[16,128]{1,0:T(8,128)S(1)}, f32[16,128]{1,0:T(8,128)S(1)}, u32[]{:S(2)}, u32[]{:S(2)}) collective-permute-start(f32[16,128]{1,0:T(8,128)S(1)} %constant_dynamic-slice_fusion), channel_id=1, source_target_pairs={{0,256},{8,264},{16,272},{24,280},{32,288},{40,296},{48,304},{56,3... | collective-permute-start | bytes 24584 | tf_op jit(solution)/shard_map/ppermute | solution.py:155
  91.7 81.7 %copy-start.5 = (f32[1024]{0:T(1024)S(1)}, f32[1024]{0:T(1024)}, u32[]{:S(2)}) copy-start(f32[1024]{0:T(1024)} %param.13) | copy-start | bytes 12292
  91.7 87.7 %copy-start.1 = (f32[1024,128]{1,0:T(8,128)S(1)}, f32[1024,128]{1,0:T(8,128)}, u32[]{:S(2)}) copy-start(f32[1024,128]{1,0:T(8,128)} %param.12) | copy-start | bytes 1572868
  118.4 62.8 %copy-start.6 = (f32[1024]{0:T(1024)S(1)}, f32[1024]{0:T(1024)}, u32[]{:S(2)}) copy-start(f32[1024]{0:T(1024)} %param.15) | copy-start | bytes 12292
  118.4 63.4 %copy-start.2 = (f32[1024,128]{1,0:T(8,128)S(1)}, f32[1024,128]{1,0:T(8,128)}, u32[]{:S(2)}) copy-start(f32[1024,128]{1,0:T(8,128)} %param.14) | copy-start | bytes 1572868
  118.4 9.6 %collective-permute-start.6 = (f32[16,128]{1,0:T(8,128)S(1)}, f32[16,128]{1,0:T(8,128)S(1)}, u32[]{:S(2)}, u32[]{:S(2)}) collective-permute-start(f32[16,128]{1,0:T(8,128)S(1)} %slice.9), channel_id=1, source_target_pairs={{0,256},{8,264},{16,272},{24,280},{32,288},{40,296},{48,304},{56,3... | collective-permute-start | bytes 24584 | tf_op jit(solution)/shard_map/ppermute | solution.py:161
  128.0 6.5 %collective-permute-start.7 = (f32[32,128]{1,0:T(8,128)S(1)}, f32[32,128]{1,0:T(8,128)S(1)}, u32[]{:S(2)}, u32[]{:S(2)}) collective-permute-start(f32[32,128]{1,0:T(8,128)S(1)} %maximum_select_fusion.5), channel_id=1, source_target_pairs={{0,128},{8,136},{16,144},{24,152},{32,160},{40,168},{48,176},{56,1... | collective-permute-start | bytes 49160 | tf_op jit(solution)/shard_map/ppermute | solution.py:161
  134.5 28.4 %collective-permute-start.8 = (f32[64,128]{1,0:T(8,128)S(1)}, f32[64,128]{1,0:T(8,128)S(1)}, u32[]{:S(2)}, u32[]{:S(2)}) collective-permute-start(f32[64,128]{1,0:T(8,128)S(1)} %maximum_select_fusion.4), channel_id=1, source_target_pairs={{0,64},{8,72},{16,80},{24,88},{32,96},{40,104},{48,112},{56,120},{... | collective-permute-start | bytes 98312 | tf_op jit(solution)/shard_map/ppermute | solution.py:161
  162.9 7.7 %collective-permute-start.9 = (f32[128,128]{1,0:T(8,128)S(1)}, f32[128,128]{1,0:T(8,128)S(1)}, u32[]{:S(2)}, u32[]{:S(2)}) collective-permute-start(f32[128,128]{1,0:T(8,128)S(1)} %maximum_select_fusion.3), channel_id=1, source_target_pairs={{0,32},{8,40},{16,48},{24,56},{32,0},{40,8},{48,16},{56,24},{64,96... | collective-permute-start | bytes 196616 | tf_op jit(solution)/shard_map/ppermute | solution.py:161
  170.6 6.9 %collective-permute-start.10 = (f32[256,128]{1,0:T(8,128)S(1)}, f32[256,128]{1,0:T(8,128)S(1)}, u32[]{:S(2)}, u32[]{:S(2)}) collective-permute-start(f32[256,128]{1,0:T(8,128)S(1)} %maximum_select_fusion.2), channel_id=1, source_target_pairs={{0,16},{8,24},{16,0},{24,8},{32,48},{40,56},{48,32},{56,40},{64,80... | collective-permute-start | bytes 393224 | tf_op jit(solution)/shard_map/ppermute | solution.py:161
  177.5 3.4 %collective-permute-start.11 = (f32[512,128]{1,0:T(8,128)S(1)}, f32[512,128]{1,0:T(8,128)S(1)}, u32[]{:S(2)}, u32[]{:S(2)}) collective-permute-start(f32[512,128]{1,0:T(8,128)S(1)} %maximum_select_fusion.1), channel_id=1, source_target_pairs={{0,8},{8,0},{16,24},{24,16},{32,40},{40,32},{48,56},{56,48},{64,72... | collective-permute-start | bytes 786440 | tf_op jit(solution)/shard_map/ppermute | solution.py:161

commit v2 on v1

--- a/solution.py
+++ b/solution.py
@@ -11,14 +11,12 @@
 GROUP = 128
 FIELDS = 8
 BITS = 4
+TILE = 16
 
 learning_rate = 0.5
 epsilon = 1e-06
 
-
-def adagrad(weights, accumulator, grad):
-    fresh = accumulator + jnp.mean(grad * grad, axis=1)
-    return (weights - learning_rate * grad / (jnp.sqrt(fresh)[:, None] + epsilon), fresh)
+PARAMS = pltpu.CompilerParams(vmem_limit_bytes=40 << 20)
 
 
 def encode_ids(cold_ids, lengths):
@@ -58,6 +56,10 @@
     return jnp.concatenate(groups, 0)
 
 
+def field_scale(field):
+    return 2.0 ** (-BITS * field) if field < FIELDS - 1 else 1.0
+
+
 def block_sum(bags, values, pair):
     total = None
     for first in range(0, len(bags), pair):
@@ -68,6 +70,37 @@
     return total
 
 
+def diagonal(rows):
+    shape = (rows, GROUP)
+    return lax.broadcasted_iota(jnp.int32, shape, 0) == lax.broadcasted_iota(jnp.int32, shape, 1)
+
+
+def to_row(column):
+    return jnp.sum(jnp.where(diagonal(column.shape[0]), column, 0.0), axis=0, keepdims=True)
+
+
+def to_column(row, rows=GROUP):
+    return jnp.sum(jnp.where(diagonal(rows), row, 0.0), axis=1, keepdims=True)
+
+
+def quantized(x):
+    top = jnp.maximum(jnp.max(jnp.abs(x), axis=1, keepdims=True), 1e-30)
+    level = jnp.ceil(8.0 * jnp.log2(top) + 0.05)
+    return jnp.round(x * jnp.exp2(15.0 - level * 0.125)).astype(jnp.int32).astype(jnp.int16), level
+
+
+def restored(codes, level):
+    return codes.astype(jnp.int32).astype(jnp.float32) * jnp.exp2(level * 0.125 - 15.0)
+
+
+def level_tile(level):
+    return jnp.broadcast_to(to_row(level), (TILE, GROUP)).astype(jnp.int32).astype(jnp.int16)
+
+
+def tile_level(tile):
+    return to_column(tile.astype(jnp.int32).astype(jnp.float32)[0:1])
+
+
 def hot_kernel(x_ref, ids_ref, out_ref, *, blocks, pair):
     step = pl.program_id(0)
 
@@ -86,7 +119,7 @@
     @pl.when(step == pl.num_programs(0) - 1)
     def _():
         for field in range(1, FIELDS - 1):
-            out_ref[field * GROUP : (field + 1) * GROUP, :] *= 2.0 ** (-BITS * field)
+            out_ref[field * GROUP : (field + 1) * GROUP, :] *= field_scale(field)
 
 
 def hot_sum(rows, ids, blocks=16, pair=4):
@@ -100,85 +133,147 @@
         ],
         out_specs=pl.BlockSpec((V, width), lambda i: (0, 0)),
         out_shape=jax.ShapeDtypeStruct((V, width), jnp.float32),
-        compiler_params=pltpu.CompilerParams(vmem_limit_bytes=40 << 20),
+        compiler_params=PARAMS,
         cost_estimate=pl.CostEstimate(flops=2 * V * count * GROUP * width, bytes_accessed=3 << 20, transcendentals=0),
         name="hot_sum",
     )(rows, ids)
 
 
-def cold_kernel(x_ref, hot_ref, out_ref, *, blocks, pair):
+def cold_kernel(x_ref, out_ref, total_ref, *, blocks, pair):
     step = pl.program_id(0)
 
     @pl.when(step == 0)
     def _():
-        out_ref[...] = jnp.zeros_like(out_ref)
+        total_ref[...] = jnp.zeros_like(total_ref)
 
     bags, values = [], []
     for block in range(blocks):
         code = x_ref[block, GROUP : GROUP + 8, :].astype(jnp.float32)
         bags.append(decode_ids(code))
         values.append(x_ref[block, 0:GROUP, :])
-    total = block_sum(bags, values, pair)
-    for field in range(FIELDS):
-        out_ref[field, 0:GROUP, :] += total[field * GROUP : (field + 1) * GROUP]
+    total_ref[...] += block_sum(bags, values, pair)
 
     @pl.when(step == pl.num_programs(0) - 1)
     def _():
         for field in range(FIELDS):
-            if 0 < field < FIELDS - 1:
-                out_ref[field, 0:GROUP, :] *= 2.0 ** (-BITS * field)
-            out_ref[field, GROUP:, :] = hot_ref[...]
-
-
-def cold_sum(rows, hot_rows, blocks=16, pair=4):
+            rows = total_ref[field * GROUP : (field + 1) * GROUP, :] * field_scale(field)
+            codes, level = quantized(rows)
+            out_ref[field, 0:GROUP, :] = codes
+            out_ref[field, GROUP:, :] = level_tile(level)
+
+
+def cold_sum(rows, blocks=16, pair=4):
     count, height, width = rows.shape
-    tall = GROUP + hot_rows.shape[0]
     return pl.pallas_call(
         functools.partial(cold_kernel, blocks=blocks, pair=pair),
         grid=(count // blocks,),
-        in_specs=[
-            pl.BlockSpec((blocks, height, width), lambda i: (i, 0, 0)),
-            pl.BlockSpec(hot_rows.shape, lambda i: (0, 0)),
-        ],
-        out_specs=pl.BlockSpec((FIELDS, tall, width), lambda i: (0, 0, 0)),
-        out_shape=jax.ShapeDtypeStruct((FIELDS, tall, width), jnp.float32),
-        compiler_params=pltpu.CompilerParams(vmem_limit_bytes=40 << 20),
-        cost_estimate=pl.CostEstimate(flops=2 * V * count * GROUP * width, bytes_accessed=3 << 20, transcendentals=0),
+        in_specs=[pl.BlockSpec((blocks, height, width), lambda i: (i, 0, 0))],
+        out_specs=pl.BlockSpec((FIELDS, GROUP + TILE, width), lambda i: (0, 0, 0)),
+        out_shape=jax.ShapeDtypeStruct((FIELDS, GROUP + TILE, width), jnp.int16),
+        scratch_shapes=[pltpu.VMEM((V, width), jnp.float32)],
+        compiler_params=PARAMS,
+        cost_estimate=pl.CostEstimate(flops=10 * V * count * GROUP * width, bytes_accessed=3 << 20, transcendentals=0),
         name="cold_sum",
-    )(rows, hot_rows)
-
-
-def halve(rows, axis, size, bit):
+    )(rows)
+
+
+def whole(body, out_shape, name, *operands):
+    return pl.pallas_call(body, out_shape=out_shape, compiler_params=PARAMS, name=name)(*operands)
+
+
+def stored_everywhere(rows, out_ref):
+    codes, level = quantized(rows)
+    tile = level_tile(level)
+    for peer in range(FIELDS):
+        out_ref[peer, 0:GROUP, :] = codes
+        out_ref[peer, GROUP:, :] = tile
+
+
+def peer_sum(pieces_ref):
+    total = None
+    for peer in range(FIELDS):
+        piece = restored(pieces_ref[peer, 0:GROUP, :], tile_level(pieces_ref[peer, GROUP:, :]))
+        total = piece if total is None else total + piece
+    return total
+
+
+def spread(rows_ref, out_ref):
+    stored_everywhere(rows_ref[...], out_ref)
+
+
+def gathered_total(pieces_ref, out_ref):
+    out_ref[...] = peer_sum(pieces_ref)
+
+
+def replica_total(pieces_ref, out_ref):
+    stored_everywhere(peer_sum(pieces_ref), out_ref)
+
+
+def update_group(group, grad, table_ref, accum_ref, new_table_ref, new_accum_ref):
+    rows = slice(group * GROUP, (group + 1) * GROUP)
+    fresh = to_column(accum_ref[group : group + 1, :]) + jnp.sum(grad * grad, axis=1, keepdims=True) * (1.0 / GROUP)
+    new_table_ref[rows, :] = table_ref[rows, :] - grad * (learning_rate / (jnp.sqrt(fresh) + epsilon))
+    new_accum_ref[group : group + 1, :] = to_row(fresh)
+
+
+def cold_update(codes_ref, table_ref, accum_ref, new_table_ref, new_accum_ref):
+    for group in range(FIELDS):
+        grad = restored(codes_ref[group, 0:GROUP, :], tile_level(codes_ref[group, GROUP:, :]))
+        update_group(group, grad, table_ref, accum_ref, new_table_ref, new_accum_ref)
+
+
+def hot_update(grad_ref, table_ref, accum_ref, new_table_ref, new_accum_ref):
+    for group in range(FIELDS):
+        grad = grad_ref[group * GROUP : (group + 1) * GROUP, :]
+        update_group(group, grad, table_ref, accum_ref, new_table_ref, new_accum_ref)
+
+
+def updated(body, name, grad, table, accum):
+    shapes = (
+        jax.ShapeDtypeStruct(table.shape, jnp.float32),
+        jax.ShapeDtypeStruct((FIELDS, GROUP), jnp.float32),
+    )
+    new_table, new_accum = whole(body, shapes, name, grad, table, accum.reshape(FIELDS, GROUP))
+    return new_table, new_accum.reshape(V)
+
+
+def halve(rows, axis, bit):
     half = rows.shape[0] // 2
     mine = (lax.axis_index(axis) // bit) % 2
-    pairs = [(i, i ^ bit) for i in range(size)]
+    pairs = [(i, i ^ bit) for i in range(lax.axis_size(axis))]
     got = lax.ppermute(lax.dynamic_slice_in_dim(rows, (1 - mine) * half, half), axis, pairs)
     return lax.dynamic_slice_in_dim(rows, mine * half, half) + got
 
 
-def double(rows, axis, size, bit):
+def double(rows, axis, bit):
     mine = (lax.axis_index(axis) // bit) % 2
-    got = lax.ppermute(rows, axis, [(i, i ^ bit) for i in range(size)])
+    got = lax.ppermute(rows, axis, [(i, i ^ bit) for i in range(lax.axis_size(axis))])
     return jnp.where(mine == 0, jnp.concatenate([rows, got], 0), jnp.concatenate([got, rows], 0))
 
 
 def per_device(pooled_grad, cold_ids, lengths, hot_ids, table, accum, hot_table, hot_accum):
-    shards = lax.axis_size("shard")
-    bits = [1 << b for b in range(6)]
+    lines = [[y * 8 + inner for y in range(8)] for inner in range(8)]
+    coded = jax.ShapeDtypeStruct((FIELDS, GROUP + TILE, GROUP), jnp.int16)
     rows = jnp.concatenate([jnp.transpose(pooled_grad, (1, 0, 2)), encode_ids(cold_ids, lengths)], 1)
     moved = lax.all_to_all(rows, "shard", split_axis=0, concat_axis=0, tiled=True)
     hot = hot_sum(rows, jnp.transpose(hot_ids, (1, 2, 0)))
-    for bit in bits:
-        hot = halve(hot, "shard", shards, bit)
-    pieces = cold_sum(moved, hot)
+    for bit in (1, 2, 4):
+        hot = halve(hot, "shard", bit)
+    for bit in (1, 2, 4):
+        hot = hot + lax.ppermute(hot, "rep", [(i, i ^ bit) for i in range(FIELDS)])
+    hot = whole(spread, coded, "spread", hot)
+    moved, hot = lax.optimization_barrier((moved, hot))
+    hot = lax.all_to_all(hot, "shard", split_axis=0, concat_axis=0, axis_index_groups=lines, tiled=True)
+    pieces = cold_sum(moved)
+    pieces, hot = lax.optimization_barrier((pieces, hot))
     shared = lax.all_to_all(pieces, "rep", split_axis=0, concat_axis=0, tiled=True)
-    total = jnp.sum(shared, axis=0)
-    cold_total = lax.all_gather(total[:GROUP], "rep", tiled=True)
-    hot = total[GROUP:]
-    for bit in reversed(bits):
-        hot = double(hot, "shard", shards, bit)
-    new_table, new_accum = adagrad(table, accum, cold_total)
-    new_hot_table, new_hot_accum = adagrad(hot_table, hot_accum, hot)
+    hot = whole(gathered_total, jax.ShapeDtypeStruct((GROUP, GROUP), jnp.float32), "gathered_total", hot)
+    payload = whole(replica_total, coded, "replica_total", shared)
+    codes = lax.all_to_all(payload, "rep", split_axis=0, concat_axis=0, tiled=True)
+    for bit in (4, 2, 1):
+        hot = double(hot, "shard", bit)
+    new_hot_table, new_hot_accum = updated(hot_update, "hot_update", hot, hot_table, hot_accum)
+    new_table, new_accum = updated(cold_update, "cold_update", codes, table, accum)
     return (new_table, new_accum, new_hot_table, new_hot_accum)
 
 

time: 184 us -> 131 us (0.71)
  blocking collectives: 52.1 us -> 0 us
  waiting for transfers between devices: 48.5 us -> 32.3 us
  starting transfers between devices: 56.6 us -> 69.7 us
  Pallas kernels: 15.8 us -> 21.8 us
  other arithmetic: 5.41 us -> 1.82 us
    all_to_all x1 -> x0, blocking collectives: 26.6 us -> none  [per_device(): lax.all_to_all(pieces, 'rep', split_axis=0, concat_axis=0, tiled=True)]
    all_gather x1 -> x0, blocking collectives: 25.5 us -> none  [per_device(): cold_total = lax.all_gather(total[:GROUP], 'rep', tiled=True)]
    ppermute x6 -> x3, waiting for transfers between devices: 35.4 us -> 12 us  [halve(): lax.ppermute(lax.dynamic_slice_in_dim(rows, (1 - mine) * half, half), axi...]
    all_to_all x0 -> x3, starting transfers between devices: none -> 22.3 us  [the longest x1 8.36 us: per_device(): lax.all_to_all(pieces, 'rep', split_axis=0, concat_axis=0, tiled=True)]
    ppermute x6 -> x3, starting transfers between devices: 23.9 us -> 9.25 us  [halve(): lax.ppermute(lax.dynamic_slice_in_dim(rows, (1 - mine) * half, half), axi...]
    all_to_all x0 -> x3, waiting for transfers between devices: none -> 6.73 us  [the longest x1 6.1 us: per_device(): lax.all_to_all(payload, 'rep', split_axis=0, concat_axis=0, tiled=True)]
    ppermute x6, starting transfers between devices: 22 us -> 27.4 us  [the longest x3 19.6 us: per_device(): hot = hot + lax.ppermute(hot, 'rep', [(i, i ^ bit) for i in range(FIELDS)])]
    pallas_call x0 -> x5, Pallas kernels: none -> 4.98 us  [whole(): pl.pallas_call(body, out_shape=out_shape, compiler_params=PARAMS, name=name)]
  transfers between devices with their start and end apart: 13 -> 13, of which waited for: 11 -> 10; matrix products, arithmetic and copies ran while one was open for 1% -> 0% of each run, Pallas kernels for 4% -> 15%
where the time goes in v2:
time: 131 us; the launch traced here: 130 us
  starting transfers between devices  69.7 us (53%)
  waiting for transfers between devices  32.3 us (25%)
  Pallas kernels  21.8 us (17%)
  local copies, waits for them, and re-layouts  3.08 us (2%)
  other arithmetic  1.82 us (1%)
    ppermute x3, starting transfers between devices, per_device(): hot = hot + lax.ppermute(hot, 'rep', [(i, i ^ bit) for i in range(FIELDS)])  19.6 us
    ppermute x3, waiting for transfers between devices, halve(): lax.ppermute(lax.dynamic_slice_in_dim(rows, (1 - mine) * half, half), axi...  12 us
    all_to_all x1, starting transfers between devices, per_device(): lax.all_to_all(rows, 'shard', split_axis=0, concat_axis=0, tiled=True)  10.7 us
    pallas_call x1, Pallas kernels, cold_sum(): pl.pallas_call(functools.partial(cold_kernel, blocks=blocks, pair=pair),...  10.2 us
    ppermute x3, starting transfers between devices, halve(): lax.ppermute(lax.dynamic_slice_in_dim(rows, (1 - mine) * half, half), axi...  9.25 us
    all_to_all x1, starting transfers between devices, per_device(): lax.all_to_all(pieces, 'rep', split_axis=0, concat_axis=0, tiled=True)  8.36 us
    ppermute x3, starting transfers between devices, double(): lax.ppermute(rows, axis, [(i, i ^ bit) for i in range(lax.axis_size(axis))])  7.74 us
    all_to_all x1, starting transfers between devices, per_device(): lax.all_to_all(payload, 'rep', split_axis=0, concat_axis=0, tiled=True)  7.19 us
  transfers between devices with their start and end apart: 13, of which 10 were waited for; matrix products, arithmetic and copies ran while one was open for 0% of the time, Pallas kernels for 15%

profile of v2, /device:TPU:6, one launch (start us, length us, event | category | flops | bytes accessed | tf_op | source)
XLA Modules:
  0.0 129.7 jit_solution(8338528190900121327)
XLA Ops:
  0.7 3.0 %copy.14 = bf16[128,64,128]{2,0,1:T(8,128)(2,1)S(1)} copy(bf16[128,64,128]{2,1,0:T(8,128)(2,1)} %param.8) | data formatting | bytes 4194304 | tf_op args[0]
  3.7 1.6 %pad_maximum_fusion.x_ref = bf16[64,136,128]{2,1,0:T(8,128)(2,1)} fusion(bf16[64,8,128]{2,1,0:T(8,128)(2,1)S(1)} %fusion, bf16[64,128,128]{2,1,0:T(8,128)(2,1)S(1)} %bitcast.16), kind=kLoop, calls=%fused_computation | loop fusion | flops 4456448 | bytes 4456448 | tf_op jit(solution)/shard_map/concatenate | solution.py:257
  5.3 10.7 %all-to-all-start = ((bf16[64,136,128]{2,1,0:T(8,128)(2,1)}), bf16[64,136,128]{2,1,0:T(8,128)(2,1)S(1)}, u32[]{:S(2)}, u32[]{:S(2)}) async-start(bf16[64,136,128]{2,1,0:T(8,128)(2,1)} %pad_maximum_fusion.x_ref), calls=%async_computation | async-start | bytes 4456448 | tf_op jit(solution)/shard_map/all_to_all | solution.py:258
  16.1 6.6 %hot_sum.1 = f32[1024,128]{1,0:T(8,128)S(1)} custom-call(bf16[64,136,128]{2,1,0:T(8,128)(2,1)} %pad_maximum_fusion.x_ref, s32[64,2,128]{2,1,0:T(2,128)S(1)} %bitcast.15), custom_call_target="tpu_custom_call" | custom-call | flops 2147483648 | bytes 3145728 | tf_op jit(solution)/shard_map/hot_sum/pallas_call | solution.py:127
  22.7 2.1 %collective-permute-start = (f32[512,128]{1,0:T(8,128)S(1)}, f32[512,128]{1,0:T(8,128)S(1)}, u32[]{:S(2)}, u32[]{:S(2)}) collective-permute-start(f32[512,128]{1,0:T(8,128)S(1)} %constant_dynamic-slice_fusion.2), channel_id=1, source_target_pairs={{0,8},{8,0},{16,24},{24,16},{32,40},{40,32},{48,56},{56,48},{64,72... | collective-permute-start | bytes 786440 | tf_op jit(solution)/shard_map/ppermute | solution.py:244
  24.9 1.3 %collective-permute-done = f32[512,128]{1,0:T(8,128)S(1)} collective-permute-done((f32[512,128]{1,0:T(8,128)S(1)}, f32[512,128]{1,0:T(8,128)S(1)}, u32[]{:S(2)}, u32[]{:S(2)}) %collective-permute-start) | collective-permute-done | bytes 262176 | tf_op jit(solution)/shard_map/ppermute | solution.py:244
  26.2 2.8 %collective-permute-start.1 = (f32[256,128]{1,0:T(8,128)S(1)}, f32[256,128]{1,0:T(8,128)S(1)}, u32[]{:S(2)}, u32[]{:S(2)}) collective-permute-start(f32[256,128]{1,0:T(8,128)S(1)} %constant_dynamic-slice_fusion.1), channel_id=1, source_target_pairs={{0,16},{8,24},{16,0},{24,8},{32,48},{40,56},{48,32},{56,40},{64,80... | collective-permute-start | bytes 393224 | tf_op jit(solution)/shard_map/ppermute | solution.py:244
  29.0 6.9 %collective-permute-done.1 = f32[256,128]{1,0:T(8,128)S(1)} collective-permute-done((f32[256,128]{1,0:T(8,128)S(1)}, f32[256,128]{1,0:T(8,128)S(1)}, u32[]{:S(2)}, u32[]{:S(2)}) %collective-permute-start.1) | collective-permute-done | bytes 131104 | tf_op jit(solution)/shard_map/ppermute | solution.py:244
  36.0 4.4 %collective-permute-start.2 = (f32[128,128]{1,0:T(8,128)S(1)}, f32[128,128]{1,0:T(8,128)S(1)}, u32[]{:S(2)}, u32[]{:S(2)}) collective-permute-start(f32[128,128]{1,0:T(8,128)S(1)} %constant_dynamic-slice_fusion), channel_id=1, source_target_pairs={{0,32},{8,40},{16,48},{24,56},{32,0},{40,8},{48,16},{56,24},{64,96... | collective-permute-start | bytes 196616 | tf_op jit(solution)/shard_map/ppermute | solution.py:244
  40.4 3.8 %collective-permute-done.2 = f32[128,128]{1,0:T(8,128)S(1)} collective-permute-done((f32[128,128]{1,0:T(8,128)S(1)}, f32[128,128]{1,0:T(8,128)S(1)}, u32[]{:S(2)}, u32[]{:S(2)}) %collective-permute-start.2) | collective-permute-done | bytes 65568 | tf_op jit(solution)/shard_map/ppermute | solution.py:244
  44.2 4.3 %collective-permute-start.3 = (f32[128,128]{1,0:T(8,128)S(1)}, f32[128,128]{1,0:T(8,128)S(1)}, u32[]{:S(2)}, u32[]{:S(2)}) collective-permute-start(f32[128,128]{1,0:T(8,128)S(1)} %dynamic-slice_add_fusion.2), channel_id=1, source_target_pairs={{0,1},{1,0},{2,3},{3,2},{4,5},{5,4},{6,7},{7,6},{8,9},{9,8},{10,11... | collective-permute-start | bytes 196616 | tf_op jit(solution)/shard_map/ppermute | solution.py:263
  48.5 2.2 %collective-permute-done.3 = f32[128,128]{1,0:T(8,128)S(1)} collective-permute-done((f32[128,128]{1,0:T(8,128)S(1)}, f32[128,128]{1,0:T(8,128)S(1)}, u32[]{:S(2)}, u32[]{:S(2)}) %collective-permute-start.3) | collective-permute-done | bytes 65568 | tf_op jit(solution)/shard_map/ppermute | solution.py:263
  50.8 6.1 %collective-permute-start.4 = (f32[128,128]{1,0:T(8,128)S(1)}, f32[128,128]{1,0:T(8,128)S(1)}, u32[]{:S(2)}, u32[]{:S(2)}) collective-permute-start(f32[128,128]{1,0:T(8,128)S(1)} %add.73), channel_id=1, source_target_pairs={{0,2},{1,3},{2,0},{3,1},{4,6},{5,7},{6,4},{7,5},{8,10},{9,11},{10,... | collective-permute-start | bytes 196616 | tf_op jit(solution)/shard_map/ppermute | solution.py:263
  56.8 2.2 %collective-permute-done.4 = f32[128,128]{1,0:T(8,128)S(1)} collective-permute-done((f32[128,128]{1,0:T(8,128)S(1)}, f32[128,128]{1,0:T(8,128)S(1)}, u32[]{:S(2)}, u32[]{:S(2)}) %collective-permute-start.4) | collective-permute-done | bytes 65568 | tf_op jit(solution)/shard_map/ppermute | solution.py:263
  59.1 9.3 %collective-permute-start.5 = (f32[128,128]{1,0:T(8,128)S(1)}, f32[128,128]{1,0:T(8,128)S(1)}, u32[]{:S(2)}, u32[]{:S(2)}) collective-permute-start(f32[128,128]{1,0:T(8,128)S(1)} %add.74), channel_id=1, source_target_pairs={{0,4},{1,5},{2,6},{3,7},{4,0},{5,1},{6,2},{7,3},{8,12},{9,13},{10,... | collective-permute-start | bytes 196616 | tf_op jit(solution)/shard_map/ppermute | solution.py:263
  68.4 2.5 %collective-permute-done.5 = f32[128,128]{1,0:T(8,128)S(1)} collective-permute-done((f32[128,128]{1,0:T(8,128)S(1)}, f32[128,128]{1,0:T(8,128)S(1)}, u32[]{:S(2)}, u32[]{:S(2)}) %collective-permute-start.5) | collective-permute-done | bytes 65568 | tf_op jit(solution)/shard_map/ppermute | solution.py:263
  70.9 0.8 spread.1
  71.7 6.8 %all-to-all-start.1 = ((s16[8,144,128]{2,1,0:T(8,128)(2,1)}), s16[8,144,128]{2,1,0:T(8,128)(2,1)S(1)}, u32[]{:S(2)}, u32[]{:S(2)}) async-start(s16[8,144,128]{2,1,0:T(8,128)(2,1)} %spread.1), calls=%async_computation.1 | async-start | bytes 589824 | tf_op jit(solution)/shard_map/all_to_all | solution.py:266
  78.5 10.2 %cold_sum.1 = s16[8,144,128]{2,1,0:T(8,128)(2,1)} custom-call(bf16[64,136,128]{2,1,0:T(8,128)(2,1)S(1)} %all-to-all-done.x_ref), custom_call_target="tpu_custom_call" | custom-call | flops 10737418240 | bytes 3145728 | tf_op jit(solution)/shard_map/cold_sum/pallas_call | solution.py:167
  88.7 0.6 all-to-all-done.1.pieces_ref
  89.3 8.4 %all-to-all-start.2 = ((s16[8,144,128]{2,1,0:T(8,128)(2,1)}), s16[8,144,128]{2,1,0:T(8,128)(2,1)S(1)}, u32[]{:S(2)}, u32[]{:S(2)}) async-start(s16[8,144,128]{2,1,0:T(8,128)(2,1)} %cold_sum.1), calls=%async_computation.2 | async-start | bytes 589824 | tf_op jit(solution)/shard_map/all_to_all | solution.py:269
  97.7 0.2 gathered_total.1
  97.9 2.9 %collective-permute-start.6 = (f32[128,128]{1,0:T(8,128)S(1)}, f32[128,128]{1,0:T(8,128)S(1)}, u32[]{:S(2)}, u32[]{:S(2)}) collective-permute-start(f32[128,128]{1,0:T(8,128)S(1)} %gathered_total.1), channel_id=1, source_target_pairs={{0,32},{8,40},{16,48},{24,56},{32,0},{40,8},{48,16},{56,24},{64,96... | collective-permute-start | bytes 196616 | tf_op jit(solution)/shard_map/ppermute | solution.py:250
  100.9 5.1 %collective-permute-done.6 = f32[128,128]{1,0:T(8,128)S(1)} collective-permute-done((f32[128,128]{1,0:T(8,128)S(1)}, f32[128,128]{1,0:T(8,128)S(1)}, u32[]{:S(2)}, u32[]{:S(2)}) %collective-permute-start.6) | collective-permute-done | bytes 65568 | tf_op jit(solution)/shard_map/ppermute | solution.py:250
  106.0 2.9 %collective-permute-start.7 = (f32[256,128]{1,0:T(8,128)S(1)}, f32[256,128]{1,0:T(8,128)S(1)}, u32[]{:S(2)}, u32[]{:S(2)}) collective-permute-start(f32[256,128]{1,0:T(8,128)S(1)} %maximum_select_fusion.2), channel_id=1, source_target_pairs={{0,16},{8,24},{16,0},{24,8},{32,48},{40,56},{48,32},{56,40},{64,80... | collective-permute-start | bytes 393224 | tf_op jit(solution)/shard_map/ppermute | solution.py:250
  108.9 1.0 replica_total.1
  110.0 7.2 %all-to-all-start.3 = ((s16[8,144,128]{2,1,0:T(8,128)(2,1)}), s16[8,144,128]{2,1,0:T(8,128)(2,1)S(1)}, u32[]{:S(2)}, u32[]{:S(2)}) async-start(s16[8,144,128]{2,1,0:T(8,128)(2,1)} %replica_total.1), calls=%async_computation.3 | async-start | bytes 589824 | tf_op jit(solution)/shard_map/all_to_all | solution.py:272
  117.2 1.9 %collective-permute-start.8 = (f32[512,128]{1,0:T(8,128)S(1)}, f32[512,128]{1,0:T(8,128)S(1)}, u32[]{:S(2)}, u32[]{:S(2)}) collective-permute-start(f32[512,128]{1,0:T(8,128)S(1)} %maximum_select_fusion.1), channel_id=1, source_target_pairs={{0,8},{8,0},{16,24},{24,16},{32,40},{40,32},{48,56},{56,48},{64,72... | collective-permute-start | bytes 786440 | tf_op jit(solution)/shard_map/ppermute | solution.py:250
  119.1 1.5 %collective-permute-done.8 = f32[512,128]{1,0:T(8,128)S(1)} collective-permute-done((f32[512,128]{1,0:T(8,128)S(1)}, f32[512,128]{1,0:T(8,128)S(1)}, u32[]{:S(2)}, u32[]{:S(2)}) %collective-permute-start.8) | collective-permute-done | bytes 262176 | tf_op jit(solution)/shard_map/ppermute | solution.py:250
  120.7 1.2 hot_update.1
  121.9 6.1 %all-to-all-done.3.codes_ref = s16[8,144,128]{2,1,0:T(8,128)(2,1)S(1)} async-done(((s16[8,144,128]{2,1,0:T(8,128)(2,1)}), s16[8,144,128]{2,1,0:T(8,128)(2,1)S(1)}, u32[]{:S(2)}, u32[]{:S(2)}) %all-to-all-start.3) | async-done | bytes 294944 | tf_op jit(solution)/shard_map/all_to_all | solution.py:272
  128.0 1.7 %cold_update.1 = (f32[1024,128]{1,0:T(8,128)}, f32[8,128]{1,0:T(8,128)}) custom-call(s16[8,144,128]{2,1,0:T(8,128)(2,1)S(1)} %all-to-all-done.3.codes_ref, f32[1024,128]{1,0:T(8,128)S(1)} %copy-done.1, f32[8,128]{1,0:T(8,128)S(1)} %bitcast.14), custom_call_target="tpu_custom_call" | custom-call | tf_op jit(solution)/shard_map/cold_update/pallas_call | solution.py:181
  (30 shorter events, 0.3 us)
Async XLA Ops:
  0.6 3.0 %copy-start.6 = (s32[128,64]{0,1:T(8,128)S(1)}, s32[128,64]{0,1:T(8,128)}, u32[]{:S(2)}) copy-start(s32[128,64]{0,1:T(8,128)} %param.10) | copy-start | bytes 98308
  0.6 3.0 %copy-start.5 = (s32[128,64,8]{0,2,1:T(8,128)S(1)}, s32[128,64,8]{0,2,1:T(8,128)}, u32[]{:S(2)}) copy-start(s32[128,64,8]{0,2,1:T(8,128)} %param.9) | copy-start | bytes 786436
  5.3 10.8 %copy-start.4 = (s32[128,64,2]{0,2,1:T(2,128)S(1)}, s32[128,64,2]{0,2,1:T(2,128)}, u32[]{:S(2)}) copy-start(s32[128,64,2]{0,2,1:T(2,128)} %param.11) | copy-start | bytes 196612
  5.3 66.4 %all-to-all-start = ((bf16[64,136,128]{2,1,0:T(8,128)(2,1)}), bf16[64,136,128]{2,1,0:T(8,128)(2,1)S(1)}, u32[]{:S(2)}, u32[]{:S(2)}) async-start(bf16[64,136,128]{2,1,0:T(8,128)(2,1)} %pad_maximum_fusion.x_ref), calls=%async_computation | async-start | bytes 4456448 | tf_op jit(solution)/shard_map/all_to_all | solution.py:258
  22.7 3.4 %collective-permute-start = (f32[512,128]{1,0:T(8,128)S(1)}, f32[512,128]{1,0:T(8,128)S(1)}, u32[]{:S(2)}, u32[]{:S(2)}) collective-permute-start(f32[512,128]{1,0:T(8,128)S(1)} %constant_dynamic-slice_fusion.2), channel_id=1, source_target_pairs={{0,8},{8,0},{16,24},{24,16},{32,40},{40,32},{48,56},{56,48},{64,72... | collective-permute-start | bytes 786440 | tf_op jit(solution)/shard_map/ppermute | solution.py:244
  26.2 9.7 %collective-permute-start.1 = (f32[256,128]{1,0:T(8,128)S(1)}, f32[256,128]{1,0:T(8,128)S(1)}, u32[]{:S(2)}, u32[]{:S(2)}) collective-permute-start(f32[256,128]{1,0:T(8,128)S(1)} %constant_dynamic-slice_fusion.1), channel_id=1, source_target_pairs={{0,16},{8,24},{16,0},{24,8},{32,48},{40,56},{48,32},{56,40},{64,80... | collective-permute-start | bytes 393224 | tf_op jit(solution)/shard_map/ppermute | solution.py:244
  36.0 8.2 %collective-permute-start.2 = (f32[128,128]{1,0:T(8,128)S(1)}, f32[128,128]{1,0:T(8,128)S(1)}, u32[]{:S(2)}, u32[]{:S(2)}) collective-permute-start(f32[128,128]{1,0:T(8,128)S(1)} %constant_dynamic-slice_fusion), channel_id=1, source_target_pairs={{0,32},{8,40},{16,48},{24,56},{32,0},{40,8},{48,16},{56,24},{64,96... | collective-permute-start | bytes 196616 | tf_op jit(solution)/shard_map/ppermute | solution.py:244
  44.2 6.5 %collective-permute-start.3 = (f32[128,128]{1,0:T(8,128)S(1)}, f32[128,128]{1,0:T(8,128)S(1)}, u32[]{:S(2)}, u32[]{:S(2)}) collective-permute-start(f32[128,128]{1,0:T(8,128)S(1)} %dynamic-slice_add_fusion.2), channel_id=1, source_target_pairs={{0,1},{1,0},{2,3},{3,2},{4,5},{5,4},{6,7},{7,6},{8,9},{9,8},{10,11... | collective-permute-start | bytes 196616 | tf_op jit(solution)/shard_map/ppermute | solution.py:263
  50.8 8.3 %collective-permute-start.4 = (f32[128,128]{1,0:T(8,128)S(1)}, f32[128,128]{1,0:T(8,128)S(1)}, u32[]{:S(2)}, u32[]{:S(2)}) collective-permute-start(f32[128,128]{1,0:T(8,128)S(1)} %add.73), channel_id=1, source_target_pairs={{0,2},{1,3},{2,0},{3,1},{4,6},{5,7},{6,4},{7,5},{8,10},{9,11},{10,... | collective-permute-start | bytes 196616 | tf_op jit(solution)/shard_map/ppermute | solution.py:263
  59.1 11.8 %collective-permute-start.5 = (f32[128,128]{1,0:T(8,128)S(1)}, f32[128,128]{1,0:T(8,128)S(1)}, u32[]{:S(2)}, u32[]{:S(2)}) collective-permute-start(f32[128,128]{1,0:T(8,128)S(1)} %add.74), channel_id=1, source_target_pairs={{0,4},{1,5},{2,6},{3,7},{4,0},{5,1},{6,2},{7,3},{8,12},{9,13},{10,... | collective-permute-start | bytes 196616 | tf_op jit(solution)/shard_map/ppermute | solution.py:263
  71.7 17.6 %all-to-all-start.1 = ((s16[8,144,128]{2,1,0:T(8,128)(2,1)}), s16[8,144,128]{2,1,0:T(8,128)(2,1)S(1)}, u32[]{:S(2)}, u32[]{:S(2)}) async-start(s16[8,144,128]{2,1,0:T(8,128)(2,1)} %spread.1), calls=%async_computation.1 | async-start | bytes 589824 | tf_op jit(solution)/shard_map/all_to_all | solution.py:266
  88.7 32.0 %copy-start = (f32[1024,128]{1,0:T(8,128)S(1)}, f32[1024,128]{1,0:T(8,128)}, u32[]{:S(2)}) copy-start(f32[1024,128]{1,0:T(8,128)} %table_ref.3) | copy-start | bytes 1572868
  88.7 32.0 %copy-start.2 = (f32[1024]{0:T(1024)S(1)}, f32[1024]{0:T(1024)}, u32[]{:S(2)}) copy-start(f32[1024]{0:T(1024)} %param.15) | copy-start | bytes 12292
  89.3 19.6 %all-to-all-start.2 = ((s16[8,144,128]{2,1,0:T(8,128)(2,1)}), s16[8,144,128]{2,1,0:T(8,128)(2,1)S(1)}, u32[]{:S(2)}, u32[]{:S(2)}) async-start(s16[8,144,128]{2,1,0:T(8,128)(2,1)} %cold_sum.1), calls=%async_computation.2 | async-start | bytes 589824 | tf_op jit(solution)/shard_map/all_to_all | solution.py:269
  97.7 30.3 %copy-start.1 = (f32[1024,128]{1,0:T(8,128)S(1)}, f32[1024,128]{1,0:T(8,128)}, u32[]{:S(2)}) copy-start(f32[1024,128]{1,0:T(8,128)} %table_ref.2) | copy-start | bytes 1572868
  97.7 30.3 %copy-start.3 = (f32[1024]{0:T(1024)S(1)}, f32[1024]{0:T(1024)}, u32[]{:S(2)}) copy-start(f32[1024]{0:T(1024)} %param.13) | copy-start | bytes 12292
  97.9 8.1 %collective-permute-start.6 = (f32[128,128]{1,0:T(8,128)S(1)}, f32[128,128]{1,0:T(8,128)S(1)}, u32[]{:S(2)}, u32[]{:S(2)}) collective-permute-start(f32[128,128]{1,0:T(8,128)S(1)} %gathered_total.1), channel_id=1, source_target_pairs={{0,32},{8,40},{16,48},{24,56},{32,0},{40,8},{48,16},{56,24},{64,96... | collective-permute-start | bytes 196616 | tf_op jit(solution)/shard_map/ppermute | solution.py:250
  106.0 11.1 %collective-permute-start.7 = (f32[256,128]{1,0:T(8,128)S(1)}, f32[256,128]{1,0:T(8,128)S(1)}, u32[]{:S(2)}, u32[]{:S(2)}) collective-permute-start(f32[256,128]{1,0:T(8,128)S(1)} %maximum_select_fusion.2), channel_id=1, source_target_pairs={{0,16},{8,24},{16,0},{24,8},{32,48},{40,56},{48,32},{56,40},{64,80... | collective-permute-start | bytes 393224 | tf_op jit(solution)/shard_map/ppermute | solution.py:250
  110.0 18.0 %all-to-all-start.3 = ((s16[8,144,128]{2,1,0:T(8,128)(2,1)}), s16[8,144,128]{2,1,0:T(8,128)(2,1)S(1)}, u32[]{:S(2)}, u32[]{:S(2)}) async-start(s16[8,144,128]{2,1,0:T(8,128)(2,1)} %replica_total.1), calls=%async_computation.3 | async-start | bytes 589824 | tf_op jit(solution)/shard_map/all_to_all | solution.py:272
  117.2 3.4 %collective-permute-start.8 = (f32[512,128]{1,0:T(8,128)S(1)}, f32[512,128]{1,0:T(8,128)S(1)}, u32[]{:S(2)}, u32[]{:S(2)}) collective-permute-start(f32[512,128]{1,0:T(8,128)S(1)} %maximum_select_fusion.1), channel_id=1, source_target_pairs={{0,8},{8,0},{16,24},{24,16},{32,40},{40,32},{48,56},{56,48},{64,72... | collective-permute-start | bytes 786440 | tf_op jit(solution)/shard_map/ppermute | solution.py:250

commit v3 on v2

v3 whole, which is shorter than its diff:
```python
import functools

import jax
import jax.numpy as jnp
from jax import lax
from jax.experimental import pallas as pl
from jax.experimental.pallas import tpu as pltpu
from jax.sharding import PartitionSpec as P

V = 1024
GROUP = 128
HALF = 64
FIELDS = 8
BITS = 4
TILE = 16
PAIRS = 0x33333333

learning_rate = 0.5
epsilon = 1e-06

PARAMS = pltpu.CompilerParams(vmem_limit_bytes=40 << 20)


def decode_ids(code):
    key = jnp.zeros(code.shape, jnp.float32)
    unit = jnp.zeros(code.shape, jnp.int32)
    for field in range(FIELDS):
        reached = code >= float(GROUP * 2**field)
        key = jnp.where(reached, code * 2.0**-field - float(GROUP), key)
        unit = jnp.where(reached, 1 << (BITS * field), unit)
    upper = key >= float(HALF)
    key = jnp.where(upper, key - float(HALF), key)
    return key.astype(jnp.int32), jnp.where(upper, unit * 4, unit)


def packed_counts(key, unit):
    rows = lax.broadcasted_iota(jnp.int32, (HALF, key.shape[1]), 0)
    even = odd = None
    for first in range(0, key.shape[0], 3):
        total = None
        for slot in range(first, min(first + 3, key.shape[0])):
            term = jnp.where(rows == key[slot : slot + 1], unit[slot : slot + 1], 0)
            total = term if total is None else total + term
        low, high = total & PAIRS, lax.shift_right_logical(total, 2) & PAIRS
        even = low if even is None else even + low
        odd = high if odd is None else odd + high
    return even, odd


def unpacked_counts(even, odd):
    groups = []
    for field in range(FIELDS):
        for packed in (even, odd):
            if field == FIELDS - 1:
                part = lax.shift_right_logical(packed, BITS * field)
            else:
                part = packed & (((1 << BITS) - 1) << (BITS * field))
            groups.append(part.astype(jnp.float32).astype(jnp.bfloat16))
    return jnp.concatenate(groups, 0)


def field_scale(field):
    return 2.0 ** (-BITS * field) if field < FIELDS - 1 else 1.0


def block_sum(bags, values):
    total = None
    for bag, rows in zip(bags, values):
        product = jnp.dot(unpacked_counts(*packed_counts(*bag)), rows, preferred_element_type=jnp.float32)
        total = product if total is None else total + product
    return total


def diagonal(rows):
    shape = (rows, GROUP)
    return lax.broadcasted_iota(jnp.int32, shape, 0) == lax.broadcasted_iota(jnp.int32, shape, 1)


def to_row(column):
    return jnp.sum(jnp.where(diagonal(column.shape[0]), column, 0.0), axis=0, keepdims=True)


def to_column(row, rows=GROUP):
    return jnp.sum(jnp.where(diagonal(rows), row, 0.0), axis=1, keepdims=True)


def quantized(x):
    top = jnp.maximum(jnp.max(jnp.abs(x), axis=1, keepdims=True), 1e-30)
    level = jnp.ceil(8.0 * jnp.log2(top) + 0.05)
    return jnp.round(x * jnp.exp2(15.0 - level * 0.125)).astype(jnp.int32).astype(jnp.int16), level


def restored(codes, level):
    return codes.astype(jnp.int32).astype(jnp.float32) * jnp.exp2(level * 0.125 - 15.0)


def level_tile(level):
    return jnp.broadcast_to(to_row(level), (TILE, GROUP)).astype(jnp.int32).astype(jnp.int16)


def tile_level(tile):
    return to_column(tile.astype(jnp.int32).astype(jnp.float32)[0:1])


def prepare_kernel(grad_ref, ids_ref, lengths_ref, out_ref, grads, ids_buf, lengths_buf, outs, in_sems, out_sems):
    parts, block = grads.shape[0], grads.shape[2]
    samples = grads.shape[1]
    small = (
        pltpu.make_async_copy(lengths_ref, lengths_buf, in_sems.at[parts]),
        pltpu.make_async_copy(ids_ref, ids_buf, in_sems.at[parts + 1]),
    )
    large = [
        pltpu.make_async_copy(grad_ref.at[:, pl.ds(part * block, block), :], grads.at[part], in_sems.at[part])
        for part in range(parts)
    ]
    for copy in small:
        copy.start()
    for copy in large:
        copy.start()
    for copy in small:
        copy.wait()
    ids = ids_buf[...]
    position = lax.broadcasted_iota(jnp.int32, ids.shape, 1)
    code = jnp.where(position < lengths_buf[...][:, None, :], (GROUP + (ids & (GROUP - 1))) << (ids >> 7), 0)
    outs[:, samples:, :] = code.astype(jnp.float32).astype(jnp.bfloat16)
    back = []
    for part in range(parts):
        rows = pl.ds(part * block, block)
        large[part].wait()
        outs[rows, 0:samples, :] = jnp.swapaxes(grads[part], 0, 1)
        back.append(pltpu.make_async_copy(outs.at[rows], out_ref.at[rows], out_sems.at[part]))
        back[part].start()
    for copy in back:
        copy.wait()


def prepare(grad, ids, lengths, parts=4):
    samples, features, width = grad.shape
    slots = ids.shape[1]
    shape = (features, samples + slots, width)
    return pl.pallas_call(
        prepare_kernel,
        in_specs=[pl.BlockSpec(memory_space=pl.ANY)] * 3,
        out_specs=pl.BlockSpec(memory_space=pl.ANY),
        out_shape=jax.ShapeDtypeStruct(shape, jnp.bfloat16),
        scratch_shapes=[
            pltpu.VMEM((parts, samples, features // parts, width), jnp.bfloat16),
            pltpu.VMEM(ids.shape, jnp.int32),
            pltpu.VMEM(lengths.shape, jnp.int32),
            pltpu.VMEM(shape, jnp.bfloat16),
            pltpu.SemaphoreType.DMA((parts + 2,)),
            pltpu.SemaphoreType.DMA((parts,)),
        ],
        compiler_params=pltpu.CompilerParams(vmem_limit_bytes=60 << 20),
        cost_estimate=pl.CostEstimate(flops=0, bytes_accessed=5 << 20, transcendentals=0),
        name="prepare",
    )(grad, ids, lengths)


def hot_kernel(x_ref, ids_ref, out_ref, *, blocks):
    step = pl.program_id(0)

    @pl.when(step == 0)
    def _():
        out_ref[...] = jnp.zeros_like(out_ref)

    bags, values = [], []
    for block in range(blocks):
        ids = ids_ref[block]
        shift = lax.shift_right_logical(ids, 6) * 2
        bags.append((ids & (HALF - 1), lax.shift_left(jnp.ones_like(ids), shift)))
        values.append(x_ref[block, 0:GROUP, :])
    out_ref[...] += block_sum(bags, values)

    @pl.when(step == pl.num_programs(0) - 1)
    def _():
        for field in range(1, FIELDS - 1):
            out_ref[field * GROUP : (field + 1) * GROUP, :] *= field_scale(field)


def hot_sum(rows, ids, blocks=16):
    count, height, width = rows.shape
    return pl.pallas_call(
        functools.partial(hot_kernel, blocks=blocks),
        grid=(count // blocks,),
        in_specs=[
            pl.BlockSpec((blocks, height, width), lambda i: (i, 0, 0)),
            pl.BlockSpec((blocks, ids.shape[1], GROUP), lambda i: (i, 0, 0)),
        ],
        out_specs=pl.BlockSpec((V, width), lambda i: (0, 0)),
        out_shape=jax.ShapeDtypeStruct((V, width), jnp.float32),
        compiler_params=PARAMS,
        cost_estimate=pl.CostEstimate(flops=2 * V * count * GROUP * width, bytes_accessed=3 << 20, transcendentals=0),
        name="hot_sum",
    )(rows, ids)


def cold_kernel(x_ref, out_ref, rows_ref, total_ref, sems, *, blocks):
    parts = x_ref.shape[0] // blocks

    def copy(part):
        at = pl.ds(part * blocks, blocks)
        return pltpu.make_async_copy(x_ref.at[at], rows_ref.at[at], sems.at[part])

    for part in range(parts):
        copy(part).start()
    total_ref[...] = jnp.zeros_like(total_ref)

    def add(part, carry):
        copy(part).wait()
        bags, values = [], []
        for block in range(blocks):
            at = part * blocks + block
            bags.append(decode_ids(rows_ref[at, GROUP : GROUP + 8, :].astype(jnp.float32)))
            values.append(rows_ref[at, 0:GROUP, :])
        total_ref[...] += block_sum(bags, values)
        return carry

    lax.fori_loop(0, parts, add, 0)
    for field in range(FIELDS):
        rows = total_ref[field * GROUP : (field + 1) * GROUP, :] * field_scale(field)
        codes, level = quantized(rows)
        out_ref[field, 0:GROUP, :] = codes
        out_ref[field, GROUP:, :] = level_tile(level)


def cold_sum(rows, blocks=16):
    count, height, width = rows.shape
    return pl.pallas_call(
        functools.partial(cold_kernel, blocks=blocks),
        in_specs=[pl.BlockSpec(memory_space=pl.ANY)],
        out_specs=pl.BlockSpec(memory_space=pltpu.VMEM),
        out_shape=jax.ShapeDtypeStruct((FIELDS, GROUP + TILE, width), jnp.int16),
        scratch_shapes=[
            pltpu.VMEM(rows.shape, rows.dtype),
            pltpu.VMEM((V, width), jnp.float32),
            pltpu.SemaphoreType.DMA((count // blocks,)),
        ],
        compiler_params=PARAMS,
        cost_estimate=pl.CostEstimate(flops=10 * V * count * GROUP * width, bytes_accessed=3 << 20, transcendentals=0),
        name="cold_sum",
    )(rows)


def whole(body, out_shape, name, *operands):
    return pl.pallas_call(body, out_shape=out_shape, compiler_params=PARAMS, name=name)(*operands)


def stored_everywhere(rows, out_ref):
    codes, level = quantized(rows)
    tile = level_tile(level)
    for peer in range(FIELDS):
        out_ref[peer, 0:GROUP, :] = codes
        out_ref[peer, GROUP:, :] = tile


def peer_sum(pieces_ref):
    total = None
    for peer in range(FIELDS):
        piece = restored(pieces_ref[peer, 0:GROUP, :], tile_level(pieces_ref[peer, GROUP:, :]))
        total = piece if total is None else total + piece
    return total


def spread(rows_ref, out_ref):
    stored_everywhere(rows_ref[...], out_ref)


def line_total(pieces_ref, out_ref):
    codes, level = quantized(peer_sum(pieces_ref))
    out_ref[0:GROUP, :] = codes
    out_ref[GROUP:, :] = level_tile(level)


def replica_total(pieces_ref, out_ref):
    stored_everywhere(peer_sum(pieces_ref), out_ref)


def update_group(group, grad, table_ref, accum_ref, new_table_ref, new_accum_ref):
    rows = slice(group * GROUP, (group + 1) * GROUP)
    fresh = to_column(accum_ref[group : group + 1, :]) + jnp.sum(grad * grad, axis=1, keepdims=True) * (1.0 / GROUP)
    new_table_ref[rows, :] = table_ref[rows, :] - grad * (learning_rate / (jnp.sqrt(fresh) + epsilon))
    new_accum_ref[group : group + 1, :] = to_row(fresh)


def update(codes_ref, table_ref, accum_ref, new_table_ref, new_accum_ref):
    for group in range(FIELDS):
        grad = restored(codes_ref[group, 0:GROUP, :], tile_level(codes_ref[group, GROUP:, :]))
        update_group(group, grad, table_ref, accum_ref, new_table_ref, new_accum_ref)


def updated(name, codes, table, accum):
    shapes = (
        jax.ShapeDtypeStruct(table.shape, jnp.float32),
        jax.ShapeDtypeStruct((FIELDS, GROUP), jnp.float32),
    )
    new_table, new_accum = whole(update, shapes, name, codes, table, accum.reshape(FIELDS, GROUP))
    return new_table, new_accum.reshape(V)


def halve(rows, axis, mask, mine):
    half = rows.shape[0] // 2
    pairs = [(i, i ^ mask) for i in range(lax.axis_size(axis))]
    got = lax.ppermute(lax.dynamic_slice_in_dim(rows, (1 - mine) * half, half), axis, pairs)
    return lax.dynamic_slice_in_dim(rows, mine * half, half) + got


def double(rows, axis, mask, mine):
    got = lax.ppermute(rows, axis, [(i, i ^ mask) for i in range(lax.axis_size(axis))])
    return jnp.where(mine == 0, jnp.concatenate([rows, got], 0), jnp.concatenate([got, rows], 0))


def per_device(pooled_grad, cold_ids, lengths, hot_ids, table, accum, hot_table, hot_accum):
    lines = [[y * 8 + inner for y in range(8)] for inner in range(8)]
    coded = jax.ShapeDtypeStruct((FIELDS, GROUP + TILE, GROUP), jnp.int16)
    rows = prepare(pooled_grad, jnp.transpose(cold_ids, (1, 2, 0)), jnp.transpose(lengths, (1, 0)))
    moved = lax.all_to_all(rows, "shard", split_axis=0, concat_axis=0, tiled=True)
    hot = hot_sum(rows, jnp.transpose(hot_ids, (1, 2, 0)))
    me = lax.axis_index("shard")
    core, low, high = me & 1, (me >> 1) & 1, (me >> 2) & 1
    rounds = ((1, core), (6, high), (2, low ^ high))
    for mask, mine in rounds:
        hot = halve(hot, "shard", mask, mine)
    for bit in (1, 2, 4):
        hot = hot + lax.ppermute(hot, "rep", [(i, i ^ bit) for i in range(FIELDS)])
    hot = whole(spread, coded, "spread", hot)
    moved, hot = lax.optimization_barrier((moved, hot))
    hot = lax.all_to_all(hot, "shard", split_axis=0, concat_axis=0, axis_index_groups=lines, tiled=True)
    pieces = cold_sum(moved)
    pieces, hot = lax.optimization_barrier((pieces, hot))
    shared = lax.all_to_all(pieces, "rep", split_axis=0, concat_axis=0, tiled=True)
    hot = whole(line_total, jax.ShapeDtypeStruct(coded.shape[1:], jnp.int16), "line_total", hot)
    payload = whole(replica_total, coded, "replica_total", shared)
    hot = double(hot, "shard", *rounds[2])
    payload, hot = lax.optimization_barrier((payload, hot))
    codes = lax.all_to_all(payload, "rep", split_axis=0, concat_axis=0, tiled=True)
    for mask, mine in rounds[1::-1]:
        hot = double(hot, "shard", mask, mine)
    new_hot_table, new_hot_accum = updated("hot_update", hot.reshape(coded.shape), hot_table, hot_accum)
    new_table, new_accum = updated("cold_update", codes, table, accum)
    return (new_table, new_accum, new_hot_table, new_hot_accum)


def solution(mesh):
    in_specs = (
        P(("shard", "rep"), None, None),
        P(("shard", "rep"), None, None),
        P(("shard", "rep"), None),
        P(("shard", "rep"), None, None),
        P("shard", None),
        P("shard"),
        P(),
        P(),
    )
    out_specs = (P("shard", None), P("shard"), P(), P())
    return jax.shard_map(
        per_device, mesh=mesh, in_specs=in_specs, out_specs=out_specs, check_vma=False
    )
```

time: 131 us -> 127 us (0.969)
  starting transfers between devices: 69.7 us -> 64 us
  waiting for transfers between devices: 32.3 us -> 37.5 us
  local copies, waits for them, and re-layouts: 3.08 us -> 0.1 us
  other arithmetic: 1.82 us -> 0.23 us
    all_to_all x1, waiting for transfers between devices: 0.01 us -> 4.63 us  [per_device(): lax.all_to_all(pieces, 'rep', split_axis=0, concat_axis=0, tiled=True)]
    all_to_all x1, starting transfers between devices: 7.19 us -> 3.43 us  [per_device(): lax.all_to_all(payload, 'rep', split_axis=0, concat_axis=0, tiled=True)]
    unnamed x15 -> x12, local copies, waits for them, and re-layouts: 3.02 us -> 0.04 us
    concatenate x1 -> x0, other arithmetic: 1.59 us -> none  [per_device(): jnp.concatenate([jnp.transpose(pooled_grad, (1, 0, 2)), encode_ids(cold_i...]
    all_to_all x1, waiting for transfers between devices: 6.1 us -> 4.53 us  [per_device(): lax.all_to_all(payload, 'rep', split_axis=0, concat_axis=0, tiled=True)]
    ppermute x3, starting transfers between devices: 9.25 us -> 7.84 us  [halve(): lax.ppermute(lax.dynamic_slice_in_dim(rows, (1 - mine) * half, half), axi...]
    pallas_call x2 -> x3, Pallas kernels: 16.8 us -> 17.1 us  [the longest x1 9.2 us: cold_sum(): pl.pallas_call(functools.partial(cold_kernel, blocks=blocks), in_specs=[p...]
  transfers between devices with their start and end apart: 13 -> 13, of which waited for: 10 -> 13; matrix products, arithmetic and copies ran while one was open for 0% -> 0% of each run, Pallas kernels for 15% -> 14%
where the time goes in v3:
time: 127 us; the launch traced here: 125 us
  starting transfers between devices  64 us (50%)
  waiting for transfers between devices  37.5 us (30%)
  Pallas kernels  22.6 us (18%)
    ppermute x3, starting transfers between devices, per_device(): hot = hot + lax.ppermute(hot, 'rep', [(i, i ^ bit) for i in range(FIELDS)])  19.6 us
    ppermute x3, waiting for transfers between devices, halve(): lax.ppermute(lax.dynamic_slice_in_dim(rows, (1 - mine) * half, half), axi...  13.3 us
    all_to_all x1, starting transfers between devices, per_device(): lax.all_to_all(rows, 'shard', split_axis=0, concat_axis=0, tiled=True)  11 us
    pallas_call x1, Pallas kernels, cold_sum(): pl.pallas_call(functools.partial(cold_kernel, blocks=blocks), in_specs=[p...  9.2 us
    all_to_all x1, starting transfers between devices, per_device(): lax.all_to_all(pieces, 'rep', split_axis=0, concat_axis=0, tiled=True)  8.49 us
    ppermute x3, starting transfers between devices, halve(): lax.ppermute(lax.dynamic_slice_in_dim(rows, (1 - mine) * half, half), axi...  7.84 us
    ppermute x3, waiting for transfers between devices, per_device(): hot = hot + lax.ppermute(hot, 'rep', [(i, i ^ bit) for i in range(FIELDS)])  6.96 us
    all_to_all x1, starting transfers between devices, per_device(): lax.all_to_all(hot, 'shard', split_axis=0, concat_axis=0, axis_index_grou...  6.93 us
  transfers between devices with their start and end apart: 13, of which 13 were waited for; matrix products, arithmetic and copies ran while one was open for 0% of the time, Pallas kernels for 14%

profile of v3, /device:TPU:6, one launch (start us, length us, event | category | flops | bytes accessed | tf_op | source)
XLA Modules:
  0.0 125.4 jit_solution(15199127189880691269)
XLA Ops:
  0.6 2.8 %prepare.1.x_ref = bf16[64,136,128]{2,1,0:T(8,128)(2,1)} custom-call(bf16[128,64,128]{2,1,0:T(8,128)(2,1)} %grad_ref.1, s32[64,8,128]{2,1,0:T(8,128)} %bitcast.12, s32[64,128]{1,0:T(8,128)} %bitcast.13), custom_call_target="tpu_custom_call" | custom-call | bytes 5242880 | tf_op jit(solution)/shard_map/prepare/pallas_call | solution.py:141
  3.4 11.0 %all-to-all-start = ((bf16[64,136,128]{2,1,0:T(8,128)(2,1)}), bf16[64,136,128]{2,1,0:T(8,128)(2,1)}, u32[]{:S(2)}, u32[]{:S(2)}) async-start(bf16[64,136,128]{2,1,0:T(8,128)(2,1)} %prepare.1.x_ref), calls=%async_computation | async-start | bytes 4456448 | tf_op jit(solution)/shard_map/all_to_all | solution.py:317
  14.4 5.1 %hot_sum.1 = f32[1024,128]{1,0:T(8,128)S(1)} custom-call(bf16[64,136,128]{2,1,0:T(8,128)(2,1)S(1)} %copy-done, s32[64,2,128]{2,1,0:T(2,128)S(1)} %bitcast.11), custom_call_target="tpu_custom_call" | custom-call | flops 2147483648 | bytes 3145728 | tf_op jit(solution)/shard_map/hot_sum/pallas_call | solution.py:183
  19.6 2.1 %collective-permute-start = (f32[512,128]{1,0:T(8,128)S(1)}, f32[512,128]{1,0:T(8,128)S(1)}, u32[]{:S(2)}, u32[]{:S(2)}) collective-permute-start(f32[512,128]{1,0:T(8,128)S(1)} %constant_dynamic-slice_fusion.2), channel_id=1, source_target_pairs={{0,8},{8,0},{16,24},{24,16},{32,40},{40,32},{48,56},{56,48},{64,72... | collective-permute-start | bytes 786440 | tf_op jit(solution)/shard_map/ppermute | solution.py:304
  21.6 1.4 %collective-permute-done = f32[512,128]{1,0:T(8,128)S(1)} collective-permute-done((f32[512,128]{1,0:T(8,128)S(1)}, f32[512,128]{1,0:T(8,128)S(1)}, u32[]{:S(2)}, u32[]{:S(2)}) %collective-permute-start) | collective-permute-done | bytes 262176 | tf_op jit(solution)/shard_map/ppermute | solution.py:304
  23.0 2.5 %collective-permute-start.1 = (f32[256,128]{1,0:T(8,128)S(1)}, f32[256,128]{1,0:T(8,128)S(1)}, u32[]{:S(2)}, u32[]{:S(2)}) collective-permute-start(f32[256,128]{1,0:T(8,128)S(1)} %constant_dynamic-slice_fusion.1), channel_id=1, source_target_pairs={{0,48},{8,56},{16,32},{24,40},{32,16},{40,24},{48,0},{56,8},{64,11... | collective-permute-start | bytes 393224 | tf_op jit(solution)/shard_map/ppermute | solution.py:304
  25.6 7.8 %collective-permute-done.1 = f32[256,128]{1,0:T(8,128)S(1)} collective-permute-done((f32[256,128]{1,0:T(8,128)S(1)}, f32[256,128]{1,0:T(8,128)S(1)}, u32[]{:S(2)}, u32[]{:S(2)}) %collective-permute-start.1) | collective-permute-done | bytes 131104 | tf_op jit(solution)/shard_map/ppermute | solution.py:304
  33.4 3.3 %collective-permute-start.2 = (f32[128,128]{1,0:T(8,128)S(1)}, f32[128,128]{1,0:T(8,128)S(1)}, u32[]{:S(2)}, u32[]{:S(2)}) collective-permute-start(f32[128,128]{1,0:T(8,128)S(1)} %constant_dynamic-slice_fusion), channel_id=1, source_target_pairs={{0,16},{8,24},{16,0},{24,8},{32,48},{40,56},{48,32},{56,40},{64,80... | collective-permute-start | bytes 196616 | tf_op jit(solution)/shard_map/ppermute | solution.py:304
  36.7 4.1 %collective-permute-done.2 = f32[128,128]{1,0:T(8,128)S(1)} collective-permute-done((f32[128,128]{1,0:T(8,128)S(1)}, f32[128,128]{1,0:T(8,128)S(1)}, u32[]{:S(2)}, u32[]{:S(2)}) %collective-permute-start.2) | collective-permute-done | bytes 65568 | tf_op jit(solution)/shard_map/ppermute | solution.py:304
  40.9 4.2 %collective-permute-start.3 = (f32[128,128]{1,0:T(8,128)S(1)}, f32[128,128]{1,0:T(8,128)S(1)}, u32[]{:S(2)}, u32[]{:S(2)}) collective-permute-start(f32[128,128]{1,0:T(8,128)S(1)} %dynamic-slice_add_fusion.2), channel_id=1, source_target_pairs={{0,1},{1,0},{2,3},{3,2},{4,5},{5,4},{6,7},{7,6},{8,9},{9,8},{10,11... | collective-permute-start | bytes 196616 | tf_op jit(solution)/shard_map/ppermute | solution.py:325
  45.1 2.2 %collective-permute-done.3 = f32[128,128]{1,0:T(8,128)S(1)} collective-permute-done((f32[128,128]{1,0:T(8,128)S(1)}, f32[128,128]{1,0:T(8,128)S(1)}, u32[]{:S(2)}, u32[]{:S(2)}) %collective-permute-start.3) | collective-permute-done | bytes 65568 | tf_op jit(solution)/shard_map/ppermute | solution.py:325
  47.3 6.1 %collective-permute-start.4 = (f32[128,128]{1,0:T(8,128)S(1)}, f32[128,128]{1,0:T(8,128)S(1)}, u32[]{:S(2)}, u32[]{:S(2)}) collective-permute-start(f32[128,128]{1,0:T(8,128)S(1)} %add.45), channel_id=1, source_target_pairs={{0,2},{1,3},{2,0},{3,1},{4,6},{5,7},{6,4},{7,5},{8,10},{9,11},{10,... | collective-permute-start | bytes 196616 | tf_op jit(solution)/shard_map/ppermute | solution.py:325
  53.4 2.2 %collective-permute-done.4 = f32[128,128]{1,0:T(8,128)S(1)} collective-permute-done((f32[128,128]{1,0:T(8,128)S(1)}, f32[128,128]{1,0:T(8,128)S(1)}, u32[]{:S(2)}, u32[]{:S(2)}) %collective-permute-start.4) | collective-permute-done | bytes 65568 | tf_op jit(solution)/shard_map/ppermute | solution.py:325
  55.7 9.3 %collective-permute-start.5 = (f32[128,128]{1,0:T(8,128)S(1)}, f32[128,128]{1,0:T(8,128)S(1)}, u32[]{:S(2)}, u32[]{:S(2)}) collective-permute-start(f32[128,128]{1,0:T(8,128)S(1)} %add.46), channel_id=1, source_target_pairs={{0,4},{1,5},{2,6},{3,7},{4,0},{5,1},{6,2},{7,3},{8,12},{9,13},{10,... | collective-permute-start | bytes 196616 | tf_op jit(solution)/shard_map/ppermute | solution.py:325
  65.0 2.5 %collective-permute-done.5 = f32[128,128]{1,0:T(8,128)S(1)} collective-permute-done((f32[128,128]{1,0:T(8,128)S(1)}, f32[128,128]{1,0:T(8,128)S(1)}, u32[]{:S(2)}, u32[]{:S(2)}) %collective-permute-start.5) | collective-permute-done | bytes 65568 | tf_op jit(solution)/shard_map/ppermute | solution.py:325
  67.5 0.8 spread.1
  68.5 6.9 %all-to-all-start.1 = ((s16[8,144,128]{2,1,0:T(8,128)(2,1)}), s16[8,144,128]{2,1,0:T(8,128)(2,1)S(1)}, u32[]{:S(2)}, u32[]{:S(2)}) async-start(s16[8,144,128]{2,1,0:T(8,128)(2,1)} %spread.1), calls=%async_computation.1 | async-start | bytes 589824 | tf_op jit(solution)/shard_map/all_to_all | solution.py:328
  75.4 9.2 %cold_sum.1 = s16[8,144,128]{2,1,0:T(8,128)(2,1)} custom-call(bf16[64,136,128]{2,1,0:T(8,128)(2,1)} %all-to-all-done.x_ref), custom_call_target="tpu_custom_call" | custom-call | flops 10737418240 | bytes 3145728 | tf_op jit(solution)/shard_map/cold_sum/pallas_call | solution.py:229
  84.7 1.6 %all-to-all-done.1.pieces_ref = s16[8,144,128]{2,1,0:T(8,128)(2,1)S(1)} async-done(((s16[8,144,128]{2,1,0:T(8,128)(2,1)}), s16[8,144,128]{2,1,0:T(8,128)(2,1)S(1)}, u32[]{:S(2)}, u32[]{:S(2)}) %all-to-all-start.1) | async-done | bytes 294944 | tf_op jit(solution)/shard_map/all_to_all | solution.py:328
  86.3 8.5 %all-to-all-start.2 = ((s16[8,144,128]{2,1,0:T(8,128)(2,1)}), s16[8,144,128]{2,1,0:T(8,128)(2,1)S(1)}, u32[]{:S(2)}, u32[]{:S(2)}) async-start(s16[8,144,128]{2,1,0:T(8,128)(2,1)} %cold_sum.1), calls=%async_computation.2 | async-start | bytes 589824 | tf_op jit(solution)/shard_map/all_to_all | solution.py:331
  95.1 2.0 %collective-permute-start.6 = (s16[144,128]{1,0:T(8,128)(2,1)S(1)}, s16[144,128]{1,0:T(8,128)(2,1)S(1)}, u32[]{:S(2)}, u32[]{:S(2)}) collective-permute-start(s16[144,128]{1,0:T(8,128)(2,1)S(1)} %line_total.1), channel_id=1, source_target_pairs={{0,16},{8,24},{16,0},{24,8},{32,48},{40,56},{48,32},{56,40},{64,80... | collective-permute-start | bytes 110600 | tf_op jit(solution)/shard_map/ppermute | solution.py:309
  97.1 3.8 %collective-permute-done.6 = s16[144,128]{1,0:T(8,128)(2,1)S(1)} collective-permute-done((s16[144,128]{1,0:T(8,128)(2,1)S(1)}, s16[144,128]{1,0:T(8,128)(2,1)S(1)}, u32[]{:S(2)}, u32[]{:S(2)}) %collective-permute-start.6) | collective-permute-done | bytes 36896 | tf_op jit(solution)/shard_map/ppermute | solution.py:309
  101.0 4.6 %all-to-all-done.2.pieces_ref = s16[8,144,128]{2,1,0:T(8,128)(2,1)S(1)} async-done(((s16[8,144,128]{2,1,0:T(8,128)(2,1)}), s16[8,144,128]{2,1,0:T(8,128)(2,1)S(1)}, u32[]{:S(2)}, u32[]{:S(2)}) %all-to-all-start.2) | async-done | bytes 294944 | tf_op jit(solution)/shard_map/all_to_all | solution.py:331
  105.6 1.0 replica_total.1
  106.6 2.9 %collective-permute-start.7 = (s16[288,128]{1,0:T(8,128)(2,1)S(1)}, s16[288,128]{1,0:T(8,128)(2,1)S(1)}, u32[]{:S(2)}, u32[]{:S(2)}) collective-permute-start(s16[288,128]{1,0:T(8,128)(2,1)S(1)} %add_select_fusion.2), channel_id=1, source_target_pairs={{0,48},{8,56},{16,32},{24,40},{32,16},{40,24},{48,0},{56,8},{64,11... | collective-permute-start | bytes 221192 | tf_op jit(solution)/shard_map/ppermute | solution.py:309
  109.5 3.4 %all-to-all-start.3 = ((s16[8,144,128]{2,1,0:T(8,128)(2,1)}), s16[8,144,128]{2,1,0:T(8,128)(2,1)S(1)}, u32[]{:S(2)}, u32[]{:S(2)}) async-start(s16[8,144,128]{2,1,0:T(8,128)(2,1)} %replica_total.1), calls=%async_computation.3 | async-start | bytes 589824 | tf_op jit(solution)/shard_map/all_to_all | solution.py:336
  113.0 1.1 collective-permute-done.7
  114.1 1.9 %collective-permute-start.8 = (s16[576,128]{1,0:T(8,128)(2,1)S(1)}, s16[576,128]{1,0:T(8,128)(2,1)S(1)}, u32[]{:S(2)}, u32[]{:S(2)}) collective-permute-start(s16[576,128]{1,0:T(8,128)(2,1)S(1)} %add_select_fusion.1), channel_id=1, source_target_pairs={{0,8},{8,0},{16,24},{24,16},{32,40},{40,32},{48,56},{56,48},{64,72... | collective-permute-start | bytes 442376 | tf_op jit(solution)/shard_map/ppermute | solution.py:309
  116.1 1.3 %collective-permute-done.8 = s16[576,128]{1,0:T(8,128)(2,1)S(1)} collective-permute-done((s16[576,128]{1,0:T(8,128)(2,1)S(1)}, s16[576,128]{1,0:T(8,128)(2,1)S(1)}, u32[]{:S(2)}, u32[]{:S(2)}) %collective-permute-start.8) | collective-permute-done | bytes 147488 | tf_op jit(solution)/shard_map/ppermute | solution.py:309
  117.5 1.7 %hot_update.1 = (f32[1024,128]{1,0:T(8,128)}, f32[8,128]{1,0:T(8,128)}) custom-call(s16[8,144,128]{2,1,0:T(8,128)(2,1)S(1)} %bitcast.8, f32[1024,128]{1,0:T(8,128)S(1)} %copy-done.1, f32[8,128]{1,0:T(8,128)S(1)} %bitcast.9), custom_call_target="tpu_custom_call" | custom-call | tf_op jit(solution)/shard_map/hot_update/pallas_call | solution.py:246
  119.2 4.5 %all-to-all-done.3.codes_ref = s16[8,144,128]{2,1,0:T(8,128)(2,1)S(1)} async-done(((s16[8,144,128]{2,1,0:T(8,128)(2,1)}), s16[8,144,128]{2,1,0:T(8,128)(2,1)S(1)}, u32[]{:S(2)}, u32[]{:S(2)}) %all-to-all-start.3) | async-done | bytes 294944 | tf_op jit(solution)/shard_map/all_to_all | solution.py:336
  123.7 1.7 %cold_update.1 = (f32[1024,128]{1,0:T(8,128)}, f32[8,128]{1,0:T(8,128)}) custom-call(s16[8,144,128]{2,1,0:T(8,128)(2,1)S(1)} %all-to-all-done.3.codes_ref, f32[1024,128]{1,0:T(8,128)S(1)} %copy-done.2, f32[8,128]{1,0:T(8,128)S(1)} %bitcast.10), custom_call_target="tpu_custom_call" | custom-call | tf_op jit(solution)/shard_map/cold_update/pallas_call | solution.py:246
  (26 shorter events, 0.8 us)
Async XLA Ops:
  3.4 11.0 %copy-start = (bf16[64,136,128]{2,1,0:T(8,128)(2,1)S(1)}, bf16[64,136,128]{2,1,0:T(8,128)(2,1)}, u32[]{:S(2)}) copy-start(bf16[64,136,128]{2,1,0:T(8,128)(2,1)} %prepare.1.x_ref) | copy-start | bytes 6684676
  3.4 11.0 %copy-start.5 = (s32[128,64,2]{0,2,1:T(2,128)S(1)}, s32[128,64,2]{0,2,1:T(2,128)}, u32[]{:S(2)}) copy-start(s32[128,64,2]{0,2,1:T(2,128)} %param.11) | copy-start | bytes 196612
  3.4 65.1 %all-to-all-start = ((bf16[64,136,128]{2,1,0:T(8,128)(2,1)}), bf16[64,136,128]{2,1,0:T(8,128)(2,1)}, u32[]{:S(2)}, u32[]{:S(2)}) async-start(bf16[64,136,128]{2,1,0:T(8,128)(2,1)} %prepare.1.x_ref), calls=%async_computation | async-start | bytes 4456448 | tf_op jit(solution)/shard_map/all_to_all | solution.py:317
  19.6 3.4 %collective-permute-start = (f32[512,128]{1,0:T(8,128)S(1)}, f32[512,128]{1,0:T(8,128)S(1)}, u32[]{:S(2)}, u32[]{:S(2)}) collective-permute-start(f32[512,128]{1,0:T(8,128)S(1)} %constant_dynamic-slice_fusion.2), channel_id=1, source_target_pairs={{0,8},{8,0},{16,24},{24,16},{32,40},{40,32},{48,56},{56,48},{64,72... | collective-permute-start | bytes 786440 | tf_op jit(solution)/shard_map/ppermute | solution.py:304
  23.0 10.4 %collective-permute-start.1 = (f32[256,128]{1,0:T(8,128)S(1)}, f32[256,128]{1,0:T(8,128)S(1)}, u32[]{:S(2)}, u32[]{:S(2)}) collective-permute-start(f32[256,128]{1,0:T(8,128)S(1)} %constant_dynamic-slice_fusion.1), channel_id=1, source_target_pairs={{0,48},{8,56},{16,32},{24,40},{32,16},{40,24},{48,0},{56,8},{64,11... | collective-permute-start | bytes 393224 | tf_op jit(solution)/shard_map/ppermute | solution.py:304
  33.4 7.4 %collective-permute-start.2 = (f32[128,128]{1,0:T(8,128)S(1)}, f32[128,128]{1,0:T(8,128)S(1)}, u32[]{:S(2)}, u32[]{:S(2)}) collective-permute-start(f32[128,128]{1,0:T(8,128)S(1)} %constant_dynamic-slice_fusion), channel_id=1, source_target_pairs={{0,16},{8,24},{16,0},{24,8},{32,48},{40,56},{48,32},{56,40},{64,80... | collective-permute-start | bytes 196616 | tf_op jit(solution)/shard_map/ppermute | solution.py:304
  40.9 6.5 %collective-permute-start.3 = (f32[128,128]{1,0:T(8,128)S(1)}, f32[128,128]{1,0:T(8,128)S(1)}, u32[]{:S(2)}, u32[]{:S(2)}) collective-permute-start(f32[128,128]{1,0:T(8,128)S(1)} %dynamic-slice_add_fusion.2), channel_id=1, source_target_pairs={{0,1},{1,0},{2,3},{3,2},{4,5},{5,4},{6,7},{7,6},{8,9},{9,8},{10,11... | collective-permute-start | bytes 196616 | tf_op jit(solution)/shard_map/ppermute | solution.py:325
  47.3 8.3 %collective-permute-start.4 = (f32[128,128]{1,0:T(8,128)S(1)}, f32[128,128]{1,0:T(8,128)S(1)}, u32[]{:S(2)}, u32[]{:S(2)}) collective-permute-start(f32[128,128]{1,0:T(8,128)S(1)} %add.45), channel_id=1, source_target_pairs={{0,2},{1,3},{2,0},{3,1},{4,6},{5,7},{6,4},{7,5},{8,10},{9,11},{10,... | collective-permute-start | bytes 196616 | tf_op jit(solution)/shard_map/ppermute | solution.py:325
  55.7 11.8 %collective-permute-start.5 = (f32[128,128]{1,0:T(8,128)S(1)}, f32[128,128]{1,0:T(8,128)S(1)}, u32[]{:S(2)}, u32[]{:S(2)}) collective-permute-start(f32[128,128]{1,0:T(8,128)S(1)} %add.46), channel_id=1, source_target_pairs={{0,4},{1,5},{2,6},{3,7},{4,0},{5,1},{6,2},{7,3},{8,12},{9,13},{10,... | collective-permute-start | bytes 196616 | tf_op jit(solution)/shard_map/ppermute | solution.py:325
  68.5 17.8 %all-to-all-start.1 = ((s16[8,144,128]{2,1,0:T(8,128)(2,1)}), s16[8,144,128]{2,1,0:T(8,128)(2,1)S(1)}, u32[]{:S(2)}, u32[]{:S(2)}) async-start(s16[8,144,128]{2,1,0:T(8,128)(2,1)} %spread.1), calls=%async_computation.1 | async-start | bytes 589824 | tf_op jit(solution)/shard_map/all_to_all | solution.py:328
  84.6 32.9 %copy-start.1 = (f32[1024,128]{1,0:T(8,128)S(1)}, f32[1024,128]{1,0:T(8,128)}, u32[]{:S(2)}) copy-start(f32[1024,128]{1,0:T(8,128)} %table_ref.3) | copy-start | bytes 1572868
  84.7 32.8 %copy-start.3 = (f32[1024]{0:T(1024)S(1)}, f32[1024]{0:T(1024)}, u32[]{:S(2)}) copy-start(f32[1024]{0:T(1024)} %param.15) | copy-start | bytes 12292
  84.7 39.0 %copy-start.2 = (f32[1024,128]{1,0:T(8,128)S(1)}, f32[1024,128]{1,0:T(8,128)}, u32[]{:S(2)}) copy-start(f32[1024,128]{1,0:T(8,128)} %table_ref.2) | copy-start | bytes 1572868
  84.7 39.0 %copy-start.4 = (f32[1024]{0:T(1024)S(1)}, f32[1024]{0:T(1024)}, u32[]{:S(2)}) copy-start(f32[1024]{0:T(1024)} %param.13) | copy-start | bytes 12292
  86.3 19.3 %all-to-all-start.2 = ((s16[8,144,128]{2,1,0:T(8,128)(2,1)}), s16[8,144,128]{2,1,0:T(8,128)(2,1)S(1)}, u32[]{:S(2)}, u32[]{:S(2)}) async-start(s16[8,144,128]{2,1,0:T(8,128)(2,1)} %cold_sum.1), calls=%async_computation.2 | async-start | bytes 589824 | tf_op jit(solution)/shard_map/all_to_all | solution.py:331
  95.1 5.9 %collective-permute-start.6 = (s16[144,128]{1,0:T(8,128)(2,1)S(1)}, s16[144,128]{1,0:T(8,128)(2,1)S(1)}, u32[]{:S(2)}, u32[]{:S(2)}) collective-permute-start(s16[144,128]{1,0:T(8,128)(2,1)S(1)} %line_total.1), channel_id=1, source_target_pairs={{0,16},{8,24},{16,0},{24,8},{32,48},{40,56},{48,32},{56,40},{64,80... | collective-permute-start | bytes 110600 | tf_op jit(solution)/shard_map/ppermute | solution.py:309
  106.6 7.4 %collective-permute-start.7 = (s16[288,128]{1,0:T(8,128)(2,1)S(1)}, s16[288,128]{1,0:T(8,128)(2,1)S(1)}, u32[]{:S(2)}, u32[]{:S(2)}) collective-permute-start(s16[288,128]{1,0:T(8,128)(2,1)S(1)} %add_select_fusion.2), channel_id=1, source_target_pairs={{0,48},{8,56},{16,32},{24,40},{32,16},{40,24},{48,0},{56,8},{64,11... | collective-permute-start | bytes 221192 | tf_op jit(solution)/shard_map/ppermute | solution.py:309
  109.5 14.2 %all-to-all-start.3 = ((s16[8,144,128]{2,1,0:T(8,128)(2,1)}), s16[8,144,128]{2,1,0:T(8,128)(2,1)S(1)}, u32[]{:S(2)}, u32[]{:S(2)}) async-start(s16[8,144,128]{2,1,0:T(8,128)(2,1)} %replica_total.1), calls=%async_computation.3 | async-start | bytes 589824 | tf_op jit(solution)/shard_map/all_to_all | solution.py:336
  114.1 3.3 %collective-permute-start.8 = (s16[576,128]{1,0:T(8,128)(2,1)S(1)}, s16[576,128]{1,0:T(8,128)(2,1)S(1)}, u32[]{:S(2)}, u32[]{:S(2)}) collective-permute-start(s16[576,128]{1,0:T(8,128)(2,1)S(1)} %add_select_fusion.1), channel_id=1, source_target_pairs={{0,8},{8,0},{16,24},{24,16},{32,40},{40,32},{48,56},{56,48},{64,72... | collective-permute-start | bytes 442376 | tf_op jit(solution)/shard_map/ppermute | solution.py:309

commit v4 on v3

--- a/solution.py
+++ b/solution.py
@@ -12,7 +12,7 @@
 HALF = 64
 FIELDS = 8
 BITS = 4
-TILE = 16
+TILE = 8
 PAIRS = 0x33333333
 
 learning_rate = 0.5
@@ -332,7 +332,6 @@
     hot = whole(line_total, jax.ShapeDtypeStruct(coded.shape[1:], jnp.int16), "line_total", hot)
     payload = whole(replica_total, coded, "replica_total", shared)
     hot = double(hot, "shard", *rounds[2])
-    payload, hot = lax.optimization_barrier((payload, hot))
     codes = lax.all_to_all(payload, "rep", split_axis=0, concat_axis=0, tiled=True)
     for mask, mine in rounds[1::-1]:
         hot = double(hot, "shard", mask, mine)

time: 127 us -> 126 us (level)
  waiting for transfers between devices: 37.5 us -> 34.3 us
  starting transfers between devices: 64 us -> 65.9 us
    all_to_all x1, waiting for transfers between devices: 4.63 us -> 1.76 us  [per_device(): lax.all_to_all(pieces, 'rep', split_axis=0, concat_axis=0, tiled=True)]
    all_to_all x1, starting transfers between devices: 3.43 us -> 5.46 us  [per_device(): lax.all_to_all(payload, 'rep', split_axis=0, concat_axis=0, tiled=True)]
  transfers between devices with their start and end apart: 13 -> 13, of which waited for: 13 -> 12; matrix products, arithmetic and copies ran while one was open for 0% -> 0% of each run, Pallas kernels for 14% -> 15%
where the time goes in v4:
time: 126 us; the launch traced here: 124 us
  starting transfers between devices  65.9 us (52%)
  waiting for transfers between devices  34.3 us (27%)
  Pallas kernels  22.6 us (18%)
    ppermute x3, starting transfers between devices, per_device(): hot = hot + lax.ppermute(hot, 'rep', [(i, i ^ bit) for i in range(FIELDS)])  19.6 us
    ppermute x3, waiting for transfers between devices, halve(): lax.ppermute(lax.dynamic_slice_in_dim(rows, (1 - mine) * half, half), axi...  13.3 us
    all_to_all x1, starting transfers between devices, per_device(): lax.all_to_all(rows, 'shard', split_axis=0, concat_axis=0, tiled=True)  11 us
    pallas_call x1, Pallas kernels, cold_sum(): pl.pallas_call(functools.partial(cold_kernel, blocks=blocks), in_specs=[p...  9.22 us
    all_to_all x1, starting transfers between devices, per_device(): lax.all_to_all(pieces, 'rep', split_axis=0, concat_axis=0, tiled=True)  8.49 us
    ppermute x3, starting transfers between devices, halve(): lax.ppermute(lax.dynamic_slice_in_dim(rows, (1 - mine) * half, half), axi...  7.84 us
    ppermute x3, waiting for transfers between devices, per_device(): hot = hot + lax.ppermute(hot, 'rep', [(i, i ^ bit) for i in range(FIELDS)])  6.96 us
    all_to_all x1, starting transfers between devices, per_device(): lax.all_to_all(hot, 'shard', split_axis=0, concat_axis=0, axis_index_grou...  6.92 us
  transfers between devices with their start and end apart: 13, of which 12 were waited for; matrix products, arithmetic and copies ran while one was open for 0% of the time, Pallas kernels for 15%

profile of v4, /device:TPU:6, one launch (start us, length us, event | category | flops | bytes accessed | tf_op | source)
XLA Modules:
  0.0 124.1 jit_solution(8983375002531095617)
XLA Ops:
  0.6 2.8 %prepare.1.x_ref = bf16[64,136,128]{2,1,0:T(8,128)(2,1)} custom-call(bf16[128,64,128]{2,1,0:T(8,128)(2,1)} %grad_ref.1, s32[64,8,128]{2,1,0:T(8,128)} %bitcast.12, s32[64,128]{1,0:T(8,128)} %bitcast.13), custom_call_target="tpu_custom_call" | custom-call | bytes 5242880 | tf_op jit(solution)/shard_map/prepare/pallas_call | solution.py:141
  3.4 11.0 %all-to-all-start = ((bf16[64,136,128]{2,1,0:T(8,128)(2,1)}), bf16[64,136,128]{2,1,0:T(8,128)(2,1)}, u32[]{:S(2)}, u32[]{:S(2)}) async-start(bf16[64,136,128]{2,1,0:T(8,128)(2,1)} %prepare.1.x_ref), calls=%async_computation | async-start | bytes 4456448 | tf_op jit(solution)/shard_map/all_to_all | solution.py:317
  14.4 5.1 %hot_sum.1 = f32[1024,128]{1,0:T(8,128)S(1)} custom-call(bf16[64,136,128]{2,1,0:T(8,128)(2,1)S(1)} %copy-done, s32[64,2,128]{2,1,0:T(2,128)S(1)} %bitcast.11), custom_call_target="tpu_custom_call" | custom-call | flops 2147483648 | bytes 3145728 | tf_op jit(solution)/shard_map/hot_sum/pallas_call | solution.py:183
  19.6 2.1 %collective-permute-start = (f32[512,128]{1,0:T(8,128)S(1)}, f32[512,128]{1,0:T(8,128)S(1)}, u32[]{:S(2)}, u32[]{:S(2)}) collective-permute-start(f32[512,128]{1,0:T(8,128)S(1)} %constant_dynamic-slice_fusion.2), channel_id=1, source_target_pairs={{0,8},{8,0},{16,24},{24,16},{32,40},{40,32},{48,56},{56,48},{64,72... | collective-permute-start | bytes 786440 | tf_op jit(solution)/shard_map/ppermute | solution.py:304
  21.6 1.4 %collective-permute-done = f32[512,128]{1,0:T(8,128)S(1)} collective-permute-done((f32[512,128]{1,0:T(8,128)S(1)}, f32[512,128]{1,0:T(8,128)S(1)}, u32[]{:S(2)}, u32[]{:S(2)}) %collective-permute-start) | collective-permute-done | bytes 262176 | tf_op jit(solution)/shard_map/ppermute | solution.py:304
  23.0 2.5 %collective-permute-start.1 = (f32[256,128]{1,0:T(8,128)S(1)}, f32[256,128]{1,0:T(8,128)S(1)}, u32[]{:S(2)}, u32[]{:S(2)}) collective-permute-start(f32[256,128]{1,0:T(8,128)S(1)} %constant_dynamic-slice_fusion.1), channel_id=1, source_target_pairs={{0,48},{8,56},{16,32},{24,40},{32,16},{40,24},{48,0},{56,8},{64,11... | collective-permute-start | bytes 393224 | tf_op jit(solution)/shard_map/ppermute | solution.py:304
  25.6 7.8 %collective-permute-done.1 = f32[256,128]{1,0:T(8,128)S(1)} collective-permute-done((f32[256,128]{1,0:T(8,128)S(1)}, f32[256,128]{1,0:T(8,128)S(1)}, u32[]{:S(2)}, u32[]{:S(2)}) %collective-permute-start.1) | collective-permute-done | bytes 131104 | tf_op jit(solution)/shard_map/ppermute | solution.py:304
  33.4 3.3 %collective-permute-start.2 = (f32[128,128]{1,0:T(8,128)S(1)}, f32[128,128]{1,0:T(8,128)S(1)}, u32[]{:S(2)}, u32[]{:S(2)}) collective-permute-start(f32[128,128]{1,0:T(8,128)S(1)} %constant_dynamic-slice_fusion), channel_id=1, source_target_pairs={{0,16},{8,24},{16,0},{24,8},{32,48},{40,56},{48,32},{56,40},{64,80... | collective-permute-start | bytes 196616 | tf_op jit(solution)/shard_map/ppermute | solution.py:304
  36.7 4.1 %collective-permute-done.2 = f32[128,128]{1,0:T(8,128)S(1)} collective-permute-done((f32[128,128]{1,0:T(8,128)S(1)}, f32[128,128]{1,0:T(8,128)S(1)}, u32[]{:S(2)}, u32[]{:S(2)}) %collective-permute-start.2) | collective-permute-done | bytes 65568 | tf_op jit(solution)/shard_map/ppermute | solution.py:304
  40.9 4.2 %collective-permute-start.3 = (f32[128,128]{1,0:T(8,128)S(1)}, f32[128,128]{1,0:T(8,128)S(1)}, u32[]{:S(2)}, u32[]{:S(2)}) collective-permute-start(f32[128,128]{1,0:T(8,128)S(1)} %dynamic-slice_add_fusion.2), channel_id=1, source_target_pairs={{0,1},{1,0},{2,3},{3,2},{4,5},{5,4},{6,7},{7,6},{8,9},{9,8},{10,11... | collective-permute-start | bytes 196616 | tf_op jit(solution)/shard_map/ppermute | solution.py:325
  45.1 2.2 %collective-permute-done.3 = f32[128,128]{1,0:T(8,128)S(1)} collective-permute-done((f32[128,128]{1,0:T(8,128)S(1)}, f32[128,128]{1,0:T(8,128)S(1)}, u32[]{:S(2)}, u32[]{:S(2)}) %collective-permute-start.3) | collective-permute-done | bytes 65568 | tf_op jit(solution)/shard_map/ppermute | solution.py:325
  47.3 6.1 %collective-permute-start.4 = (f32[128,128]{1,0:T(8,128)S(1)}, f32[128,128]{1,0:T(8,128)S(1)}, u32[]{:S(2)}, u32[]{:S(2)}) collective-permute-start(f32[128,128]{1,0:T(8,128)S(1)} %add.45), channel_id=1, source_target_pairs={{0,2},{1,3},{2,0},{3,1},{4,6},{5,7},{6,4},{7,5},{8,10},{9,11},{10,... | collective-permute-start | bytes 196616 | tf_op jit(solution)/shard_map/ppermute | solution.py:325
  53.4 2.2 %collective-permute-done.4 = f32[128,128]{1,0:T(8,128)S(1)} collective-permute-done((f32[128,128]{1,0:T(8,128)S(1)}, f32[128,128]{1,0:T(8,128)S(1)}, u32[]{:S(2)}, u32[]{:S(2)}) %collective-permute-start.4) | collective-permute-done | bytes 65568 | tf_op jit(solution)/shard_map/ppermute | solution.py:325
  55.7 9.3 %collective-permute-start.5 = (f32[128,128]{1,0:T(8,128)S(1)}, f32[128,128]{1,0:T(8,128)S(1)}, u32[]{:S(2)}, u32[]{:S(2)}) collective-permute-start(f32[128,128]{1,0:T(8,128)S(1)} %add.46), channel_id=1, source_target_pairs={{0,4},{1,5},{2,6},{3,7},{4,0},{5,1},{6,2},{7,3},{8,12},{9,13},{10,... | collective-permute-start | bytes 196616 | tf_op jit(solution)/shard_map/ppermute | solution.py:325
  65.0 2.5 %collective-permute-done.5 = f32[128,128]{1,0:T(8,128)S(1)} collective-permute-done((f32[128,128]{1,0:T(8,128)S(1)}, f32[128,128]{1,0:T(8,128)S(1)}, u32[]{:S(2)}, u32[]{:S(2)}) %collective-permute-start.5) | collective-permute-done | bytes 65568 | tf_op jit(solution)/shard_map/ppermute | solution.py:325
  67.5 0.8 spread.1
  68.5 6.9 %all-to-all-start.1 = ((s16[8,136,128]{2,1,0:T(8,128)(2,1)}), s16[8,136,128]{2,1,0:T(8,128)(2,1)S(1)}, u32[]{:S(2)}, u32[]{:S(2)}) async-start(s16[8,136,128]{2,1,0:T(8,128)(2,1)} %spread.1), calls=%async_computation.1 | async-start | bytes 557056 | tf_op jit(solution)/shard_map/all_to_all | solution.py:328
  75.4 9.2 %cold_sum.1 = s16[8,136,128]{2,1,0:T(8,128)(2,1)} custom-call(bf16[64,136,128]{2,1,0:T(8,128)(2,1)} %all-to-all-done.x_ref), custom_call_target="tpu_custom_call" | custom-call | flops 10737418240 | bytes 3145728 | tf_op jit(solution)/shard_map/cold_sum/pallas_call | solution.py:229
  84.7 1.4 %all-to-all-done.1.pieces_ref = s16[8,136,128]{2,1,0:T(8,128)(2,1)S(1)} async-done(((s16[8,136,128]{2,1,0:T(8,128)(2,1)}), s16[8,136,128]{2,1,0:T(8,128)(2,1)S(1)}, u32[]{:S(2)}, u32[]{:S(2)}) %all-to-all-start.1) | async-done | bytes 278560 | tf_op jit(solution)/shard_map/all_to_all | solution.py:328
  86.1 8.5 %all-to-all-start.2 = ((s16[8,136,128]{2,1,0:T(8,128)(2,1)}), s16[8,136,128]{2,1,0:T(8,128)(2,1)S(1)}, u32[]{:S(2)}, u32[]{:S(2)}) async-start(s16[8,136,128]{2,1,0:T(8,128)(2,1)} %cold_sum.1), calls=%async_computation.2 | async-start | bytes 557056 | tf_op jit(solution)/shard_map/all_to_all | solution.py:331
  94.6 0.3 line_total.1
  94.9 2.0 %collective-permute-start.6 = (s16[136,128]{1,0:T(8,128)(2,1)S(1)}, s16[136,128]{1,0:T(8,128)(2,1)S(1)}, u32[]{:S(2)}, u32[]{:S(2)}) collective-permute-start(s16[136,128]{1,0:T(8,128)(2,1)S(1)} %line_total.1), channel_id=1, source_target_pairs={{0,16},{8,24},{16,0},{24,8},{32,48},{40,56},{48,32},{56,40},{64,80... | collective-permute-start | bytes 104456 | tf_op jit(solution)/shard_map/ppermute | solution.py:309
  96.9 3.8 %collective-permute-done.6 = s16[136,128]{1,0:T(8,128)(2,1)S(1)} collective-permute-done((s16[136,128]{1,0:T(8,128)(2,1)S(1)}, s16[136,128]{1,0:T(8,128)(2,1)S(1)}, u32[]{:S(2)}, u32[]{:S(2)}) %collective-permute-start.6) | collective-permute-done | bytes 34848 | tf_op jit(solution)/shard_map/ppermute | solution.py:309
  100.8 2.7 %collective-permute-start.7 = (s16[272,128]{1,0:T(8,128)(2,1)S(1)}, s16[272,128]{1,0:T(8,128)(2,1)S(1)}, u32[]{:S(2)}, u32[]{:S(2)}) collective-permute-start(s16[272,128]{1,0:T(8,128)(2,1)S(1)} %add_select_fusion.2), channel_id=1, source_target_pairs={{0,48},{8,56},{16,32},{24,40},{32,16},{40,24},{48,0},{56,8},{64,11... | collective-permute-start | bytes 208904 | tf_op jit(solution)/shard_map/ppermute | solution.py:309
  103.5 1.8 %all-to-all-done.2.pieces_ref = s16[8,136,128]{2,1,0:T(8,128)(2,1)S(1)} async-done(((s16[8,136,128]{2,1,0:T(8,128)(2,1)}), s16[8,136,128]{2,1,0:T(8,128)(2,1)S(1)}, u32[]{:S(2)}, u32[]{:S(2)}) %all-to-all-start.2) | async-done | bytes 278560 | tf_op jit(solution)/shard_map/all_to_all | solution.py:331
  105.2 1.0 replica_total.1
  106.3 5.5 %all-to-all-start.3 = ((s16[8,136,128]{2,1,0:T(8,128)(2,1)}), s16[8,136,128]{2,1,0:T(8,128)(2,1)S(1)}, u32[]{:S(2)}, u32[]{:S(2)}) async-start(s16[8,136,128]{2,1,0:T(8,128)(2,1)} %replica_total.1), calls=%async_computation.3 | async-start | bytes 557056 | tf_op jit(solution)/shard_map/all_to_all | solution.py:335
  111.8 1.9 %collective-permute-start.8 = (s16[544,128]{1,0:T(8,128)(2,1)S(1)}, s16[544,128]{1,0:T(8,128)(2,1)S(1)}, u32[]{:S(2)}, u32[]{:S(2)}) collective-permute-start(s16[544,128]{1,0:T(8,128)(2,1)S(1)} %add_select_fusion.1), channel_id=1, source_target_pairs={{0,8},{8,0},{16,24},{24,16},{32,40},{40,32},{48,56},{56,48},{64,72... | collective-permute-start | bytes 417800 | tf_op jit(solution)/shard_map/ppermute | solution.py:309
  113.7 1.3 %collective-permute-done.8 = s16[544,128]{1,0:T(8,128)(2,1)S(1)} collective-permute-done((s16[544,128]{1,0:T(8,128)(2,1)S(1)}, s16[544,128]{1,0:T(8,128)(2,1)S(1)}, u32[]{:S(2)}, u32[]{:S(2)}) %collective-permute-start.8) | collective-permute-done | bytes 139296 | tf_op jit(solution)/shard_map/ppermute | solution.py:309
  115.1 1.7 %hot_update.1 = (f32[1024,128]{1,0:T(8,128)}, f32[8,128]{1,0:T(8,128)}) custom-call(s16[8,136,128]{2,1,0:T(8,128)(2,1)S(1)} %bitcast.8, f32[1024,128]{1,0:T(8,128)S(1)} %copy-done.1, f32[8,128]{1,0:T(8,128)S(1)} %bitcast.9), custom_call_target="tpu_custom_call" | custom-call | tf_op jit(solution)/shard_map/hot_update/pallas_call | solution.py:246
  116.8 5.6 %all-to-all-done.3.codes_ref = s16[8,136,128]{2,1,0:T(8,128)(2,1)S(1)} async-done(((s16[8,136,128]{2,1,0:T(8,128)(2,1)}), s16[8,136,128]{2,1,0:T(8,128)(2,1)S(1)}, u32[]{:S(2)}, u32[]{:S(2)}) %all-to-all-start.3) | async-done | bytes 278560 | tf_op jit(solution)/shard_map/all_to_all | solution.py:335
  122.4 1.7 %cold_update.1 = (f32[1024,128]{1,0:T(8,128)}, f32[8,128]{1,0:T(8,128)}) custom-call(s16[8,136,128]{2,1,0:T(8,128)(2,1)S(1)} %all-to-all-done.3.codes_ref, f32[1024,128]{1,0:T(8,128)S(1)} %copy-done.2, f32[8,128]{1,0:T(8,128)S(1)} %bitcast.10), custom_call_target="tpu_custom_call" | custom-call | tf_op jit(solution)/shard_map/cold_update/pallas_call | solution.py:246
  (26 shorter events, 0.5 us)
Async XLA Ops:
  3.4 11.0 %copy-start = (bf16[64,136,128]{2,1,0:T(8,128)(2,1)S(1)}, bf16[64,136,128]{2,1,0:T(8,128)(2,1)}, u32[]{:S(2)}) copy-start(bf16[64,136,128]{2,1,0:T(8,128)(2,1)} %prepare.1.x_ref) | copy-start | bytes 6684676
  3.4 11.0 %copy-start.5 = (s32[128,64,2]{0,2,1:T(2,128)S(1)}, s32[128,64,2]{0,2,1:T(2,128)}, u32[]{:S(2)}) copy-start(s32[128,64,2]{0,2,1:T(2,128)} %param.11) | copy-start | bytes 196612
  3.4 65.1 %all-to-all-start = ((bf16[64,136,128]{2,1,0:T(8,128)(2,1)}), bf16[64,136,128]{2,1,0:T(8,128)(2,1)}, u32[]{:S(2)}, u32[]{:S(2)}) async-start(bf16[64,136,128]{2,1,0:T(8,128)(2,1)} %prepare.1.x_ref), calls=%async_computation | async-start | bytes 4456448 | tf_op jit(solution)/shard_map/all_to_all | solution.py:317
  19.6 3.4 %collective-permute-start = (f32[512,128]{1,0:T(8,128)S(1)}, f32[512,128]{1,0:T(8,128)S(1)}, u32[]{:S(2)}, u32[]{:S(2)}) collective-permute-start(f32[512,128]{1,0:T(8,128)S(1)} %constant_dynamic-slice_fusion.2), channel_id=1, source_target_pairs={{0,8},{8,0},{16,24},{24,16},{32,40},{40,32},{48,56},{56,48},{64,72... | collective-permute-start | bytes 786440 | tf_op jit(solution)/shard_map/ppermute | solution.py:304
  23.0 10.4 %collective-permute-start.1 = (f32[256,128]{1,0:T(8,128)S(1)}, f32[256,128]{1,0:T(8,128)S(1)}, u32[]{:S(2)}, u32[]{:S(2)}) collective-permute-start(f32[256,128]{1,0:T(8,128)S(1)} %constant_dynamic-slice_fusion.1), channel_id=1, source_target_pairs={{0,48},{8,56},{16,32},{24,40},{32,16},{40,24},{48,0},{56,8},{64,11... | collective-permute-start | bytes 393224 | tf_op jit(solution)/shard_map/ppermute | solution.py:304
  33.4 7.4 %collective-permute-start.2 = (f32[128,128]{1,0:T(8,128)S(1)}, f32[128,128]{1,0:T(8,128)S(1)}, u32[]{:S(2)}, u32[]{:S(2)}) collective-permute-start(f32[128,128]{1,0:T(8,128)S(1)} %constant_dynamic-slice_fusion), channel_id=1, source_target_pairs={{0,16},{8,24},{16,0},{24,8},{32,48},{40,56},{48,32},{56,40},{64,80... | collective-permute-start | bytes 196616 | tf_op jit(solution)/shard_map/ppermute | solution.py:304
  40.9 6.5 %collective-permute-start.3 = (f32[128,128]{1,0:T(8,128)S(1)}, f32[128,128]{1,0:T(8,128)S(1)}, u32[]{:S(2)}, u32[]{:S(2)}) collective-permute-start(f32[128,128]{1,0:T(8,128)S(1)} %dynamic-slice_add_fusion.2), channel_id=1, source_target_pairs={{0,1},{1,0},{2,3},{3,2},{4,5},{5,4},{6,7},{7,6},{8,9},{9,8},{10,11... | collective-permute-start | bytes 196616 | tf_op jit(solution)/shard_map/ppermute | solution.py:325
  47.3 8.3 %collective-permute-start.4 = (f32[128,128]{1,0:T(8,128)S(1)}, f32[128,128]{1,0:T(8,128)S(1)}, u32[]{:S(2)}, u32[]{:S(2)}) collective-permute-start(f32[128,128]{1,0:T(8,128)S(1)} %add.45), channel_id=1, source_target_pairs={{0,2},{1,3},{2,0},{3,1},{4,6},{5,7},{6,4},{7,5},{8,10},{9,11},{10,... | collective-permute-start | bytes 196616 | tf_op jit(solution)/shard_map/ppermute | solution.py:325
  55.7 11.8 %collective-permute-start.5 = (f32[128,128]{1,0:T(8,128)S(1)}, f32[128,128]{1,0:T(8,128)S(1)}, u32[]{:S(2)}, u32[]{:S(2)}) collective-permute-start(f32[128,128]{1,0:T(8,128)S(1)} %add.46), channel_id=1, source_target_pairs={{0,4},{1,5},{2,6},{3,7},{4,0},{5,1},{6,2},{7,3},{8,12},{9,13},{10,... | collective-permute-start | bytes 196616 | tf_op jit(solution)/shard_map/ppermute | solution.py:325
  68.5 17.6 %all-to-all-start.1 = ((s16[8,136,128]{2,1,0:T(8,128)(2,1)}), s16[8,136,128]{2,1,0:T(8,128)(2,1)S(1)}, u32[]{:S(2)}, u32[]{:S(2)}) async-start(s16[8,136,128]{2,1,0:T(8,128)(2,1)} %spread.1), calls=%async_computation.1 | async-start | bytes 557056 | tf_op jit(solution)/shard_map/all_to_all | solution.py:328
  84.7 30.5 %copy-start.1 = (f32[1024,128]{1,0:T(8,128)S(1)}, f32[1024,128]{1,0:T(8,128)}, u32[]{:S(2)}) copy-start(f32[1024,128]{1,0:T(8,128)} %table_ref.3) | copy-start | bytes 1572868
  84.7 30.5 %copy-start.3 = (f32[1024]{0:T(1024)S(1)}, f32[1024]{0:T(1024)}, u32[]{:S(2)}) copy-start(f32[1024]{0:T(1024)} %param.15) | copy-start | bytes 12292
  84.7 37.7 %copy-start.2 = (f32[1024,128]{1,0:T(8,128)S(1)}, f32[1024,128]{1,0:T(8,128)}, u32[]{:S(2)}) copy-start(f32[1024,128]{1,0:T(8,128)} %table_ref.2) | copy-start | bytes 1572868
  84.7 37.7 %copy-start.4 = (f32[1024]{0:T(1024)S(1)}, f32[1024]{0:T(1024)}, u32[]{:S(2)}) copy-start(f32[1024]{0:T(1024)} %param.13) | copy-start | bytes 12292
  86.1 19.1 %all-to-all-start.2 = ((s16[8,136,128]{2,1,0:T(8,128)(2,1)}), s16[8,136,128]{2,1,0:T(8,128)(2,1)S(1)}, u32[]{:S(2)}, u32[]{:S(2)}) async-start(s16[8,136,128]{2,1,0:T(8,128)(2,1)} %cold_sum.1), calls=%async_computation.2 | async-start | bytes 557056 | tf_op jit(solution)/shard_map/all_to_all | solution.py:331
  94.9 5.8 %collective-permute-start.6 = (s16[136,128]{1,0:T(8,128)(2,1)S(1)}, s16[136,128]{1,0:T(8,128)(2,1)S(1)}, u32[]{:S(2)}, u32[]{:S(2)}) collective-permute-start(s16[136,128]{1,0:T(8,128)(2,1)S(1)} %line_total.1), channel_id=1, source_target_pairs={{0,16},{8,24},{16,0},{24,8},{32,48},{40,56},{48,32},{56,40},{64,80... | collective-permute-start | bytes 104456 | tf_op jit(solution)/shard_map/ppermute | solution.py:309
  100.8 11.0 %collective-permute-start.7 = (s16[272,128]{1,0:T(8,128)(2,1)S(1)}, s16[272,128]{1,0:T(8,128)(2,1)S(1)}, u32[]{:S(2)}, u32[]{:S(2)}) collective-permute-start(s16[272,128]{1,0:T(8,128)(2,1)S(1)} %add_select_fusion.2), channel_id=1, source_target_pairs={{0,48},{8,56},{16,32},{24,40},{32,16},{40,24},{48,0},{56,8},{64,11... | collective-permute-start | bytes 208904 | tf_op jit(solution)/shard_map/ppermute | solution.py:309
  106.3 16.1 %all-to-all-start.3 = ((s16[8,136,128]{2,1,0:T(8,128)(2,1)}), s16[8,136,128]{2,1,0:T(8,128)(2,1)S(1)}, u32[]{:S(2)}, u32[]{:S(2)}) async-start(s16[8,136,128]{2,1,0:T(8,128)(2,1)} %replica_total.1), calls=%async_computation.3 | async-start | bytes 557056 | tf_op jit(solution)/shard_map/all_to_all | solution.py:335
  111.8 3.3 %collective-permute-start.8 = (s16[544,128]{1,0:T(8,128)(2,1)S(1)}, s16[544,128]{1,0:T(8,128)(2,1)S(1)}, u32[]{:S(2)}, u32[]{:S(2)}) collective-permute-start(s16[544,128]{1,0:T(8,128)(2,1)S(1)} %add_select_fusion.1), channel_id=1, source_target_pairs={{0,8},{8,0},{16,24},{24,16},{32,40},{40,32},{48,56},{56,48},{64,72... | collective-permute-start | bytes 417800 | tf_op jit(solution)/shard_map/ppermute | solution.py:309

commit v5 on v4

--- a/solution.py
+++ b/solution.py
@@ -90,16 +90,16 @@
     return jnp.round(x * jnp.exp2(15.0 - level * 0.125)).astype(jnp.int32).astype(jnp.int16), level
 
 
-def restored(codes, level):
-    return codes.astype(jnp.int32).astype(jnp.float32) * jnp.exp2(level * 0.125 - 15.0)
+def as_float(codes):
+    return codes.astype(jnp.int32).astype(jnp.float32)
+
+
+def row_scales(tile):
+    return jnp.exp2(as_float(tile)[0:1] * 0.125 - 15.0)
 
 
 def level_tile(level):
     return jnp.broadcast_to(to_row(level), (TILE, GROUP)).astype(jnp.int32).astype(jnp.int16)
-
-
-def tile_level(tile):
-    return to_column(tile.astype(jnp.int32).astype(jnp.float32)[0:1])
 
 
 def prepare_kernel(grad_ref, ids_ref, lengths_ref, out_ref, grads, ids_buf, lengths_buf, outs, in_sems, out_sems):
@@ -178,7 +178,7 @@
             out_ref[field * GROUP : (field + 1) * GROUP, :] *= field_scale(field)
 
 
-def hot_sum(rows, ids, blocks=16):
+def hot_sum(rows, ids, blocks=32):
     count, height, width = rows.shape
     return pl.pallas_call(
         functools.partial(hot_kernel, blocks=blocks),
@@ -257,7 +257,7 @@
 def peer_sum(pieces_ref):
     total = None
     for peer in range(FIELDS):
-        piece = restored(pieces_ref[peer, 0:GROUP, :], tile_level(pieces_ref[peer, GROUP:, :]))
+        piece = as_float(pieces_ref[peer, 0:GROUP, :]) * to_column(row_scales(pieces_ref[peer, GROUP:, :]))
         total = piece if total is None else total + piece
     return total
 
@@ -276,17 +276,16 @@
     stored_everywhere(peer_sum(pieces_ref), out_ref)
 
 
-def update_group(group, grad, table_ref, accum_ref, new_table_ref, new_accum_ref):
-    rows = slice(group * GROUP, (group + 1) * GROUP)
-    fresh = to_column(accum_ref[group : group + 1, :]) + jnp.sum(grad * grad, axis=1, keepdims=True) * (1.0 / GROUP)
-    new_table_ref[rows, :] = table_ref[rows, :] - grad * (learning_rate / (jnp.sqrt(fresh) + epsilon))
-    new_accum_ref[group : group + 1, :] = to_row(fresh)
-
-
 def update(codes_ref, table_ref, accum_ref, new_table_ref, new_accum_ref):
     for group in range(FIELDS):
-        grad = restored(codes_ref[group, 0:GROUP, :], tile_level(codes_ref[group, GROUP:, :]))
-        update_group(group, grad, table_ref, accum_ref, new_table_ref, new_accum_ref)
+        rows, one = slice(group * GROUP, (group + 1) * GROUP), slice(group, group + 1)
+        codes = as_float(codes_ref[group, 0:GROUP, :])
+        scales = row_scales(codes_ref[group, GROUP:, :])
+        squares = to_row(jnp.sum(codes * codes, axis=1, keepdims=True))
+        fresh = accum_ref[one, :] + squares * scales * scales * (1.0 / GROUP)
+        step = to_column(scales * (learning_rate / (jnp.sqrt(fresh) + epsilon)))
+        new_accum_ref[one, :] = fresh
+        new_table_ref[rows, :] = table_ref[rows, :] - codes * step
 
 
 def updated(name, codes, table, accum):

time: 126 us -> 125 us (level)
  starting transfers between devices: 65.9 us -> 67.9 us
  waiting for transfers between devices: 34.3 us -> 33 us
    ppermute x3, starting transfers between devices: 6.63 us -> 8.2 us  [double(): lax.ppermute(rows, axis, [(i, i ^ mask) for i in range(lax.axis_size(axis...]
  transfers between devices with their start and end apart: 13 -> 13, of which waited for: 12 -> 12; matrix products, arithmetic and copies ran while one was open for 0% -> 0% of each run, Pallas kernels for 15% -> 14%
where the time goes in v5:
time: 125 us; the launch traced here: 124 us
  starting transfers between devices  67.9 us (54%)
  waiting for transfers between devices  33 us (26%)
  Pallas kernels  21.5 us (17%)
    ppermute x3, starting transfers between devices, per_device(): hot = hot + lax.ppermute(hot, 'rep', [(i, i ^ bit) for i in range(FIELDS)])  20.1 us
    ppermute x3, waiting for transfers between devices, halve(): lax.ppermute(lax.dynamic_slice_in_dim(rows, (1 - mine) * half, half), axi...  12.4 us
    all_to_all x1, starting transfers between devices, per_device(): lax.all_to_all(rows, 'shard', split_axis=0, concat_axis=0, tiled=True)  11 us
    pallas_call x1, Pallas kernels, cold_sum(): pl.pallas_call(functools.partial(cold_kernel, blocks=blocks), in_specs=[p...  9.19 us
    ppermute x3, starting transfers between devices, double(): lax.ppermute(rows, axis, [(i, i ^ mask) for i in range(lax.axis_size(axis...  8.2 us
    ppermute x3, starting transfers between devices, halve(): lax.ppermute(lax.dynamic_slice_in_dim(rows, (1 - mine) * half, half), axi...  7.8 us
    all_to_all x1, starting transfers between devices, per_device(): lax.all_to_all(pieces, 'rep', split_axis=0, concat_axis=0, tiled=True)  7.7 us
    all_to_all x1, starting transfers between devices, per_device(): lax.all_to_all(hot, 'shard', split_axis=0, concat_axis=0, axis_index_grou...  6.97 us
  transfers between devices with their start and end apart: 13, of which 12 were waited for; matrix products, arithmetic and copies ran while one was open for 0% of the time, Pallas kernels for 14%

profile of v5, /device:TPU:6, one launch (start us, length us, event | category | flops | bytes accessed | tf_op | source)
XLA Modules:
  0.0 123.7 jit_solution(18412949770890815202)
XLA Ops:
  0.6 2.8 %prepare.1.x_ref = bf16[64,136,128]{2,1,0:T(8,128)(2,1)} custom-call(bf16[128,64,128]{2,1,0:T(8,128)(2,1)} %grad_ref.1, s32[64,8,128]{2,1,0:T(8,128)} %bitcast.12, s32[64,128]{1,0:T(8,128)} %bitcast.13), custom_call_target="tpu_custom_call" | custom-call | bytes 5242880 | tf_op jit(solution)/shard_map/prepare/pallas_call | solution.py:141
  3.4 11.0 %all-to-all-start = ((bf16[64,136,128]{2,1,0:T(8,128)(2,1)}), bf16[64,136,128]{2,1,0:T(8,128)(2,1)}, u32[]{:S(2)}, u32[]{:S(2)}) async-start(bf16[64,136,128]{2,1,0:T(8,128)(2,1)} %prepare.1.x_ref), calls=%async_computation | async-start | bytes 4456448 | tf_op jit(solution)/shard_map/all_to_all | solution.py:316
  14.4 4.8 %hot_sum.1 = f32[1024,128]{1,0:T(8,128)S(1)} custom-call(bf16[64,136,128]{2,1,0:T(8,128)(2,1)S(1)} %copy-done, s32[64,2,128]{2,1,0:T(2,128)S(1)} %bitcast.11), custom_call_target="tpu_custom_call" | custom-call | flops 2147483648 | bytes 3145728 | tf_op jit(solution)/shard_map/hot_sum/pallas_call | solution.py:183
  19.2 2.1 %collective-permute-start = (f32[512,128]{1,0:T(8,128)S(1)}, f32[512,128]{1,0:T(8,128)S(1)}, u32[]{:S(2)}, u32[]{:S(2)}) collective-permute-start(f32[512,128]{1,0:T(8,128)S(1)} %constant_dynamic-slice_fusion.2), channel_id=1, source_target_pairs={{0,8},{8,0},{16,24},{24,16},{32,40},{40,32},{48,56},{56,48},{64,72... | collective-permute-start | bytes 786440 | tf_op jit(solution)/shard_map/ppermute | solution.py:303
  21.3 1.4 %collective-permute-done = f32[512,128]{1,0:T(8,128)S(1)} collective-permute-done((f32[512,128]{1,0:T(8,128)S(1)}, f32[512,128]{1,0:T(8,128)S(1)}, u32[]{:S(2)}, u32[]{:S(2)}) %collective-permute-start) | collective-permute-done | bytes 262176 | tf_op jit(solution)/shard_map/ppermute | solution.py:303
  22.7 2.5 %collective-permute-start.1 = (f32[256,128]{1,0:T(8,128)S(1)}, f32[256,128]{1,0:T(8,128)S(1)}, u32[]{:S(2)}, u32[]{:S(2)}) collective-permute-start(f32[256,128]{1,0:T(8,128)S(1)} %constant_dynamic-slice_fusion.1), channel_id=1, source_target_pairs={{0,48},{8,56},{16,32},{24,40},{32,16},{40,24},{48,0},{56,8},{64,11... | collective-permute-start | bytes 393224 | tf_op jit(solution)/shard_map/ppermute | solution.py:303
  25.2 7.9 %collective-permute-done.1 = f32[256,128]{1,0:T(8,128)S(1)} collective-permute-done((f32[256,128]{1,0:T(8,128)S(1)}, f32[256,128]{1,0:T(8,128)S(1)}, u32[]{:S(2)}, u32[]{:S(2)}) %collective-permute-start.1) | collective-permute-done | bytes 131104 | tf_op jit(solution)/shard_map/ppermute | solution.py:303
  33.1 3.2 %collective-permute-start.2 = (f32[128,128]{1,0:T(8,128)S(1)}, f32[128,128]{1,0:T(8,128)S(1)}, u32[]{:S(2)}, u32[]{:S(2)}) collective-permute-start(f32[128,128]{1,0:T(8,128)S(1)} %constant_dynamic-slice_fusion), channel_id=1, source_target_pairs={{0,16},{8,24},{16,0},{24,8},{32,48},{40,56},{48,32},{56,40},{64,80... | collective-permute-start | bytes 196616 | tf_op jit(solution)/shard_map/ppermute | solution.py:303
  36.4 3.2 %collective-permute-done.2 = f32[128,128]{1,0:T(8,128)S(1)} collective-permute-done((f32[128,128]{1,0:T(8,128)S(1)}, f32[128,128]{1,0:T(8,128)S(1)}, u32[]{:S(2)}, u32[]{:S(2)}) %collective-permute-start.2) | collective-permute-done | bytes 65568 | tf_op jit(solution)/shard_map/ppermute | solution.py:303
  39.6 4.7 %collective-permute-start.3 = (f32[128,128]{1,0:T(8,128)S(1)}, f32[128,128]{1,0:T(8,128)S(1)}, u32[]{:S(2)}, u32[]{:S(2)}) collective-permute-start(f32[128,128]{1,0:T(8,128)S(1)} %dynamic-slice_add_fusion.2), channel_id=1, source_target_pairs={{0,1},{1,0},{2,3},{3,2},{4,5},{5,4},{6,7},{7,6},{8,9},{9,8},{10,11... | collective-permute-start | bytes 196616 | tf_op jit(solution)/shard_map/ppermute | solution.py:324
  44.3 2.2 %collective-permute-done.3 = f32[128,128]{1,0:T(8,128)S(1)} collective-permute-done((f32[128,128]{1,0:T(8,128)S(1)}, f32[128,128]{1,0:T(8,128)S(1)}, u32[]{:S(2)}, u32[]{:S(2)}) %collective-permute-start.3) | collective-permute-done | bytes 65568 | tf_op jit(solution)/shard_map/ppermute | solution.py:324
  46.6 6.1 %collective-permute-start.4 = (f32[128,128]{1,0:T(8,128)S(1)}, f32[128,128]{1,0:T(8,128)S(1)}, u32[]{:S(2)}, u32[]{:S(2)}) collective-permute-start(f32[128,128]{1,0:T(8,128)S(1)} %add.45), channel_id=1, source_target_pairs={{0,2},{1,3},{2,0},{3,1},{4,6},{5,7},{6,4},{7,5},{8,10},{9,11},{10,... | collective-permute-start | bytes 196616 | tf_op jit(solution)/shard_map/ppermute | solution.py:324
  52.7 2.2 %collective-permute-done.4 = f32[128,128]{1,0:T(8,128)S(1)} collective-permute-done((f32[128,128]{1,0:T(8,128)S(1)}, f32[128,128]{1,0:T(8,128)S(1)}, u32[]{:S(2)}, u32[]{:S(2)}) %collective-permute-start.4) | collective-permute-done | bytes 65568 | tf_op jit(solution)/shard_map/ppermute | solution.py:324
  54.9 9.3 %collective-permute-start.5 = (f32[128,128]{1,0:T(8,128)S(1)}, f32[128,128]{1,0:T(8,128)S(1)}, u32[]{:S(2)}, u32[]{:S(2)}) collective-permute-start(f32[128,128]{1,0:T(8,128)S(1)} %add.46), channel_id=1, source_target_pairs={{0,4},{1,5},{2,6},{3,7},{4,0},{5,1},{6,2},{7,3},{8,12},{9,13},{10,... | collective-permute-start | bytes 196616 | tf_op jit(solution)/shard_map/ppermute | solution.py:324
  64.2 2.5 %collective-permute-done.5 = f32[128,128]{1,0:T(8,128)S(1)} collective-permute-done((f32[128,128]{1,0:T(8,128)S(1)}, f32[128,128]{1,0:T(8,128)S(1)}, u32[]{:S(2)}, u32[]{:S(2)}) %collective-permute-start.5) | collective-permute-done | bytes 65568 | tf_op jit(solution)/shard_map/ppermute | solution.py:324
  66.7 0.8 spread.1
  67.5 1.0 all-to-all-done.x_ref
  68.5 7.0 %all-to-all-start.1 = ((s16[8,136,128]{2,1,0:T(8,128)(2,1)}), s16[8,136,128]{2,1,0:T(8,128)(2,1)S(1)}, u32[]{:S(2)}, u32[]{:S(2)}) async-start(s16[8,136,128]{2,1,0:T(8,128)(2,1)} %spread.1), calls=%async_computation.1 | async-start | bytes 557056 | tf_op jit(solution)/shard_map/all_to_all | solution.py:327
  75.5 9.2 %cold_sum.1 = s16[8,136,128]{2,1,0:T(8,128)(2,1)} custom-call(bf16[64,136,128]{2,1,0:T(8,128)(2,1)} %all-to-all-done.x_ref), custom_call_target="tpu_custom_call" | custom-call | flops 10737418240 | bytes 3145728 | tf_op jit(solution)/shard_map/cold_sum/pallas_call | solution.py:229
  84.7 1.4 %all-to-all-done.1.pieces_ref = s16[8,136,128]{2,1,0:T(8,128)(2,1)S(1)} async-done(((s16[8,136,128]{2,1,0:T(8,128)(2,1)}), s16[8,136,128]{2,1,0:T(8,128)(2,1)S(1)}, u32[]{:S(2)}, u32[]{:S(2)}) %all-to-all-start.1) | async-done | bytes 278560 | tf_op jit(solution)/shard_map/all_to_all | solution.py:327
  86.1 7.7 %all-to-all-start.2 = ((s16[8,136,128]{2,1,0:T(8,128)(2,1)}), s16[8,136,128]{2,1,0:T(8,128)(2,1)S(1)}, u32[]{:S(2)}, u32[]{:S(2)}) async-start(s16[8,136,128]{2,1,0:T(8,128)(2,1)} %cold_sum.1), calls=%async_computation.2 | async-start | bytes 557056 | tf_op jit(solution)/shard_map/all_to_all | solution.py:330
  94.2 2.8 %collective-permute-start.6 = (s16[136,128]{1,0:T(8,128)(2,1)S(1)}, s16[136,128]{1,0:T(8,128)(2,1)S(1)}, u32[]{:S(2)}, u32[]{:S(2)}) collective-permute-start(s16[136,128]{1,0:T(8,128)(2,1)S(1)} %line_total.1), channel_id=1, source_target_pairs={{0,16},{8,24},{16,0},{24,8},{32,48},{40,56},{48,32},{56,40},{64,80... | collective-permute-start | bytes 104456 | tf_op jit(solution)/shard_map/ppermute | solution.py:308
  97.0 3.0 %collective-permute-done.6 = s16[136,128]{1,0:T(8,128)(2,1)S(1)} collective-permute-done((s16[136,128]{1,0:T(8,128)(2,1)S(1)}, s16[136,128]{1,0:T(8,128)(2,1)S(1)}, u32[]{:S(2)}, u32[]{:S(2)}) %collective-permute-start.6) | collective-permute-done | bytes 34848 | tf_op jit(solution)/shard_map/ppermute | solution.py:308
  100.0 3.4 %collective-permute-start.7 = (s16[272,128]{1,0:T(8,128)(2,1)S(1)}, s16[272,128]{1,0:T(8,128)(2,1)S(1)}, u32[]{:S(2)}, u32[]{:S(2)}) collective-permute-start(s16[272,128]{1,0:T(8,128)(2,1)S(1)} %add_select_fusion.2), channel_id=1, source_target_pairs={{0,48},{8,56},{16,32},{24,40},{32,16},{40,24},{48,0},{56,8},{64,11... | collective-permute-start | bytes 208904 | tf_op jit(solution)/shard_map/ppermute | solution.py:308
  103.5 1.0 all-to-all-done.2.pieces_ref
  104.5 1.0 replica_total.1
  105.5 6.2 %all-to-all-start.3 = ((s16[8,136,128]{2,1,0:T(8,128)(2,1)}), s16[8,136,128]{2,1,0:T(8,128)(2,1)S(1)}, u32[]{:S(2)}, u32[]{:S(2)}) async-start(s16[8,136,128]{2,1,0:T(8,128)(2,1)} %replica_total.1), calls=%async_computation.3 | async-start | bytes 557056 | tf_op jit(solution)/shard_map/all_to_all | solution.py:334
  111.8 1.9 %collective-permute-start.8 = (s16[544,128]{1,0:T(8,128)(2,1)S(1)}, s16[544,128]{1,0:T(8,128)(2,1)S(1)}, u32[]{:S(2)}, u32[]{:S(2)}) collective-permute-start(s16[544,128]{1,0:T(8,128)(2,1)S(1)} %add_select_fusion.1), channel_id=1, source_target_pairs={{0,8},{8,0},{16,24},{24,16},{32,40},{40,32},{48,56},{56,48},{64,72... | collective-permute-start | bytes 417800 | tf_op jit(solution)/shard_map/ppermute | solution.py:308
  113.7 1.3 %collective-permute-done.8 = s16[544,128]{1,0:T(8,128)(2,1)S(1)} collective-permute-done((s16[544,128]{1,0:T(8,128)(2,1)S(1)}, s16[544,128]{1,0:T(8,128)(2,1)S(1)}, u32[]{:S(2)}, u32[]{:S(2)}) %collective-permute-start.8) | collective-permute-done | bytes 139296 | tf_op jit(solution)/shard_map/ppermute | solution.py:308
  115.1 1.3 %hot_update.1 = (f32[1024,128]{1,0:T(8,128)}, f32[8,128]{1,0:T(8,128)}) custom-call(s16[8,136,128]{2,1,0:T(8,128)(2,1)S(1)} %bitcast.8, f32[1024,128]{1,0:T(8,128)S(1)} %copy-done.1, f32[8,128]{1,0:T(8,128)S(1)} %bitcast.9), custom_call_target="tpu_custom_call" | custom-call | tf_op jit(solution)/shard_map/hot_update/pallas_call | solution.py:246
  116.5 5.9 %all-to-all-done.3.codes_ref = s16[8,136,128]{2,1,0:T(8,128)(2,1)S(1)} async-done(((s16[8,136,128]{2,1,0:T(8,128)(2,1)}), s16[8,136,128]{2,1,0:T(8,128)(2,1)S(1)}, u32[]{:S(2)}, u32[]{:S(2)}) %all-to-all-start.3) | async-done | bytes 278560 | tf_op jit(solution)/shard_map/all_to_all | solution.py:334
  122.4 1.3 %cold_update.1 = (f32[1024,128]{1,0:T(8,128)}, f32[8,128]{1,0:T(8,128)}) custom-call(s16[8,136,128]{2,1,0:T(8,128)(2,1)S(1)} %all-to-all-done.3.codes_ref, f32[1024,128]{1,0:T(8,128)S(1)} %copy-done.2, f32[8,128]{1,0:T(8,128)S(1)} %bitcast.10), custom_call_target="tpu_custom_call" | custom-call | tf_op jit(solution)/shard_map/cold_update/pallas_call | solution.py:246
  (26 shorter events, 0.6 us)
Async XLA Ops:
  3.4 11.0 %copy-start = (bf16[64,136,128]{2,1,0:T(8,128)(2,1)S(1)}, bf16[64,136,128]{2,1,0:T(8,128)(2,1)}, u32[]{:S(2)}) copy-start(bf16[64,136,128]{2,1,0:T(8,128)(2,1)} %prepare.1.x_ref) | copy-start | bytes 6684676
  3.4 11.0 %copy-start.5 = (s32[128,64,2]{0,2,1:T(2,128)S(1)}, s32[128,64,2]{0,2,1:T(2,128)}, u32[]{:S(2)}) copy-start(s32[128,64,2]{0,2,1:T(2,128)} %param.11) | copy-start | bytes 196612
  3.4 65.1 %all-to-all-start = ((bf16[64,136,128]{2,1,0:T(8,128)(2,1)}), bf16[64,136,128]{2,1,0:T(8,128)(2,1)}, u32[]{:S(2)}, u32[]{:S(2)}) async-start(bf16[64,136,128]{2,1,0:T(8,128)(2,1)} %prepare.1.x_ref), calls=%async_computation | async-start | bytes 4456448 | tf_op jit(solution)/shard_map/all_to_all | solution.py:316
  19.2 3.4 %collective-permute-start = (f32[512,128]{1,0:T(8,128)S(1)}, f32[512,128]{1,0:T(8,128)S(1)}, u32[]{:S(2)}, u32[]{:S(2)}) collective-permute-start(f32[512,128]{1,0:T(8,128)S(1)} %constant_dynamic-slice_fusion.2), channel_id=1, source_target_pairs={{0,8},{8,0},{16,24},{24,16},{32,40},{40,32},{48,56},{56,48},{64,72... | collective-permute-start | bytes 786440 | tf_op jit(solution)/shard_map/ppermute | solution.py:303
  22.7 10.4 %collective-permute-start.1 = (f32[256,128]{1,0:T(8,128)S(1)}, f32[256,128]{1,0:T(8,128)S(1)}, u32[]{:S(2)}, u32[]{:S(2)}) collective-permute-start(f32[256,128]{1,0:T(8,128)S(1)} %constant_dynamic-slice_fusion.1), channel_id=1, source_target_pairs={{0,48},{8,56},{16,32},{24,40},{32,16},{40,24},{48,0},{56,8},{64,11... | collective-permute-start | bytes 393224 | tf_op jit(solution)/shard_map/ppermute | solution.py:303
  33.1 6.5 %collective-permute-start.2 = (f32[128,128]{1,0:T(8,128)S(1)}, f32[128,128]{1,0:T(8,128)S(1)}, u32[]{:S(2)}, u32[]{:S(2)}) collective-permute-start(f32[128,128]{1,0:T(8,128)S(1)} %constant_dynamic-slice_fusion), channel_id=1, source_target_pairs={{0,16},{8,24},{16,0},{24,8},{32,48},{40,56},{48,32},{56,40},{64,80... | collective-permute-start | bytes 196616 | tf_op jit(solution)/shard_map/ppermute | solution.py:303
  39.6 6.9 %collective-permute-start.3 = (f32[128,128]{1,0:T(8,128)S(1)}, f32[128,128]{1,0:T(8,128)S(1)}, u32[]{:S(2)}, u32[]{:S(2)}) collective-permute-start(f32[128,128]{1,0:T(8,128)S(1)} %dynamic-slice_add_fusion.2), channel_id=1, source_target_pairs={{0,1},{1,0},{2,3},{3,2},{4,5},{5,4},{6,7},{7,6},{8,9},{9,8},{10,11... | collective-permute-start | bytes 196616 | tf_op jit(solution)/shard_map/ppermute | solution.py:324
  46.6 8.3 %collective-permute-start.4 = (f32[128,128]{1,0:T(8,128)S(1)}, f32[128,128]{1,0:T(8,128)S(1)}, u32[]{:S(2)}, u32[]{:S(2)}) collective-permute-start(f32[128,128]{1,0:T(8,128)S(1)} %add.45), channel_id=1, source_target_pairs={{0,2},{1,3},{2,0},{3,1},{4,6},{5,7},{6,4},{7,5},{8,10},{9,11},{10,... | collective-permute-start | bytes 196616 | tf_op jit(solution)/shard_map/ppermute | solution.py:324
  54.9 11.7 %collective-permute-start.5 = (f32[128,128]{1,0:T(8,128)S(1)}, f32[128,128]{1,0:T(8,128)S(1)}, u32[]{:S(2)}, u32[]{:S(2)}) collective-permute-start(f32[128,128]{1,0:T(8,128)S(1)} %add.46), channel_id=1, source_target_pairs={{0,4},{1,5},{2,6},{3,7},{4,0},{5,1},{6,2},{7,3},{8,12},{9,13},{10,... | collective-permute-start | bytes 196616 | tf_op jit(solution)/shard_map/ppermute | solution.py:324
  68.5 17.6 %all-to-all-start.1 = ((s16[8,136,128]{2,1,0:T(8,128)(2,1)}), s16[8,136,128]{2,1,0:T(8,128)(2,1)S(1)}, u32[]{:S(2)}, u32[]{:S(2)}) async-start(s16[8,136,128]{2,1,0:T(8,128)(2,1)} %spread.1), calls=%async_computation.1 | async-start | bytes 557056 | tf_op jit(solution)/shard_map/all_to_all | solution.py:327
  84.7 30.4 %copy-start.1 = (f32[1024,128]{1,0:T(8,128)S(1)}, f32[1024,128]{1,0:T(8,128)}, u32[]{:S(2)}) copy-start(f32[1024,128]{1,0:T(8,128)} %table_ref.3) | copy-start | bytes 1572868
  84.7 30.4 %copy-start.3 = (f32[1024]{0:T(1024)S(1)}, f32[1024]{0:T(1024)}, u32[]{:S(2)}) copy-start(f32[1024]{0:T(1024)} %param.15) | copy-start | bytes 12292
  84.7 37.7 %copy-start.2 = (f32[1024,128]{1,0:T(8,128)S(1)}, f32[1024,128]{1,0:T(8,128)}, u32[]{:S(2)}) copy-start(f32[1024,128]{1,0:T(8,128)} %table_ref.2) | copy-start | bytes 1572868
  84.7 37.7 %copy-start.4 = (f32[1024]{0:T(1024)S(1)}, f32[1024]{0:T(1024)}, u32[]{:S(2)}) copy-start(f32[1024]{0:T(1024)} %param.13) | copy-start | bytes 12292
  86.1 18.4 %all-to-all-start.2 = ((s16[8,136,128]{2,1,0:T(8,128)(2,1)}), s16[8,136,128]{2,1,0:T(8,128)(2,1)S(1)}, u32[]{:S(2)}, u32[]{:S(2)}) async-start(s16[8,136,128]{2,1,0:T(8,128)(2,1)} %cold_sum.1), calls=%async_computation.2 | async-start | bytes 557056 | tf_op jit(solution)/shard_map/all_to_all | solution.py:330
  94.2 5.8 %collective-permute-start.6 = (s16[136,128]{1,0:T(8,128)(2,1)S(1)}, s16[136,128]{1,0:T(8,128)(2,1)S(1)}, u32[]{:S(2)}, u32[]{:S(2)}) collective-permute-start(s16[136,128]{1,0:T(8,128)(2,1)S(1)} %line_total.1), channel_id=1, source_target_pairs={{0,16},{8,24},{16,0},{24,8},{32,48},{40,56},{48,32},{56,40},{64,80... | collective-permute-start | bytes 104456 | tf_op jit(solution)/shard_map/ppermute | solution.py:308
  100.0 11.7 %collective-permute-start.7 = (s16[272,128]{1,0:T(8,128)(2,1)S(1)}, s16[272,128]{1,0:T(8,128)(2,1)S(1)}, u32[]{:S(2)}, u32[]{:S(2)}) collective-permute-start(s16[272,128]{1,0:T(8,128)(2,1)S(1)} %add_select_fusion.2), channel_id=1, source_target_pairs={{0,48},{8,56},{16,32},{24,40},{32,16},{40,24},{48,0},{56,8},{64,11... | collective-permute-start | bytes 208904 | tf_op jit(solution)/shard_map/ppermute | solution.py:308
  105.5 16.9 %all-to-all-start.3 = ((s16[8,136,128]{2,1,0:T(8,128)(2,1)}), s16[8,136,128]{2,1,0:T(8,128)(2,1)S(1)}, u32[]{:S(2)}, u32[]{:S(2)}) async-start(s16[8,136,128]{2,1,0:T(8,128)(2,1)} %replica_total.1), calls=%async_computation.3 | async-start | bytes 557056 | tf_op jit(solution)/shard_map/all_to_all | solution.py:334
  111.8 3.3 %collective-permute-start.8 = (s16[544,128]{1,0:T(8,128)(2,1)S(1)}, s16[544,128]{1,0:T(8,128)(2,1)S(1)}, u32[]{:S(2)}, u32[]{:S(2)}) collective-permute-start(s16[544,128]{1,0:T(8,128)(2,1)S(1)} %add_select_fusion.1), channel_id=1, source_target_pairs={{0,8},{8,0},{16,24},{24,16},{32,40},{40,32},{48,56},{56,48},{64,72... | collective-permute-start | bytes 417800 | tf_op jit(solution)/shard_map/ppermute | solution.py:308

commit v6 on v5

--- a/solution.py
+++ b/solution.py
@@ -22,15 +22,11 @@
 
 
 def decode_ids(code):
-    key = jnp.zeros(code.shape, jnp.float32)
-    unit = jnp.zeros(code.shape, jnp.int32)
-    for field in range(FIELDS):
-        reached = code >= float(GROUP * 2**field)
-        key = jnp.where(reached, code * 2.0**-field - float(GROUP), key)
-        unit = jnp.where(reached, 1 << (BITS * field), unit)
-    upper = key >= float(HALF)
-    key = jnp.where(upper, key - float(HALF), key)
-    return key.astype(jnp.int32), jnp.where(upper, unit * 4, unit)
+    number = code.astype(jnp.int32)
+    zeros = lax.clz(number)
+    low = lax.shift_right_logical(number, 24 - zeros)
+    bit = 4 * (24 - zeros) + (lax.shift_right_logical(low, 5) & 2)
+    return low & (HALF - 1), jnp.where(number > 0, lax.shift_left(jnp.ones_like(number), bit), 0)
 
 
 def packed_counts(key, unit):
@@ -88,6 +84,17 @@
     top = jnp.maximum(jnp.max(jnp.abs(x), axis=1, keepdims=True), 1e-30)
     level = jnp.ceil(8.0 * jnp.log2(top) + 0.05)
     return jnp.round(x * jnp.exp2(15.0 - level * 0.125)).astype(jnp.int32).astype(jnp.int16), level
+
+
+def quantized_in_row(x):
+    top = jnp.maximum(to_row(jnp.max(jnp.abs(x), axis=1, keepdims=True)), 1e-30)
+    level = jnp.ceil(8.0 * jnp.log2(top) + 0.05)
+    scaled = x * to_column(jnp.exp2(15.0 - level * 0.125))
+    return jnp.round(scaled).astype(jnp.int32).astype(jnp.int16), level
+
+
+def row_tile(level):
+    return jnp.broadcast_to(level, (TILE, GROUP)).astype(jnp.int32).astype(jnp.int16)
 
 
 def as_float(codes):
@@ -247,8 +254,8 @@
 
 
 def stored_everywhere(rows, out_ref):
-    codes, level = quantized(rows)
-    tile = level_tile(level)
+    codes, level = quantized_in_row(rows)
+    tile = row_tile(level)
     for peer in range(FIELDS):
         out_ref[peer, 0:GROUP, :] = codes
         out_ref[peer, GROUP:, :] = tile
@@ -267,9 +274,9 @@
 
 
 def line_total(pieces_ref, out_ref):
-    codes, level = quantized(peer_sum(pieces_ref))
+    codes, level = quantized_in_row(peer_sum(pieces_ref))
     out_ref[0:GROUP, :] = codes
-    out_ref[GROUP:, :] = level_tile(level)
+    out_ref[GROUP:, :] = row_tile(level)
 
 
 def replica_total(pieces_ref, out_ref):

time: 125 us -> 125 us (level)
  no operation moved by 1% of the time
where the time goes in v6:
time: 125 us; the launch traced here: 124 us
  starting transfers between devices  67.9 us (54%)
  waiting for transfers between devices  33.1 us (26%)
  Pallas kernels  21.7 us (17%)
    ppermute x3, starting transfers between devices, per_device(): hot = hot + lax.ppermute(hot, 'rep', [(i, i ^ bit) for i in range(FIELDS)])  20.1 us
    ppermute x3, waiting for transfers between devices, halve(): lax.ppermute(lax.dynamic_slice_in_dim(rows, (1 - mine) * half, half), axi...  12.4 us
    all_to_all x1, starting transfers between devices, per_device(): lax.all_to_all(rows, 'shard', split_axis=0, concat_axis=0, tiled=True)  11 us
    pallas_call x1, Pallas kernels, cold_sum(): pl.pallas_call(functools.partial(cold_kernel, blocks=blocks), in_specs=[p...  9.06 us
    ppermute x3, starting transfers between devices, double(): lax.ppermute(rows, axis, [(i, i ^ mask) for i in range(lax.axis_size(axis...  8.1 us
    ppermute x3, starting transfers between devices, halve(): lax.ppermute(lax.dynamic_slice_in_dim(rows, (1 - mine) * half, half), axi...  7.8 us
    all_to_all x1, starting transfers between devices, per_device(): lax.all_to_all(pieces, 'rep', split_axis=0, concat_axis=0, tiled=True)  7.7 us
    all_to_all x1, starting transfers between devices, per_device(): lax.all_to_all(hot, 'shard', split_axis=0, concat_axis=0, axis_index_grou...  7.07 us
  transfers between devices with their start and end apart: 13, of which 12 were waited for; matrix products, arithmetic and copies ran while one was open for 0% of the time, Pallas kernels for 14%

profile of v6, /device:TPU:6, one launch (start us, length us, event | category | flops | bytes accessed | tf_op | source)
XLA Modules:
  0.0 123.9 jit_solution(14717680885881432010)
XLA Ops:
  0.6 2.8 %prepare.1.x_ref = bf16[64,136,128]{2,1,0:T(8,128)(2,1)} custom-call(bf16[128,64,128]{2,1,0:T(8,128)(2,1)} %grad_ref.1, s32[64,8,128]{2,1,0:T(8,128)} %bitcast.12, s32[64,128]{1,0:T(8,128)} %bitcast.13), custom_call_target="tpu_custom_call" | custom-call | bytes 5242880 | tf_op jit(solution)/shard_map/prepare/pallas_call | solution.py:148
  3.4 11.0 %all-to-all-start = ((bf16[64,136,128]{2,1,0:T(8,128)(2,1)}), bf16[64,136,128]{2,1,0:T(8,128)(2,1)}, u32[]{:S(2)}, u32[]{:S(2)}) async-start(bf16[64,136,128]{2,1,0:T(8,128)(2,1)} %prepare.1.x_ref), calls=%async_computation | async-start | bytes 4456448 | tf_op jit(solution)/shard_map/all_to_all | solution.py:323
  14.4 4.8 %hot_sum.1 = f32[1024,128]{1,0:T(8,128)S(1)} custom-call(bf16[64,136,128]{2,1,0:T(8,128)(2,1)S(1)} %copy-done, s32[64,2,128]{2,1,0:T(2,128)S(1)} %bitcast.11), custom_call_target="tpu_custom_call" | custom-call | flops 2147483648 | bytes 3145728 | tf_op jit(solution)/shard_map/hot_sum/pallas_call | solution.py:190
  19.2 2.1 %collective-permute-start = (f32[512,128]{1,0:T(8,128)S(1)}, f32[512,128]{1,0:T(8,128)S(1)}, u32[]{:S(2)}, u32[]{:S(2)}) collective-permute-start(f32[512,128]{1,0:T(8,128)S(1)} %constant_dynamic-slice_fusion.2), channel_id=1, source_target_pairs={{0,8},{8,0},{16,24},{24,16},{32,40},{40,32},{48,56},{56,48},{64,72... | collective-permute-start | bytes 786440 | tf_op jit(solution)/shard_map/ppermute | solution.py:310
  21.3 1.4 %collective-permute-done = f32[512,128]{1,0:T(8,128)S(1)} collective-permute-done((f32[512,128]{1,0:T(8,128)S(1)}, f32[512,128]{1,0:T(8,128)S(1)}, u32[]{:S(2)}, u32[]{:S(2)}) %collective-permute-start) | collective-permute-done | bytes 262176 | tf_op jit(solution)/shard_map/ppermute | solution.py:310
  22.7 2.5 %collective-permute-start.1 = (f32[256,128]{1,0:T(8,128)S(1)}, f32[256,128]{1,0:T(8,128)S(1)}, u32[]{:S(2)}, u32[]{:S(2)}) collective-permute-start(f32[256,128]{1,0:T(8,128)S(1)} %constant_dynamic-slice_fusion.1), channel_id=1, source_target_pairs={{0,48},{8,56},{16,32},{24,40},{32,16},{40,24},{48,0},{56,8},{64,11... | collective-permute-start | bytes 393224 | tf_op jit(solution)/shard_map/ppermute | solution.py:310
  25.2 7.9 %collective-permute-done.1 = f32[256,128]{1,0:T(8,128)S(1)} collective-permute-done((f32[256,128]{1,0:T(8,128)S(1)}, f32[256,128]{1,0:T(8,128)S(1)}, u32[]{:S(2)}, u32[]{:S(2)}) %collective-permute-start.1) | collective-permute-done | bytes 131104 | tf_op jit(solution)/shard_map/ppermute | solution.py:310
  33.1 3.2 %collective-permute-start.2 = (f32[128,128]{1,0:T(8,128)S(1)}, f32[128,128]{1,0:T(8,128)S(1)}, u32[]{:S(2)}, u32[]{:S(2)}) collective-permute-start(f32[128,128]{1,0:T(8,128)S(1)} %constant_dynamic-slice_fusion), channel_id=1, source_target_pairs={{0,16},{8,24},{16,0},{24,8},{32,48},{40,56},{48,32},{56,40},{64,80... | collective-permute-start | bytes 196616 | tf_op jit(solution)/shard_map/ppermute | solution.py:310
  36.4 3.2 %collective-permute-done.2 = f32[128,128]{1,0:T(8,128)S(1)} collective-permute-done((f32[128,128]{1,0:T(8,128)S(1)}, f32[128,128]{1,0:T(8,128)S(1)}, u32[]{:S(2)}, u32[]{:S(2)}) %collective-permute-start.2) | collective-permute-done | bytes 65568 | tf_op jit(solution)/shard_map/ppermute | solution.py:310
  39.6 4.7 %collective-permute-start.3 = (f32[128,128]{1,0:T(8,128)S(1)}, f32[128,128]{1,0:T(8,128)S(1)}, u32[]{:S(2)}, u32[]{:S(2)}) collective-permute-start(f32[128,128]{1,0:T(8,128)S(1)} %dynamic-slice_add_fusion.2), channel_id=1, source_target_pairs={{0,1},{1,0},{2,3},{3,2},{4,5},{5,4},{6,7},{7,6},{8,9},{9,8},{10,11... | collective-permute-start | bytes 196616 | tf_op jit(solution)/shard_map/ppermute | solution.py:331
  44.3 2.2 %collective-permute-done.3 = f32[128,128]{1,0:T(8,128)S(1)} collective-permute-done((f32[128,128]{1,0:T(8,128)S(1)}, f32[128,128]{1,0:T(8,128)S(1)}, u32[]{:S(2)}, u32[]{:S(2)}) %collective-permute-start.3) | collective-permute-done | bytes 65568 | tf_op jit(solution)/shard_map/ppermute | solution.py:331
  46.6 6.1 %collective-permute-start.4 = (f32[128,128]{1,0:T(8,128)S(1)}, f32[128,128]{1,0:T(8,128)S(1)}, u32[]{:S(2)}, u32[]{:S(2)}) collective-permute-start(f32[128,128]{1,0:T(8,128)S(1)} %add.45), channel_id=1, source_target_pairs={{0,2},{1,3},{2,0},{3,1},{4,6},{5,7},{6,4},{7,5},{8,10},{9,11},{10,... | collective-permute-start | bytes 196616 | tf_op jit(solution)/shard_map/ppermute | solution.py:331
  52.7 2.2 %collective-permute-done.4 = f32[128,128]{1,0:T(8,128)S(1)} collective-permute-done((f32[128,128]{1,0:T(8,128)S(1)}, f32[128,128]{1,0:T(8,128)S(1)}, u32[]{:S(2)}, u32[]{:S(2)}) %collective-permute-start.4) | collective-permute-done | bytes 65568 | tf_op jit(solution)/shard_map/ppermute | solution.py:331
  54.9 9.3 %collective-permute-start.5 = (f32[128,128]{1,0:T(8,128)S(1)}, f32[128,128]{1,0:T(8,128)S(1)}, u32[]{:S(2)}, u32[]{:S(2)}) collective-permute-start(f32[128,128]{1,0:T(8,128)S(1)} %add.46), channel_id=1, source_target_pairs={{0,4},{1,5},{2,6},{3,7},{4,0},{5,1},{6,2},{7,3},{8,12},{9,13},{10,... | collective-permute-start | bytes 196616 | tf_op jit(solution)/shard_map/ppermute | solution.py:331
  64.2 2.5 %collective-permute-done.5 = f32[128,128]{1,0:T(8,128)S(1)} collective-permute-done((f32[128,128]{1,0:T(8,128)S(1)}, f32[128,128]{1,0:T(8,128)S(1)}, u32[]{:S(2)}, u32[]{:S(2)}) %collective-permute-start.5) | collective-permute-done | bytes 65568 | tf_op jit(solution)/shard_map/ppermute | solution.py:331
  66.7 0.9 spread.1
  67.6 0.9 all-to-all-done.x_ref
  68.5 7.1 %all-to-all-start.1 = ((s16[8,136,128]{2,1,0:T(8,128)(2,1)}), s16[8,136,128]{2,1,0:T(8,128)(2,1)S(1)}, u32[]{:S(2)}, u32[]{:S(2)}) async-start(s16[8,136,128]{2,1,0:T(8,128)(2,1)} %spread.1), calls=%async_computation.1 | async-start | bytes 557056 | tf_op jit(solution)/shard_map/all_to_all | solution.py:334
  75.6 9.1 %cold_sum.1 = s16[8,136,128]{2,1,0:T(8,128)(2,1)} custom-call(bf16[64,136,128]{2,1,0:T(8,128)(2,1)} %all-to-all-done.x_ref), custom_call_target="tpu_custom_call" | custom-call | flops 10737418240 | bytes 3145728 | tf_op jit(solution)/shard_map/cold_sum/pallas_call | solution.py:236
  84.7 1.5 %all-to-all-done.1.pieces_ref = s16[8,136,128]{2,1,0:T(8,128)(2,1)S(1)} async-done(((s16[8,136,128]{2,1,0:T(8,128)(2,1)}), s16[8,136,128]{2,1,0:T(8,128)(2,1)S(1)}, u32[]{:S(2)}, u32[]{:S(2)}) %all-to-all-start.1) | async-done | bytes 278560 | tf_op jit(solution)/shard_map/all_to_all | solution.py:334
  86.2 7.7 %all-to-all-start.2 = ((s16[8,136,128]{2,1,0:T(8,128)(2,1)}), s16[8,136,128]{2,1,0:T(8,128)(2,1)S(1)}, u32[]{:S(2)}, u32[]{:S(2)}) async-start(s16[8,136,128]{2,1,0:T(8,128)(2,1)} %cold_sum.1), calls=%async_computation.2 | async-start | bytes 557056 | tf_op jit(solution)/shard_map/all_to_all | solution.py:337
  94.4 2.8 %collective-permute-start.6 = (s16[136,128]{1,0:T(8,128)(2,1)S(1)}, s16[136,128]{1,0:T(8,128)(2,1)S(1)}, u32[]{:S(2)}, u32[]{:S(2)}) collective-permute-start(s16[136,128]{1,0:T(8,128)(2,1)S(1)} %line_total.1), channel_id=1, source_target_pairs={{0,16},{8,24},{16,0},{24,8},{32,48},{40,56},{48,32},{56,40},{64,80... | collective-permute-start | bytes 104456 | tf_op jit(solution)/shard_map/ppermute | solution.py:315
  97.2 3.0 %collective-permute-done.6 = s16[136,128]{1,0:T(8,128)(2,1)S(1)} collective-permute-done((s16[136,128]{1,0:T(8,128)(2,1)S(1)}, s16[136,128]{1,0:T(8,128)(2,1)S(1)}, u32[]{:S(2)}, u32[]{:S(2)}) %collective-permute-start.6) | collective-permute-done | bytes 34848 | tf_op jit(solution)/shard_map/ppermute | solution.py:315
  100.2 3.3 %collective-permute-start.7 = (s16[272,128]{1,0:T(8,128)(2,1)S(1)}, s16[272,128]{1,0:T(8,128)(2,1)S(1)}, u32[]{:S(2)}, u32[]{:S(2)}) collective-permute-start(s16[272,128]{1,0:T(8,128)(2,1)S(1)} %add_select_fusion.2), channel_id=1, source_target_pairs={{0,48},{8,56},{16,32},{24,40},{32,16},{40,24},{48,0},{56,8},{64,11... | collective-permute-start | bytes 208904 | tf_op jit(solution)/shard_map/ppermute | solution.py:315
  103.6 1.0 all-to-all-done.2.pieces_ref
  104.6 1.1 replica_total.1
  105.7 6.2 %all-to-all-start.3 = ((s16[8,136,128]{2,1,0:T(8,128)(2,1)}), s16[8,136,128]{2,1,0:T(8,128)(2,1)S(1)}, u32[]{:S(2)}, u32[]{:S(2)}) async-start(s16[8,136,128]{2,1,0:T(8,128)(2,1)} %replica_total.1), calls=%async_computation.3 | async-start | bytes 557056 | tf_op jit(solution)/shard_map/all_to_all | solution.py:341
  112.0 1.9 %collective-permute-start.8 = (s16[544,128]{1,0:T(8,128)(2,1)S(1)}, s16[544,128]{1,0:T(8,128)(2,1)S(1)}, u32[]{:S(2)}, u32[]{:S(2)}) collective-permute-start(s16[544,128]{1,0:T(8,128)(2,1)S(1)} %add_select_fusion.1), channel_id=1, source_target_pairs={{0,8},{8,0},{16,24},{24,16},{32,40},{40,32},{48,56},{56,48},{64,72... | collective-permute-start | bytes 417800 | tf_op jit(solution)/shard_map/ppermute | solution.py:315
  113.9 1.3 %collective-permute-done.8 = s16[544,128]{1,0:T(8,128)(2,1)S(1)} collective-permute-done((s16[544,128]{1,0:T(8,128)(2,1)S(1)}, s16[544,128]{1,0:T(8,128)(2,1)S(1)}, u32[]{:S(2)}, u32[]{:S(2)}) %collective-permute-start.8) | collective-permute-done | bytes 139296 | tf_op jit(solution)/shard_map/ppermute | solution.py:315
  115.4 1.3 %hot_update.1 = (f32[1024,128]{1,0:T(8,128)}, f32[8,128]{1,0:T(8,128)}) custom-call(s16[8,136,128]{2,1,0:T(8,128)(2,1)S(1)} %bitcast.8, f32[1024,128]{1,0:T(8,128)S(1)} %copy-done.1, f32[8,128]{1,0:T(8,128)S(1)} %bitcast.9), custom_call_target="tpu_custom_call" | custom-call | tf_op jit(solution)/shard_map/hot_update/pallas_call | solution.py:253
  116.7 5.9 %all-to-all-done.3.codes_ref = s16[8,136,128]{2,1,0:T(8,128)(2,1)S(1)} async-done(((s16[8,136,128]{2,1,0:T(8,128)(2,1)}), s16[8,136,128]{2,1,0:T(8,128)(2,1)S(1)}, u32[]{:S(2)}, u32[]{:S(2)}) %all-to-all-start.3) | async-done | bytes 278560 | tf_op jit(solution)/shard_map/all_to_all | solution.py:341
  122.6 1.3 %cold_update.1 = (f32[1024,128]{1,0:T(8,128)}, f32[8,128]{1,0:T(8,128)}) custom-call(s16[8,136,128]{2,1,0:T(8,128)(2,1)S(1)} %all-to-all-done.3.codes_ref, f32[1024,128]{1,0:T(8,128)S(1)} %copy-done.2, f32[8,128]{1,0:T(8,128)S(1)} %bitcast.10), custom_call_target="tpu_custom_call" | custom-call | tf_op jit(solution)/shard_map/cold_update/pallas_call | solution.py:253
  (26 shorter events, 0.7 us)
Async XLA Ops:
  3.4 11.0 %copy-start = (bf16[64,136,128]{2,1,0:T(8,128)(2,1)S(1)}, bf16[64,136,128]{2,1,0:T(8,128)(2,1)}, u32[]{:S(2)}) copy-start(bf16[64,136,128]{2,1,0:T(8,128)(2,1)} %prepare.1.x_ref) | copy-start | bytes 6684676
  3.4 11.0 %copy-start.5 = (s32[128,64,2]{0,2,1:T(2,128)S(1)}, s32[128,64,2]{0,2,1:T(2,128)}, u32[]{:S(2)}) copy-start(s32[128,64,2]{0,2,1:T(2,128)} %param.11) | copy-start | bytes 196612
  3.4 65.1 %all-to-all-start = ((bf16[64,136,128]{2,1,0:T(8,128)(2,1)}), bf16[64,136,128]{2,1,0:T(8,128)(2,1)}, u32[]{:S(2)}, u32[]{:S(2)}) async-start(bf16[64,136,128]{2,1,0:T(8,128)(2,1)} %prepare.1.x_ref), calls=%async_computation | async-start | bytes 4456448 | tf_op jit(solution)/shard_map/all_to_all | solution.py:323
  19.2 3.4 %collective-permute-start = (f32[512,128]{1,0:T(8,128)S(1)}, f32[512,128]{1,0:T(8,128)S(1)}, u32[]{:S(2)}, u32[]{:S(2)}) collective-permute-start(f32[512,128]{1,0:T(8,128)S(1)} %constant_dynamic-slice_fusion.2), channel_id=1, source_target_pairs={{0,8},{8,0},{16,24},{24,16},{32,40},{40,32},{48,56},{56,48},{64,72... | collective-permute-start | bytes 786440 | tf_op jit(solution)/shard_map/ppermute | solution.py:310
  22.7 10.4 %collective-permute-start.1 = (f32[256,128]{1,0:T(8,128)S(1)}, f32[256,128]{1,0:T(8,128)S(1)}, u32[]{:S(2)}, u32[]{:S(2)}) collective-permute-start(f32[256,128]{1,0:T(8,128)S(1)} %constant_dynamic-slice_fusion.1), channel_id=1, source_target_pairs={{0,48},{8,56},{16,32},{24,40},{32,16},{40,24},{48,0},{56,8},{64,11... | collective-permute-start | bytes 393224 | tf_op jit(solution)/shard_map/ppermute | solution.py:310
  33.1 6.5 %collective-permute-start.2 = (f32[128,128]{1,0:T(8,128)S(1)}, f32[128,128]{1,0:T(8,128)S(1)}, u32[]{:S(2)}, u32[]{:S(2)}) collective-permute-start(f32[128,128]{1,0:T(8,128)S(1)} %constant_dynamic-slice_fusion), channel_id=1, source_target_pairs={{0,16},{8,24},{16,0},{24,8},{32,48},{40,56},{48,32},{56,40},{64,80... | collective-permute-start | bytes 196616 | tf_op jit(solution)/shard_map/ppermute | solution.py:310
  39.6 6.9 %collective-permute-start.3 = (f32[128,128]{1,0:T(8,128)S(1)}, f32[128,128]{1,0:T(8,128)S(1)}, u32[]{:S(2)}, u32[]{:S(2)}) collective-permute-start(f32[128,128]{1,0:T(8,128)S(1)} %dynamic-slice_add_fusion.2), channel_id=1, source_target_pairs={{0,1},{1,0},{2,3},{3,2},{4,5},{5,4},{6,7},{7,6},{8,9},{9,8},{10,11... | collective-permute-start | bytes 196616 | tf_op jit(solution)/shard_map/ppermute | solution.py:331
  46.6 8.3 %collective-permute-start.4 = (f32[128,128]{1,0:T(8,128)S(1)}, f32[128,128]{1,0:T(8,128)S(1)}, u32[]{:S(2)}, u32[]{:S(2)}) collective-permute-start(f32[128,128]{1,0:T(8,128)S(1)} %add.45), channel_id=1, source_target_pairs={{0,2},{1,3},{2,0},{3,1},{4,6},{5,7},{6,4},{7,5},{8,10},{9,11},{10,... | collective-permute-start | bytes 196616 | tf_op jit(solution)/shard_map/ppermute | solution.py:331
  54.9 11.7 %collective-permute-start.5 = (f32[128,128]{1,0:T(8,128)S(1)}, f32[128,128]{1,0:T(8,128)S(1)}, u32[]{:S(2)}, u32[]{:S(2)}) collective-permute-start(f32[128,128]{1,0:T(8,128)S(1)} %add.46), channel_id=1, source_target_pairs={{0,4},{1,5},{2,6},{3,7},{4,0},{5,1},{6,2},{7,3},{8,12},{9,13},{10,... | collective-permute-start | bytes 196616 | tf_op jit(solution)/shard_map/ppermute | solution.py:331
  68.5 17.7 %all-to-all-start.1 = ((s16[8,136,128]{2,1,0:T(8,128)(2,1)}), s16[8,136,128]{2,1,0:T(8,128)(2,1)S(1)}, u32[]{:S(2)}, u32[]{:S(2)}) async-start(s16[8,136,128]{2,1,0:T(8,128)(2,1)} %spread.1), calls=%async_computation.1 | async-start | bytes 557056 | tf_op jit(solution)/shard_map/all_to_all | solution.py:334
  84.7 30.7 %copy-start.1 = (f32[1024,128]{1,0:T(8,128)S(1)}, f32[1024,128]{1,0:T(8,128)}, u32[]{:S(2)}) copy-start(f32[1024,128]{1,0:T(8,128)} %table_ref.3) | copy-start | bytes 1572868
  84.7 30.7 %copy-start.3 = (f32[1024]{0:T(1024)S(1)}, f32[1024]{0:T(1024)}, u32[]{:S(2)}) copy-start(f32[1024]{0:T(1024)} %param.15) | copy-start | bytes 12292
  84.7 37.9 %copy-start.2 = (f32[1024,128]{1,0:T(8,128)S(1)}, f32[1024,128]{1,0:T(8,128)}, u32[]{:S(2)}) copy-start(f32[1024,128]{1,0:T(8,128)} %table_ref.2) | copy-start | bytes 1572868
  84.7 37.9 %copy-start.4 = (f32[1024]{0:T(1024)S(1)}, f32[1024]{0:T(1024)}, u32[]{:S(2)}) copy-start(f32[1024]{0:T(1024)} %param.13) | copy-start | bytes 12292
  86.2 18.4 %all-to-all-start.2 = ((s16[8,136,128]{2,1,0:T(8,128)(2,1)}), s16[8,136,128]{2,1,0:T(8,128)(2,1)S(1)}, u32[]{:S(2)}, u32[]{:S(2)}) async-start(s16[8,136,128]{2,1,0:T(8,128)(2,1)} %cold_sum.1), calls=%async_computation.2 | async-start | bytes 557056 | tf_op jit(solution)/shard_map/all_to_all | solution.py:337
  94.4 5.8 %collective-permute-start.6 = (s16[136,128]{1,0:T(8,128)(2,1)S(1)}, s16[136,128]{1,0:T(8,128)(2,1)S(1)}, u32[]{:S(2)}, u32[]{:S(2)}) collective-permute-start(s16[136,128]{1,0:T(8,128)(2,1)S(1)} %line_total.1), channel_id=1, source_target_pairs={{0,16},{8,24},{16,0},{24,8},{32,48},{40,56},{48,32},{56,40},{64,80... | collective-permute-start | bytes 104456 | tf_op jit(solution)/shard_map/ppermute | solution.py:315
  100.2 11.7 %collective-permute-start.7 = (s16[272,128]{1,0:T(8,128)(2,1)S(1)}, s16[272,128]{1,0:T(8,128)(2,1)S(1)}, u32[]{:S(2)}, u32[]{:S(2)}) collective-permute-start(s16[272,128]{1,0:T(8,128)(2,1)S(1)} %add_select_fusion.2), channel_id=1, source_target_pairs={{0,48},{8,56},{16,32},{24,40},{32,16},{40,24},{48,0},{56,8},{64,11... | collective-permute-start | bytes 208904 | tf_op jit(solution)/shard_map/ppermute | solution.py:315
  105.7 16.8 %all-to-all-start.3 = ((s16[8,136,128]{2,1,0:T(8,128)(2,1)}), s16[8,136,128]{2,1,0:T(8,128)(2,1)S(1)}, u32[]{:S(2)}, u32[]{:S(2)}) async-start(s16[8,136,128]{2,1,0:T(8,128)(2,1)} %replica_total.1), calls=%async_computation.3 | async-start | bytes 557056 | tf_op jit(solution)/shard_map/all_to_all | solution.py:341
  112.0 3.3 %collective-permute-start.8 = (s16[544,128]{1,0:T(8,128)(2,1)S(1)}, s16[544,128]{1,0:T(8,128)(2,1)S(1)}, u32[]{:S(2)}, u32[]{:S(2)}) collective-permute-start(s16[544,128]{1,0:T(8,128)(2,1)S(1)} %add_select_fusion.1), channel_id=1, source_target_pairs={{0,8},{8,0},{16,24},{24,16},{32,40},{40,32},{48,56},{56,48},{64,72... | collective-permute-start | bytes 417800 | tf_op jit(solution)/shard_map/ppermute | solution.py:315

commit v7 on v5

--- a/solution.py
+++ b/solution.py
@@ -224,7 +224,7 @@
         out_ref[field, GROUP:, :] = level_tile(level)
 
 
-def cold_sum(rows, blocks=16):
+def cold_sum(rows, blocks=32):
     count, height, width = rows.shape
     return pl.pallas_call(
         functools.partial(cold_kernel, blocks=blocks),

time: 125 us -> 125 us (level)
  no operation moved by 1% of the time
where the time goes in v7:
time: 125 us; the launch traced here: 124 us
  starting transfers between devices  67.9 us (54%)
  waiting for transfers between devices  33.2 us (27%)
  Pallas kernels  21.4 us (17%)
    ppermute x3, starting transfers between devices, per_device(): hot = hot + lax.ppermute(hot, 'rep', [(i, i ^ bit) for i in range(FIELDS)])  20.1 us
    ppermute x3, waiting for transfers between devices, halve(): lax.ppermute(lax.dynamic_slice_in_dim(rows, (1 - mine) * half, half), axi...  12.4 us
    all_to_all x1, starting transfers between devices, per_device(): lax.all_to_all(rows, 'shard', split_axis=0, concat_axis=0, tiled=True)  11 us
    pallas_call x1, Pallas kernels, cold_sum(): pl.pallas_call(functools.partial(cold_kernel, blocks=blocks), in_specs=[p...  9.04 us
    ppermute x3, starting transfers between devices, double(): lax.ppermute(rows, axis, [(i, i ^ mask) for i in range(lax.axis_size(axis...  8.2 us
    ppermute x3, starting transfers between devices, halve(): lax.ppermute(lax.dynamic_slice_in_dim(rows, (1 - mine) * half, half), axi...  7.8 us
    all_to_all x1, starting transfers between devices, per_device(): lax.all_to_all(pieces, 'rep', split_axis=0, concat_axis=0, tiled=True)  7.7 us
    all_to_all x1, starting transfers between devices, per_device(): lax.all_to_all(hot, 'shard', split_axis=0, concat_axis=0, axis_index_grou...  6.97 us
  transfers between devices with their start and end apart: 13, of which 12 were waited for; matrix products, arithmetic and copies ran while one was open for 0% of the time, Pallas kernels for 14%

profile of v7, /device:TPU:6, one launch (start us, length us, event | category | flops | bytes accessed | tf_op | source)
XLA Modules:
  0.0 123.7 jit_solution(16104967138855617428)
XLA Ops:
  0.6 2.8 %prepare.1.x_ref = bf16[64,136,128]{2,1,0:T(8,128)(2,1)} custom-call(bf16[128,64,128]{2,1,0:T(8,128)(2,1)} %grad_ref.1, s32[64,8,128]{2,1,0:T(8,128)} %bitcast.12, s32[64,128]{1,0:T(8,128)} %bitcast.13), custom_call_target="tpu_custom_call" | custom-call | bytes 5242880 | tf_op jit(solution)/shard_map/prepare/pallas_call | solution.py:141
  3.4 11.0 %all-to-all-start = ((bf16[64,136,128]{2,1,0:T(8,128)(2,1)}), bf16[64,136,128]{2,1,0:T(8,128)(2,1)}, u32[]{:S(2)}, u32[]{:S(2)}) async-start(bf16[64,136,128]{2,1,0:T(8,128)(2,1)} %prepare.1.x_ref), calls=%async_computation | async-start | bytes 4456448 | tf_op jit(solution)/shard_map/all_to_all | solution.py:316
  14.4 4.8 %hot_sum.1 = f32[1024,128]{1,0:T(8,128)S(1)} custom-call(bf16[64,136,128]{2,1,0:T(8,128)(2,1)S(1)} %copy-done, s32[64,2,128]{2,1,0:T(2,128)S(1)} %bitcast.11), custom_call_target="tpu_custom_call" | custom-call | flops 2147483648 | bytes 3145728 | tf_op jit(solution)/shard_map/hot_sum/pallas_call | solution.py:183
  19.2 2.1 %collective-permute-start = (f32[512,128]{1,0:T(8,128)S(1)}, f32[512,128]{1,0:T(8,128)S(1)}, u32[]{:S(2)}, u32[]{:S(2)}) collective-permute-start(f32[512,128]{1,0:T(8,128)S(1)} %constant_dynamic-slice_fusion.2), channel_id=1, source_target_pairs={{0,8},{8,0},{16,24},{24,16},{32,40},{40,32},{48,56},{56,48},{64,72... | collective-permute-start | bytes 786440 | tf_op jit(solution)/shard_map/ppermute | solution.py:303
  21.3 1.4 %collective-permute-done = f32[512,128]{1,0:T(8,128)S(1)} collective-permute-done((f32[512,128]{1,0:T(8,128)S(1)}, f32[512,128]{1,0:T(8,128)S(1)}, u32[]{:S(2)}, u32[]{:S(2)}) %collective-permute-start) | collective-permute-done | bytes 262176 | tf_op jit(solution)/shard_map/ppermute | solution.py:303
  22.7 2.5 %collective-permute-start.1 = (f32[256,128]{1,0:T(8,128)S(1)}, f32[256,128]{1,0:T(8,128)S(1)}, u32[]{:S(2)}, u32[]{:S(2)}) collective-permute-start(f32[256,128]{1,0:T(8,128)S(1)} %constant_dynamic-slice_fusion.1), channel_id=1, source_target_pairs={{0,48},{8,56},{16,32},{24,40},{32,16},{40,24},{48,0},{56,8},{64,11... | collective-permute-start | bytes 393224 | tf_op jit(solution)/shard_map/ppermute | solution.py:303
  25.2 7.9 %collective-permute-done.1 = f32[256,128]{1,0:T(8,128)S(1)} collective-permute-done((f32[256,128]{1,0:T(8,128)S(1)}, f32[256,128]{1,0:T(8,128)S(1)}, u32[]{:S(2)}, u32[]{:S(2)}) %collective-permute-start.1) | collective-permute-done | bytes 131104 | tf_op jit(solution)/shard_map/ppermute | solution.py:303
  33.1 3.2 %collective-permute-start.2 = (f32[128,128]{1,0:T(8,128)S(1)}, f32[128,128]{1,0:T(8,128)S(1)}, u32[]{:S(2)}, u32[]{:S(2)}) collective-permute-start(f32[128,128]{1,0:T(8,128)S(1)} %constant_dynamic-slice_fusion), channel_id=1, source_target_pairs={{0,16},{8,24},{16,0},{24,8},{32,48},{40,56},{48,32},{56,40},{64,80... | collective-permute-start | bytes 196616 | tf_op jit(solution)/shard_map/ppermute | solution.py:303
  36.4 3.2 %collective-permute-done.2 = f32[128,128]{1,0:T(8,128)S(1)} collective-permute-done((f32[128,128]{1,0:T(8,128)S(1)}, f32[128,128]{1,0:T(8,128)S(1)}, u32[]{:S(2)}, u32[]{:S(2)}) %collective-permute-start.2) | collective-permute-done | bytes 65568 | tf_op jit(solution)/shard_map/ppermute | solution.py:303
  39.6 4.7 %collective-permute-start.3 = (f32[128,128]{1,0:T(8,128)S(1)}, f32[128,128]{1,0:T(8,128)S(1)}, u32[]{:S(2)}, u32[]{:S(2)}) collective-permute-start(f32[128,128]{1,0:T(8,128)S(1)} %dynamic-slice_add_fusion.2), channel_id=1, source_target_pairs={{0,1},{1,0},{2,3},{3,2},{4,5},{5,4},{6,7},{7,6},{8,9},{9,8},{10,11... | collective-permute-start | bytes 196616 | tf_op jit(solution)/shard_map/ppermute | solution.py:324
  44.3 2.2 %collective-permute-done.3 = f32[128,128]{1,0:T(8,128)S(1)} collective-permute-done((f32[128,128]{1,0:T(8,128)S(1)}, f32[128,128]{1,0:T(8,128)S(1)}, u32[]{:S(2)}, u32[]{:S(2)}) %collective-permute-start.3) | collective-permute-done | bytes 65568 | tf_op jit(solution)/shard_map/ppermute | solution.py:324
  46.6 6.1 %collective-permute-start.4 = (f32[128,128]{1,0:T(8,128)S(1)}, f32[128,128]{1,0:T(8,128)S(1)}, u32[]{:S(2)}, u32[]{:S(2)}) collective-permute-start(f32[128,128]{1,0:T(8,128)S(1)} %add.45), channel_id=1, source_target_pairs={{0,2},{1,3},{2,0},{3,1},{4,6},{5,7},{6,4},{7,5},{8,10},{9,11},{10,... | collective-permute-start | bytes 196616 | tf_op jit(solution)/shard_map/ppermute | solution.py:324
  52.7 2.2 %collective-permute-done.4 = f32[128,128]{1,0:T(8,128)S(1)} collective-permute-done((f32[128,128]{1,0:T(8,128)S(1)}, f32[128,128]{1,0:T(8,128)S(1)}, u32[]{:S(2)}, u32[]{:S(2)}) %collective-permute-start.4) | collective-permute-done | bytes 65568 | tf_op jit(solution)/shard_map/ppermute | solution.py:324
  54.9 9.3 %collective-permute-start.5 = (f32[128,128]{1,0:T(8,128)S(1)}, f32[128,128]{1,0:T(8,128)S(1)}, u32[]{:S(2)}, u32[]{:S(2)}) collective-permute-start(f32[128,128]{1,0:T(8,128)S(1)} %add.46), channel_id=1, source_target_pairs={{0,4},{1,5},{2,6},{3,7},{4,0},{5,1},{6,2},{7,3},{8,12},{9,13},{10,... | collective-permute-start | bytes 196616 | tf_op jit(solution)/shard_map/ppermute | solution.py:324
  64.2 2.5 %collective-permute-done.5 = f32[128,128]{1,0:T(8,128)S(1)} collective-permute-done((f32[128,128]{1,0:T(8,128)S(1)}, f32[128,128]{1,0:T(8,128)S(1)}, u32[]{:S(2)}, u32[]{:S(2)}) %collective-permute-start.5) | collective-permute-done | bytes 65568 | tf_op jit(solution)/shard_map/ppermute | solution.py:324
  66.7 0.8 spread.1
  67.5 1.0 all-to-all-done.x_ref
  68.5 7.0 %all-to-all-start.1 = ((s16[8,136,128]{2,1,0:T(8,128)(2,1)}), s16[8,136,128]{2,1,0:T(8,128)(2,1)S(1)}, u32[]{:S(2)}, u32[]{:S(2)}) async-start(s16[8,136,128]{2,1,0:T(8,128)(2,1)} %spread.1), calls=%async_computation.1 | async-start | bytes 557056 | tf_op jit(solution)/shard_map/all_to_all | solution.py:327
  75.5 9.0 %cold_sum.1 = s16[8,136,128]{2,1,0:T(8,128)(2,1)} custom-call(bf16[64,136,128]{2,1,0:T(8,128)(2,1)} %all-to-all-done.x_ref), custom_call_target="tpu_custom_call" | custom-call | flops 10737418240 | bytes 3145728 | tf_op jit(solution)/shard_map/cold_sum/pallas_call | solution.py:229
  84.6 1.6 %all-to-all-done.1.pieces_ref = s16[8,136,128]{2,1,0:T(8,128)(2,1)S(1)} async-done(((s16[8,136,128]{2,1,0:T(8,128)(2,1)}), s16[8,136,128]{2,1,0:T(8,128)(2,1)S(1)}, u32[]{:S(2)}, u32[]{:S(2)}) %all-to-all-start.1) | async-done | bytes 278560 | tf_op jit(solution)/shard_map/all_to_all | solution.py:327
  86.1 7.7 %all-to-all-start.2 = ((s16[8,136,128]{2,1,0:T(8,128)(2,1)}), s16[8,136,128]{2,1,0:T(8,128)(2,1)S(1)}, u32[]{:S(2)}, u32[]{:S(2)}) async-start(s16[8,136,128]{2,1,0:T(8,128)(2,1)} %cold_sum.1), calls=%async_computation.2 | async-start | bytes 557056 | tf_op jit(solution)/shard_map/all_to_all | solution.py:330
  94.2 2.8 %collective-permute-start.6 = (s16[136,128]{1,0:T(8,128)(2,1)S(1)}, s16[136,128]{1,0:T(8,128)(2,1)S(1)}, u32[]{:S(2)}, u32[]{:S(2)}) collective-permute-start(s16[136,128]{1,0:T(8,128)(2,1)S(1)} %line_total.1), channel_id=1, source_target_pairs={{0,16},{8,24},{16,0},{24,8},{32,48},{40,56},{48,32},{56,40},{64,80... | collective-permute-start | bytes 104456 | tf_op jit(solution)/shard_map/ppermute | solution.py:308
  97.0 3.0 %collective-permute-done.6 = s16[136,128]{1,0:T(8,128)(2,1)S(1)} collective-permute-done((s16[136,128]{1,0:T(8,128)(2,1)S(1)}, s16[136,128]{1,0:T(8,128)(2,1)S(1)}, u32[]{:S(2)}, u32[]{:S(2)}) %collective-permute-start.6) | collective-permute-done | bytes 34848 | tf_op jit(solution)/shard_map/ppermute | solution.py:308
  100.0 3.4 %collective-permute-start.7 = (s16[272,128]{1,0:T(8,128)(2,1)S(1)}, s16[272,128]{1,0:T(8,128)(2,1)S(1)}, u32[]{:S(2)}, u32[]{:S(2)}) collective-permute-start(s16[272,128]{1,0:T(8,128)(2,1)S(1)} %add_select_fusion.2), channel_id=1, source_target_pairs={{0,48},{8,56},{16,32},{24,40},{32,16},{40,24},{48,0},{56,8},{64,11... | collective-permute-start | bytes 208904 | tf_op jit(solution)/shard_map/ppermute | solution.py:308
  103.5 1.0 all-to-all-done.2.pieces_ref
  104.5 1.0 replica_total.1
  105.5 6.2 %all-to-all-start.3 = ((s16[8,136,128]{2,1,0:T(8,128)(2,1)}), s16[8,136,128]{2,1,0:T(8,128)(2,1)S(1)}, u32[]{:S(2)}, u32[]{:S(2)}) async-start(s16[8,136,128]{2,1,0:T(8,128)(2,1)} %replica_total.1), calls=%async_computation.3 | async-start | bytes 557056 | tf_op jit(solution)/shard_map/all_to_all | solution.py:334
  111.8 1.9 %collective-permute-start.8 = (s16[544,128]{1,0:T(8,128)(2,1)S(1)}, s16[544,128]{1,0:T(8,128)(2,1)S(1)}, u32[]{:S(2)}, u32[]{:S(2)}) collective-permute-start(s16[544,128]{1,0:T(8,128)(2,1)S(1)} %add_select_fusion.1), channel_id=1, source_target_pairs={{0,8},{8,0},{16,24},{24,16},{32,40},{40,32},{48,56},{56,48},{64,72... | collective-permute-start | bytes 417800 | tf_op jit(solution)/shard_map/ppermute | solution.py:308
  113.7 1.3 %collective-permute-done.8 = s16[544,128]{1,0:T(8,128)(2,1)S(1)} collective-permute-done((s16[544,128]{1,0:T(8,128)(2,1)S(1)}, s16[544,128]{1,0:T(8,128)(2,1)S(1)}, u32[]{:S(2)}, u32[]{:S(2)}) %collective-permute-start.8) | collective-permute-done | bytes 139296 | tf_op jit(solution)/shard_map/ppermute | solution.py:308
  115.1 1.3 %hot_update.1 = (f32[1024,128]{1,0:T(8,128)}, f32[8,128]{1,0:T(8,128)}) custom-call(s16[8,136,128]{2,1,0:T(8,128)(2,1)S(1)} %bitcast.8, f32[1024,128]{1,0:T(8,128)S(1)} %copy-done.1, f32[8,128]{1,0:T(8,128)S(1)} %bitcast.9), custom_call_target="tpu_custom_call" | custom-call | tf_op jit(solution)/shard_map/hot_update/pallas_call | solution.py:246
  116.5 5.9 %all-to-all-done.3.codes_ref = s16[8,136,128]{2,1,0:T(8,128)(2,1)S(1)} async-done(((s16[8,136,128]{2,1,0:T(8,128)(2,1)}), s16[8,136,128]{2,1,0:T(8,128)(2,1)S(1)}, u32[]{:S(2)}, u32[]{:S(2)}) %all-to-all-start.3) | async-done | bytes 278560 | tf_op jit(solution)/shard_map/all_to_all | solution.py:334
  122.4 1.3 %cold_update.1 = (f32[1024,128]{1,0:T(8,128)}, f32[8,128]{1,0:T(8,128)}) custom-call(s16[8,136,128]{2,1,0:T(8,128)(2,1)S(1)} %all-to-all-done.3.codes_ref, f32[1024,128]{1,0:T(8,128)S(1)} %copy-done.2, f32[8,128]{1,0:T(8,128)S(1)} %bitcast.10), custom_call_target="tpu_custom_call" | custom-call | tf_op jit(solution)/shard_map/cold_update/pallas_call | solution.py:246
  (26 shorter events, 0.6 us)
Async XLA Ops:
  3.4 11.0 %copy-start = (bf16[64,136,128]{2,1,0:T(8,128)(2,1)S(1)}, bf16[64,136,128]{2,1,0:T(8,128)(2,1)}, u32[]{:S(2)}) copy-start(bf16[64,136,128]{2,1,0:T(8,128)(2,1)} %prepare.1.x_ref) | copy-start | bytes 6684676
  3.4 11.0 %copy-start.5 = (s32[128,64,2]{0,2,1:T(2,128)S(1)}, s32[128,64,2]{0,2,1:T(2,128)}, u32[]{:S(2)}) copy-start(s32[128,64,2]{0,2,1:T(2,128)} %param.11) | copy-start | bytes 196612
  3.4 65.1 %all-to-all-start = ((bf16[64,136,128]{2,1,0:T(8,128)(2,1)}), bf16[64,136,128]{2,1,0:T(8,128)(2,1)}, u32[]{:S(2)}, u32[]{:S(2)}) async-start(bf16[64,136,128]{2,1,0:T(8,128)(2,1)} %prepare.1.x_ref), calls=%async_computation | async-start | bytes 4456448 | tf_op jit(solution)/shard_map/all_to_all | solution.py:316
  19.2 3.4 %collective-permute-start = (f32[512,128]{1,0:T(8,128)S(1)}, f32[512,128]{1,0:T(8,128)S(1)}, u32[]{:S(2)}, u32[]{:S(2)}) collective-permute-start(f32[512,128]{1,0:T(8,128)S(1)} %constant_dynamic-slice_fusion.2), channel_id=1, source_target_pairs={{0,8},{8,0},{16,24},{24,16},{32,40},{40,32},{48,56},{56,48},{64,72... | collective-permute-start | bytes 786440 | tf_op jit(solution)/shard_map/ppermute | solution.py:303
  22.7 10.4 %collective-permute-start.1 = (f32[256,128]{1,0:T(8,128)S(1)}, f32[256,128]{1,0:T(8,128)S(1)}, u32[]{:S(2)}, u32[]{:S(2)}) collective-permute-start(f32[256,128]{1,0:T(8,128)S(1)} %constant_dynamic-slice_fusion.1), channel_id=1, source_target_pairs={{0,48},{8,56},{16,32},{24,40},{32,16},{40,24},{48,0},{56,8},{64,11... | collective-permute-start | bytes 393224 | tf_op jit(solution)/shard_map/ppermute | solution.py:303
  33.1 6.5 %collective-permute-start.2 = (f32[128,128]{1,0:T(8,128)S(1)}, f32[128,128]{1,0:T(8,128)S(1)}, u32[]{:S(2)}, u32[]{:S(2)}) collective-permute-start(f32[128,128]{1,0:T(8,128)S(1)} %constant_dynamic-slice_fusion), channel_id=1, source_target_pairs={{0,16},{8,24},{16,0},{24,8},{32,48},{40,56},{48,32},{56,40},{64,80... | collective-permute-start | bytes 196616 | tf_op jit(solution)/shard_map/ppermute | solution.py:303
  39.6 6.9 %collective-permute-start.3 = (f32[128,128]{1,0:T(8,128)S(1)}, f32[128,128]{1,0:T(8,128)S(1)}, u32[]{:S(2)}, u32[]{:S(2)}) collective-permute-start(f32[128,128]{1,0:T(8,128)S(1)} %dynamic-slice_add_fusion.2), channel_id=1, source_target_pairs={{0,1},{1,0},{2,3},{3,2},{4,5},{5,4},{6,7},{7,6},{8,9},{9,8},{10,11... | collective-permute-start | bytes 196616 | tf_op jit(solution)/shard_map/ppermute | solution.py:324
  46.6 8.3 %collective-permute-start.4 = (f32[128,128]{1,0:T(8,128)S(1)}, f32[128,128]{1,0:T(8,128)S(1)}, u32[]{:S(2)}, u32[]{:S(2)}) collective-permute-start(f32[128,128]{1,0:T(8,128)S(1)} %add.45), channel_id=1, source_target_pairs={{0,2},{1,3},{2,0},{3,1},{4,6},{5,7},{6,4},{7,5},{8,10},{9,11},{10,... | collective-permute-start | bytes 196616 | tf_op jit(solution)/shard_map/ppermute | solution.py:324
  54.9 11.7 %collective-permute-start.5 = (f32[128,128]{1,0:T(8,128)S(1)}, f32[128,128]{1,0:T(8,128)S(1)}, u32[]{:S(2)}, u32[]{:S(2)}) collective-permute-start(f32[128,128]{1,0:T(8,128)S(1)} %add.46), channel_id=1, source_target_pairs={{0,4},{1,5},{2,6},{3,7},{4,0},{5,1},{6,2},{7,3},{8,12},{9,13},{10,... | collective-permute-start | bytes 196616 | tf_op jit(solution)/shard_map/ppermute | solution.py:324
  68.5 17.6 %all-to-all-start.1 = ((s16[8,136,128]{2,1,0:T(8,128)(2,1)}), s16[8,136,128]{2,1,0:T(8,128)(2,1)S(1)}, u32[]{:S(2)}, u32[]{:S(2)}) async-start(s16[8,136,128]{2,1,0:T(8,128)(2,1)} %spread.1), calls=%async_computation.1 | async-start | bytes 557056 | tf_op jit(solution)/shard_map/all_to_all | solution.py:327
  84.5 30.6 %copy-start.1 = (f32[1024,128]{1,0:T(8,128)S(1)}, f32[1024,128]{1,0:T(8,128)}, u32[]{:S(2)}) copy-start(f32[1024,128]{1,0:T(8,128)} %table_ref.3) | copy-start | bytes 1572868
  84.5 30.6 %copy-start.3 = (f32[1024]{0:T(1024)S(1)}, f32[1024]{0:T(1024)}, u32[]{:S(2)}) copy-start(f32[1024]{0:T(1024)} %param.15) | copy-start | bytes 12292
  84.6 37.8 %copy-start.2 = (f32[1024,128]{1,0:T(8,128)S(1)}, f32[1024,128]{1,0:T(8,128)}, u32[]{:S(2)}) copy-start(f32[1024,128]{1,0:T(8,128)} %table_ref.2) | copy-start | bytes 1572868
  84.6 37.8 %copy-start.4 = (f32[1024]{0:T(1024)S(1)}, f32[1024]{0:T(1024)}, u32[]{:S(2)}) copy-start(f32[1024]{0:T(1024)} %param.13) | copy-start | bytes 12292
  86.1 18.4 %all-to-all-start.2 = ((s16[8,136,128]{2,1,0:T(8,128)(2,1)}), s16[8,136,128]{2,1,0:T(8,128)(2,1)S(1)}, u32[]{:S(2)}, u32[]{:S(2)}) async-start(s16[8,136,128]{2,1,0:T(8,128)(2,1)} %cold_sum.1), calls=%async_computation.2 | async-start | bytes 557056 | tf_op jit(solution)/shard_map/all_to_all | solution.py:330
  94.2 5.8 %collective-permute-start.6 = (s16[136,128]{1,0:T(8,128)(2,1)S(1)}, s16[136,128]{1,0:T(8,128)(2,1)S(1)}, u32[]{:S(2)}, u32[]{:S(2)}) collective-permute-start(s16[136,128]{1,0:T(8,128)(2,1)S(1)} %line_total.1), channel_id=1, source_target_pairs={{0,16},{8,24},{16,0},{24,8},{32,48},{40,56},{48,32},{56,40},{64,80... | collective-permute-start | bytes 104456 | tf_op jit(solution)/shard_map/ppermute | solution.py:308
  100.0 11.7 %collective-permute-start.7 = (s16[272,128]{1,0:T(8,128)(2,1)S(1)}, s16[272,128]{1,0:T(8,128)(2,1)S(1)}, u32[]{:S(2)}, u32[]{:S(2)}) collective-permute-start(s16[272,128]{1,0:T(8,128)(2,1)S(1)} %add_select_fusion.2), channel_id=1, source_target_pairs={{0,48},{8,56},{16,32},{24,40},{32,16},{40,24},{48,0},{56,8},{64,11... | collective-permute-start | bytes 208904 | tf_op jit(solution)/shard_map/ppermute | solution.py:308
  105.5 16.9 %all-to-all-start.3 = ((s16[8,136,128]{2,1,0:T(8,128)(2,1)}), s16[8,136,128]{2,1,0:T(8,128)(2,1)S(1)}, u32[]{:S(2)}, u32[]{:S(2)}) async-start(s16[8,136,128]{2,1,0:T(8,128)(2,1)} %replica_total.1), calls=%async_computation.3 | async-start | bytes 557056 | tf_op jit(solution)/shard_map/all_to_all | solution.py:334
  111.8 3.3 %collective-permute-start.8 = (s16[544,128]{1,0:T(8,128)(2,1)S(1)}, s16[544,128]{1,0:T(8,128)(2,1)S(1)}, u32[]{:S(2)}, u32[]{:S(2)}) collective-permute-start(s16[544,128]{1,0:T(8,128)(2,1)S(1)} %add_select_fusion.1), channel_id=1, source_target_pairs={{0,8},{8,0},{16,24},{24,16},{32,40},{40,32},{48,56},{56,48},{64,72... | collective-permute-start | bytes 417800 | tf_op jit(solution)/shard_map/ppermute | solution.py:308
